TPU v7x, 32 devices: a whole 2x2x4 slice. The times are simulated.
32 devices in a mesh: dp: 16 (over z, y, core), vocab: 2 (over x).
Axes of the slice: x: 2, y: 2, z: 4, core: 2. Of those that a mesh axis runs over, the one named last changes fastest.
Arguments:
- src_tokens: int32 [32, 256], P('dp'), may hold values from 0 to 31999
- tgt_tokens: int32 [32, 256], P('dp'), may hold values from 0 to 31999
- src_segments: int32 [32, 256], P('dp'), may hold values from 0 to 7, never falling along the last dimension, each value on 1 to 96 neighbouring positions
- tgt_lengths: int32 [32, 8], P('dp'), may hold values from 1 to 96, 256 in all within a row
- mask_order: int32 [32, 256], P('dp'), may hold values from 0 to 255, each once within a row
- attn_project: float32 [3, 512, 1536], P(None, 'dp'), may hold values from -0.1875 to 0.1875
- attn_output: float32 [3, 512, 512], P(None, 'dp'), may hold values from -0.5 to 0.5
- ffn_expand: float32 [2, 512, 2048], P(None, 'dp'), may hold values from -0.25 to 0.25
- ffn_reduce: float32 [2, 2048, 512], P(None, 'dp'), may hold values from -0.125 to 0.125
- norm_gains: float32 [7, 512], P(None, 'dp')
- length_table: float32 [256, 512], P(None, 'dp'), may hold values from -1.5 to 1.5
- embedding: float32 [32000, 512], P(('vocab', 'dp'))
- momentum_attn_project: float32 [3, 512, 1536], P(None, 'dp'), may hold values from -2.2888184e-05 to 2.2888184e-05
- momentum_attn_output: float32 [3, 512, 512], P(None, 'dp'), may hold values from -2.2888184e-05 to 2.2888184e-05
- momentum_ffn_expand: float32 [2, 512, 2048], P(None, 'dp'), may hold values from -2.2888184e-05 to 2.2888184e-05
- momentum_ffn_reduce: float32 [2, 2048, 512], P(None, 'dp'), may hold values from -2.2888184e-05 to 2.2888184e-05
- momentum_norm_gains: float32 [7, 512], P(None, 'dp'), may hold values from -0.00024414062 to 0.00024414062
- momentum_length_table: float32 [256, 512], P(None, 'dp'), may hold values from -3.8146973e-06 to 3.8146973e-06
- momentum_embedding: float32 [32000, 512], P(('vocab', 'dp')), may hold values from -2.3841858e-06 to 2.3841858e-06
- average_attn_project: float32 [3, 512, 1536], P(None, 'dp'), may hold values from -0.1875 to 0.1875
- average_attn_output: float32 [3, 512, 512], P(None, 'dp'), may hold values from -0.5 to 0.5
- average_ffn_expand: float32 [2, 512, 2048], P(None, 'dp'), may hold values from -0.25 to 0.25
- average_ffn_reduce: float32 [2, 2048, 512], P(None, 'dp'), may hold values from -0.125 to 0.125
- average_norm_gains: float32 [7, 512], P(None, 'dp'), may hold values from 0.5 to 1.5
- average_length_table: float32 [256, 512], P(None, 'dp'), may hold values from -1.5 to 1.5
- average_embedding: float32 [32000, 512], P(('vocab', 'dp')), may hold values from -0.25 to 0.25
Outputs:
- loss_sum: float32 [], replicated
- grad_norm: float32 [], replicated
- new_attn_project: float32 [3, 512, 1536], P(None, 'dp')
- new_attn_output: float32 [3, 512, 512], P(None, 'dp')
- new_ffn_expand: float32 [2, 512, 2048], P(None, 'dp')
- new_ffn_reduce: float32 [2, 2048, 512], P(None, 'dp')
- new_norm_gains: float32 [7, 512], P(None, 'dp')
- new_length_table: float32 [256, 512], P(None, 'dp')
- new_embedding: float32 [32000, 512], P(('vocab', 'dp'))
- new_momentum_attn_project: float32 [3, 512, 1536], P(None, 'dp')
- new_momentum_attn_output: float32 [3, 512, 512], P(None, 'dp')
- new_momentum_ffn_expand: float32 [2, 512, 2048], P(None, 'dp')
- new_momentum_ffn_reduce: float32 [2, 2048, 512], P(None, 'dp')
- new_momentum_norm_gains: float32 [7, 512], P(None, 'dp')
- new_momentum_length_table: float32 [256, 512], P(None, 'dp')
- new_momentum_embedding: float32 [32000, 512], P(('vocab', 'dp'))
- new_average_attn_project: float32 [3, 512, 1536], P(None, 'dp')
- new_average_attn_output: float32 [3, 512, 512], P(None, 'dp')
- new_average_ffn_expand: float32 [2, 512, 2048], P(None, 'dp')
- new_average_ffn_reduce: float32 [2, 2048, 512], P(None, 'dp')
- new_average_norm_gains: float32 [7, 512], P(None, 'dp')
- new_average_length_table: float32 [256, 512], P(None, 'dp')
- new_average_embedding: float32 [32000, 512], P(('vocab', 'dp'))
- copy_attn_project: bfloat16 [3, 512, 1536], P(None, 'dp')
- copy_attn_output: bfloat16 [3, 512, 512], P(None, 'dp')
- copy_ffn_expand: bfloat16 [2, 512, 2048], P(None, 'dp')
- copy_ffn_reduce: bfloat16 [2, 2048, 512], P(None, 'dp')
- copy_norm_gains: bfloat16 [7, 512], P(None, 'dp')
- copy_length_table: bfloat16 [256, 512], P(None, 'dp')
- copy_embedding: bfloat16 [32000, 512], P(('vocab', 'dp'))
Inputs may be any that keep to these rules, and one draw needn't show every extreme that they name: `src_segments`: segment numbers never fall along a row; each of the 8 sentences has 1 to 96 source tokens, one exactly 96. `tgt_lengths`: A row's 8 lengths sum to 256; the largest is 96. `mask_order`: each row is a permutation of the 256 target positions.
All inputs are finite; a program needn't handle non-finite values.
Results may differ from a plain program's by a relative error of at most 0.012.
The roundings to bfloat16 on the way count: a program that leaves them out, or rounds other values in their place, can miss the bound.
Values may be sent and summed in bfloat16 or wider, within the bound.
No kernel may reach another device: no remote copies, remote signals or barrier semaphores. Data moves between devices by JAX's collectives and lax.ppermute only.
A program may use at most 384 MiB of HBM per device.

v0:
```python
import math

import jax
import jax.numpy as jnp
from jax import lax
from jax.sharding import PartitionSpec as P

D = 512
HDIM = 64
LCLS = 256
ROW = 256
SENTS = 8
MASKED = 96
NPARAM = 23858688


HIGHEST = lax.Precision.HIGHEST
EPSILON = 1e-05
MASK_TOKEN = 3
MOMENTUM = 0.9
KEEP = 0.9
CLIP = 0.02
LENGTH_WEIGHT = 0.1
NEGATIVE = -1e30
RATE_SCALE = 0.25
RATE_FACTORS = (1.0, 1.0, 1.0, 1.0, 6.0, 24.0, 1.0)


def layer_norm(stream, gain):
    centred = stream - jnp.mean(stream, axis=-1, keepdims=True)
    spread = jnp.mean(centred * centred, axis=-1, keepdims=True)
    return centred * lax.rsqrt(spread + EPSILON) * gain


def sinusoid(count, width):
    place = jnp.arange(count, dtype=jnp.float32)[:, None]
    index = jnp.arange(width // 2, dtype=jnp.float32)[None, :]
    angle = place * jnp.exp(-math.log(10000.0) * 2.0 * index / width)
    return jnp.concatenate([jnp.sin(angle), jnp.cos(angle)], axis=1)


def attend_fwd(a_query, a_memory, w_in, w_out, allowed):
    count, width = a_query.shape
    heads = width // HDIM
    low_query = a_query.astype(jnp.bfloat16)
    low_memory = a_memory.astype(jnp.bfloat16)
    query = (
        jnp.dot(low_query, w_in[:, :width], preferred_element_type=jnp.float32)
        .astype(jnp.bfloat16)
        .reshape(count, heads, HDIM)
    )
    memory = jnp.dot(low_memory, w_in[:, width:], preferred_element_type=jnp.float32).astype(
        jnp.bfloat16
    )
    keys = memory[:, :width].reshape(-1, heads, HDIM)
    values = memory[:, width:].reshape(-1, heads, HDIM)
    scores = jnp.einsum("qhd,khd->hqk", query, keys, preferred_element_type=jnp.float32) * HDIM ** (
        -0.5
    )
    scores = jnp.where(allowed[None], scores, NEGATIVE)
    expo = jnp.exp(scores - jnp.max(scores, axis=-1, keepdims=True))
    probs = expo / jnp.sum(expo, axis=-1, keepdims=True)
    low_probs = probs.astype(jnp.bfloat16)
    mixed = (
        jnp.einsum("hqk,khd->qhd", low_probs, values, preferred_element_type=jnp.float32)
        .reshape(count, width)
        .astype(jnp.bfloat16)
    )
    branch = jnp.dot(mixed, w_out, preferred_element_type=jnp.float32)
    return (branch, (low_query, low_memory, query, keys, values, probs, low_probs, mixed))


def attend_bwd(grad_out, cache, w_in, w_out):
    low_query, low_memory, query, keys, values, probs, low_probs, mixed = cache
    count, width = mixed.shape
    heads = width // HDIM
    scale = HDIM ** (-0.5)
    grad_low = grad_out.astype(jnp.bfloat16)
    grad_wout = jnp.einsum("rd,re->de", mixed, grad_low, preferred_element_type=jnp.float32)
    grad_mixed = (
        jnp.einsum("re,de->rd", grad_low, w_out, preferred_element_type=jnp.float32)
        .astype(jnp.bfloat16)
        .reshape(count, heads, HDIM)
    )
    grad_probs = jnp.einsum("qhd,khd->hqk", grad_mixed, values, preferred_element_type=jnp.float32)
    grad_scores = (
        probs * (grad_probs - jnp.sum(probs * grad_probs, axis=-1, keepdims=True))
    ).astype(jnp.bfloat16)
    grad_query = (
        (jnp.einsum("hqk,khd->qhd", grad_scores, keys, preferred_element_type=jnp.float32) * scale)
        .astype(jnp.bfloat16)
        .reshape(count, width)
    )
    grad_keys = (
        (jnp.einsum("hqk,qhd->khd", grad_scores, query, preferred_element_type=jnp.float32) * scale)
        .astype(jnp.bfloat16)
        .reshape(-1, width)
    )
    grad_values = (
        jnp.einsum("hqk,qhd->khd", low_probs, grad_mixed, preferred_element_type=jnp.float32)
        .astype(jnp.bfloat16)
        .reshape(-1, width)
    )
    grad_memory = jnp.concatenate([grad_keys, grad_values], axis=1)
    grad_win = jnp.concatenate(
        [
            jnp.einsum("rd,re->de", low_query, grad_query, preferred_element_type=jnp.float32),
            jnp.einsum("rd,re->de", low_memory, grad_memory, preferred_element_type=jnp.float32),
        ],
        axis=1,
    )
    grad_aq = jnp.einsum(
        "re,de->rd", grad_query, w_in[:, :width], preferred_element_type=jnp.float32
    )
    grad_am = jnp.einsum(
        "re,de->rd", grad_memory, w_in[:, width:], preferred_element_type=jnp.float32
    )
    return (grad_aq, grad_am, grad_win, grad_wout)


def ffn_fwd(normed, w_up, w_down):
    low_normed = normed.astype(jnp.bfloat16)
    hidden = jnp.dot(low_normed, w_up, preferred_element_type=jnp.float32)
    active = jax.nn.gelu(hidden).astype(jnp.bfloat16)
    branch = jnp.dot(active, w_down, preferred_element_type=jnp.float32)
    return (branch, (low_normed, hidden, active))


def ffn_bwd(grad_out, cache, w_up, w_down):
    low_normed, hidden, active = cache
    grad_low = grad_out.astype(jnp.bfloat16)
    grad_down = jnp.einsum("rf,rd->fd", active, grad_low, preferred_element_type=jnp.float32)
    grad_active = jnp.einsum("rd,fd->rf", grad_low, w_down, preferred_element_type=jnp.float32)
    _, gelu_back = jax.vjp(jax.nn.gelu, hidden)
    grad_hidden = gelu_back(grad_active)[0].astype(jnp.bfloat16)
    grad_up = jnp.einsum("rd,rf->df", low_normed, grad_hidden, preferred_element_type=jnp.float32)
    grad_normed = jnp.einsum("rf,df->rd", grad_hidden, w_up, preferred_element_type=jnp.float32)
    return (grad_normed, grad_up, grad_down)


def layer_fwd(stream, weights, depth, allowed, memory, cross_allowed):
    w_in, w_out, w_up, w_down, gain = weights
    base = 3 * depth
    records = []
    normed, norm_back = jax.vjp(layer_norm, stream, gain[base])
    branch, cache = attend_fwd(normed, normed, w_in[depth], w_out[depth], allowed)
    records.append((norm_back, cache))
    stream = stream + branch
    if memory is not None:
        base = base + 1
        normed, norm_back = jax.vjp(layer_norm, stream, gain[base])
        branch, cache = attend_fwd(normed, memory, w_in[2], w_out[2], cross_allowed)
        records.append((norm_back, cache))
        stream = stream + branch
    normed, norm_back = jax.vjp(layer_norm, stream, gain[base + 1])
    branch, cache = ffn_fwd(normed, w_up[depth], w_down[depth])
    records.append((norm_back, cache))
    stream = stream + branch
    top, final_back = jax.vjp(layer_norm, stream, gain[base + 2])
    return (top, (records, final_back))


def layer_bwd(grad_top, kept, weights, depth):
    w_in, w_out, w_up, w_down, gain = weights
    records, final_back = kept
    grad_stream, final_gain = final_back(grad_top)
    ffn_back, ffn_cache = records[-1]
    grad_normed, grad_up, grad_down = ffn_bwd(grad_stream, ffn_cache, w_up[depth], w_down[depth])
    extra, ffn_gain = ffn_back(grad_normed)
    grad_stream = grad_stream + extra
    gain_grads = [ffn_gain, final_gain]
    attn_grads = {}
    memory_grad = None
    for place in range(len(records) - 2, -1, -1):
        attn_back, attn_cache = records[place]
        index = depth if place == 0 else 2
        grad_aq, grad_am, grad_win, grad_wout = attend_bwd(
            grad_stream, attn_cache, w_in[index], w_out[index]
        )
        if place == 0:
            grad_aq = grad_aq + grad_am
        else:
            memory_grad = grad_am
        extra, attn_gain = attn_back(grad_aq)
        grad_stream = grad_stream + extra
        gain_grads.insert(0, attn_gain)
        attn_grads[index] = (grad_win, grad_wout)
    return (grad_stream, memory_grad, gain_grads, attn_grads, (grad_up, grad_down))


def shards(
    src_tokens,
    tgt_tokens,
    src_segments,
    tgt_lengths,
    mask_order,
    attn_project,
    attn_output,
    ffn_expand,
    ffn_reduce,
    norm_gains,
    length_table,
    embedding,
    momentum_attn_project,
    momentum_attn_output,
    momentum_ffn_expand,
    momentum_ffn_reduce,
    momentum_norm_gains,
    momentum_length_table,
    momentum_embedding,
    average_attn_project,
    average_attn_output,
    average_ffn_expand,
    average_ffn_reduce,
    average_norm_gains,
    average_length_table,
    average_embedding,
):
    masters = (
        attn_project,
        attn_output,
        ffn_expand,
        ffn_reduce,
        norm_gains,
        length_table,
        embedding,
    )
    moments = (
        momentum_attn_project,
        momentum_attn_output,
        momentum_ffn_expand,
        momentum_ffn_reduce,
        momentum_norm_gains,
        momentum_length_table,
        momentum_embedding,
    )
    averages = (
        average_attn_project,
        average_attn_output,
        average_ffn_expand,
        average_ffn_reduce,
        average_norm_gains,
        average_length_table,
        average_embedding,
    )
    w_in, w_out, w_up, w_down, gain_low, table, embed = (
        lax.all_gather(attn_project.astype(jnp.bfloat16), "dp", axis=1, tiled=True),
        lax.all_gather(attn_output.astype(jnp.bfloat16), "dp", axis=1, tiled=True),
        lax.all_gather(ffn_expand.astype(jnp.bfloat16), "dp", axis=1, tiled=True),
        lax.all_gather(ffn_reduce.astype(jnp.bfloat16), "dp", axis=1, tiled=True),
        lax.all_gather(norm_gains.astype(jnp.bfloat16), "dp", axis=1, tiled=True),
        lax.all_gather(length_table.astype(jnp.bfloat16), "dp", axis=1, tiled=True),
        lax.all_gather(embedding.astype(jnp.bfloat16), "dp", axis=0, tiled=True),
    )
    gain = gain_low.astype(jnp.float32)
    weights = (w_in, w_out, w_up, w_down, gain)
    vocab_rows = embed.shape[0]
    start = lax.axis_index("vocab") * vocab_rows
    columns = jnp.arange(vocab_rows, dtype=jnp.int32)
    places = jnp.arange(ROW, dtype=jnp.int32)
    position = sinusoid(ROW, D)
    scale_in = math.sqrt(D)
    rows_here = src_tokens.shape[0]
    inverse = 1.0 / (SENTS * rows_here * lax.axis_size("dp"))
    class_ids = jnp.arange(LCLS, dtype=jnp.int32)
    sentence_ids = jnp.arange(SENTS, dtype=jnp.int32)
    gathered = None
    loss_local = jnp.zeros((), jnp.float32)
    for row in range(rows_here):
        source = src_tokens[row]
        target = tgt_tokens[row]
        segments = src_segments[row]
        lengths = tgt_lengths[row]
        masked = mask_order[row, :MASKED]
        flag = jnp.any(places[:, None] == masked[None, :], axis=1)
        dec_in = jnp.where(flag, MASK_TOKEN, target)
        bounds = jnp.cumsum(lengths)
        tsegs = jnp.sum((places[:, None] >= bounds[None, :]).astype(jnp.int32), axis=1)
        src_allowed = segments[:, None] == segments[None, :]
        tgt_allowed = tsegs[:, None] == tsegs[None, :]
        cross_allowed = tsegs[:, None] == segments[None, :]
        src_hot = (source[:, None] - start == columns[None, :]).astype(jnp.bfloat16)
        dec_hot = (dec_in[:, None] - start == columns[None, :]).astype(jnp.bfloat16)
        src_emb, dec_emb = (
            lax.psum(
                jnp.dot(src_hot, embed, preferred_element_type=jnp.float32).astype(jnp.bfloat16),
                "vocab",
            ).astype(jnp.float32),
            lax.psum(
                jnp.dot(dec_hot, embed, preferred_element_type=jnp.float32).astype(jnp.bfloat16),
                "vocab",
            ).astype(jnp.float32),
        )
        enc_top, enc_kept = layer_fwd(
            scale_in * src_emb + position, weights, 0, src_allowed, None, None
        )
        dec_top, dec_kept = layer_fwd(
            scale_in * dec_emb + position, weights, 1, tgt_allowed, enc_top, cross_allowed
        )
        top_low = dec_top[masked].astype(jnp.bfloat16)
        logits = jnp.einsum("md,vd->mv", top_low, embed, preferred_element_type=jnp.float32)
        target_hot = masked_hot = target[masked][:, None] - start == columns[None, :]
        picked = jnp.sum(jnp.where(target_hot, logits, 0.0), axis=1)
        row_peak = lax.pmax(jnp.max(logits, axis=1), "vocab")
        row_total, row_pick = lax.psum(
            (jnp.sum(jnp.exp(logits - row_peak[:, None]), axis=1), picked), "vocab"
        )
        log_total = row_peak + jnp.log(row_total)
        token_loss = log_total - row_pick
        member = (segments[None, :] == sentence_ids[:, None]).astype(jnp.float32)
        members = jnp.sum(member, axis=1, keepdims=True)
        pooled_low = (jnp.dot(member, enc_top, precision=HIGHEST) / members).astype(jnp.bfloat16)
        length_logits = jnp.einsum(
            "sd,cd->sc", pooled_low, table, preferred_element_type=jnp.float32
        )
        length_total = jax.nn.logsumexp(length_logits, axis=1)
        class_hot = (lengths[:, None] - 1 == class_ids[None, :]).astype(jnp.float32)
        length_loss = length_total - jnp.sum(length_logits * class_hot, axis=1)
        loss_local = loss_local + jnp.sum(token_loss) + LENGTH_WEIGHT * jnp.sum(length_loss)
        grad_logits = (
            (jnp.exp(logits - log_total[:, None]) - masked_hot.astype(jnp.float32)) * inverse
        ).astype(jnp.bfloat16)
        grad_embed = jnp.einsum(
            "mv,md->vd", grad_logits, top_low, preferred_element_type=jnp.float32
        )
        grad_rows = lax.psum(
            jnp.einsum("mv,vd->md", grad_logits, embed, preferred_element_type=jnp.float32).astype(
                jnp.bfloat16
            ),
            "vocab",
        ).astype(jnp.float32)
        grad_top = jnp.zeros((ROW, D), jnp.float32).at[masked].set(grad_rows)
        grad_length = (
            (jnp.exp(length_logits - length_total[:, None]) - class_hot) * (LENGTH_WEIGHT * inverse)
        ).astype(jnp.bfloat16)
        grad_table = jnp.einsum(
            "sc,sd->cd", grad_length, pooled_low, preferred_element_type=jnp.float32
        )
        grad_pooled = jnp.einsum(
            "sc,cd->sd", grad_length, table, preferred_element_type=jnp.float32
        )
        grad_enc = jnp.dot(member.T, grad_pooled / members, precision=HIGHEST)
        dec_stream, memory_grad, dec_gains, dec_attn, dec_ffn = layer_bwd(
            grad_top, dec_kept, weights, 1
        )
        enc_stream, _, enc_gains, enc_attn, enc_ffn = layer_bwd(
            grad_enc + memory_grad, enc_kept, weights, 0
        )
        grad_embed = grad_embed + jnp.einsum(
            "rv,rd->vd",
            src_hot,
            (scale_in * enc_stream).astype(jnp.bfloat16),
            preferred_element_type=jnp.float32,
        )
        grad_embed = grad_embed + jnp.einsum(
            "rv,rd->vd",
            dec_hot,
            (scale_in * dec_stream).astype(jnp.bfloat16),
            preferred_element_type=jnp.float32,
        )
        grads = (
            jnp.stack([enc_attn[0][0], dec_attn[1][0], dec_attn[2][0]]),
            jnp.stack([enc_attn[0][1], dec_attn[1][1], dec_attn[2][1]]),
            jnp.stack([enc_ffn[0], dec_ffn[0]]),
            jnp.stack([enc_ffn[1], dec_ffn[1]]),
            jnp.stack(enc_gains + dec_gains),
            grad_table,
            grad_embed,
        )
        gathered = (
            grads
            if gathered is None
            else tuple((left + right for left, right in zip(gathered, grads)))
        )
    reduced = (
        lax.psum_scatter(gathered[0], "dp", scatter_dimension=1, tiled=True),
        lax.psum_scatter(gathered[1], "dp", scatter_dimension=1, tiled=True),
        lax.psum_scatter(gathered[2], "dp", scatter_dimension=1, tiled=True),
        lax.psum_scatter(gathered[3], "dp", scatter_dimension=1, tiled=True),
        lax.psum_scatter(gathered[4], "dp", scatter_dimension=1, tiled=True),
        lax.psum_scatter(gathered[5], "dp", scatter_dimension=1, tiled=True),
        lax.psum_scatter(gathered[6], "dp", scatter_dimension=0, tiled=True),
    )
    layer_squares = jnp.zeros((), jnp.float32)
    for grad in reduced[:6]:
        layer_squares = layer_squares + jnp.sum(grad * grad)
    table_squares = jnp.sum(reduced[6] * reduced[6])
    vocab_count = lax.axis_size("vocab")
    squares, loss_sum = lax.psum(
        (layer_squares / vocab_count + table_squares, loss_local / vocab_count), ("dp", "vocab")
    )
    grad_norm = jnp.sqrt(squares)
    factor = jnp.minimum(1.0, CLIP / grad_norm)
    rate = RATE_SCALE * math.sqrt(NPARAM / D) / CLIP
    fresh, moved, smooth, copies = ([], [], [], [])
    for weight, grad, moment, average, boost in zip(
        masters, reduced, moments, averages, RATE_FACTORS
    ):
        clipped = grad * factor
        moment = MOMENTUM * moment + clipped
        weight = weight - boost * rate * (clipped + MOMENTUM * moment)
        average = KEEP * average + (1.0 - KEEP) * weight
        fresh.append(weight)
        moved.append(moment)
        smooth.append(average)
        copies.append(weight.astype(jnp.bfloat16))
    return (loss_sum, grad_norm) + tuple(fresh) + tuple(moved) + tuple(smooth) + tuple(copies)


def solution(mesh):
    return jax.shard_map(
        shards,
        mesh=mesh,
        in_specs=(
            P("dp", None),
            P("dp", None),
            P("dp", None),
            P("dp", None),
            P("dp", None),
            P(None, "dp", None),
            P(None, "dp", None),
            P(None, "dp", None),
            P(None, "dp", None),
            P(None, "dp"),
            P(None, "dp"),
            P(("vocab", "dp"), None),
            P(None, "dp", None),
            P(None, "dp", None),
            P(None, "dp", None),
            P(None, "dp", None),
            P(None, "dp"),
            P(None, "dp"),
            P(("vocab", "dp"), None),
            P(None, "dp", None),
            P(None, "dp", None),
            P(None, "dp", None),
            P(None, "dp", None),
            P(None, "dp"),
            P(None, "dp"),
            P(("vocab", "dp"), None),
        ),
        out_specs=(
            P(),
            P(),
            P(None, "dp", None),
            P(None, "dp", None),
            P(None, "dp", None),
            P(None, "dp", None),
            P(None, "dp"),
            P(None, "dp"),
            P(("vocab", "dp"), None),
            P(None, "dp", None),
            P(None, "dp", None),
            P(None, "dp", None),
            P(None, "dp", None),
            P(None, "dp"),
            P(None, "dp"),
            P(("vocab", "dp"), None),
            P(None, "dp", None),
            P(None, "dp", None),
            P(None, "dp", None),
            P(None, "dp", None),
            P(None, "dp"),
            P(None, "dp"),
            P(("vocab", "dp"), None),
            P(None, "dp", None),
            P(None, "dp", None),
            P(None, "dp", None),
            P(None, "dp", None),
            P(None, "dp"),
            P(None, "dp"),
            P(("vocab", "dp"), None),
        ),
        check_vma=False,
    )
```

profile of v0, /device:TPU:0, one launch (start us, length us, event | category | flops | bytes accessed | tf_op | source)
XLA Modules:
  0.0 1549.0 jit_solution(11471495711738088604)
XLA Ops:
  7.3 2.7 convert_element_type.503
  11.2 126.9 %all-gather.7.cloned.1.call-done = bf16[16000,512]{1,0:T(8,128)(2,1)} async-done(((bf16[1000,512]{1,0:T(8,128)(2,1)}), bf16[16000,512]{1,0:T(8,128)(2,1)}) %all-gather.7.cloned.1.call-update) | async-done | bytes 16384016 | tf_op jit(solution)/shard_map/all_gather | solution.py:253
  138.0 11.3 fusion.90
  149.4 5.2 fusion.89
  154.5 5.2 fusion.88
  159.7 5.2 fusion.87
  172.8 18.8 %all-gather = bf16[16,32,7]{1,2,0:T(8,128)(2,1)S(1)} all-gather(bf16[1,32,7]{1,2,0:T(8,128)(2,1)S(1)} %convert_bitcast_fusion), channel_id=1, replica_groups=mesh['dp'=16,'vocab'=2] {'dp'}, dimensions={0}, use_global_device_ids=true | all-gather | bytes 7616 | tf_op jit(solution)/shard_map/all_gather | solution.py:251
  193.8 18.4 %all_gather.27 = bf16[256,512]{0,1:T(8,128)(2,1)S(1)} all-gather(bf16[256,32]{0,1:T(8,128)(2,1)S(1)} %convert_element_type.544), channel_id=1, replica_groups=mesh['dp'=16,'vocab'=2] {'dp'}, dimensions={1}, use_global_device_ids=true | all-gather | bytes 278528 | tf_op jit(solution)/shard_map/all_gather | solution.py:252
  213.8 4.7 slice_bitcast_fusion.5
  218.4 17.0 %all-reduce.10.cloned.1.call-done = (bf16[256,512]{1,0:T(8,128)(2,1)}, bf16[256,512]{1,0:T(8,128)(2,1)}, bf16[256,512]{1,0:T(8,128)(2,1)}, bf16[256,512]{1,0:T(8,128)(2,1)}) async-done(((bf16[256,512]{1,0:T(8,128)(2,1)}, bf16[256,512]{1,0:T(8,128)(2,1)}, bf16[256,512]{1,0:T(8,128)(2,1)}, bf16[256,512]{1,0:T(8,128)(2,1)}), (bf16[256,512]{1,0:T(8,128)(2,1)}, bf16[256,512]{1,0:T(8,128)(2,1)}, ...) | async-done | bytes 1048592 | tf_op jit(solution)/shard_map/psum | solution.py:289
  242.6 2.2 fusion.317
  246.7 31.3 %all-gather.11.cloned.1.call-done = bf16[3,512,512]{2,1,0:T(8,128)(2,1)} async-done(((bf16[3,32,512]{2,1,0:T(8,128)(2,1)}), bf16[3,512,512]{2,1,0:T(8,128)(2,1)}) %all-gather.11.cloned.1.call-update) | async-done | bytes 1572880 | tf_op jit(solution)/shard_map/all_gather | solution.py:248
  285.4 45.0 %all-gather.13.cloned.1.call-done = bf16[2,512,2048]{2,1,0:T(8,128)(2,1)} async-done(((bf16[2,32,2048]{2,1,0:T(8,128)(2,1)}), bf16[2,512,2048]{2,1,0:T(8,128)(2,1)}) %all-gather.13.cloned.1.call-update) | async-done | bytes 4194320 | tf_op jit(solution)/shard_map/all_gather | solution.py:249
  330.4 3.7 fusion.58
  334.0 48.3 %all-gather.15.cloned.1.call-done = bf16[2,2048,512]{2,1,0:T(8,128)(2,1)} async-done(((bf16[2,128,512]{2,1,0:T(8,128)(2,1)}), bf16[2,2048,512]{2,1,0:T(8,128)(2,1)}) %all-gather.15.cloned.1.call-update) | async-done | bytes 4194320 | tf_op jit(solution)/shard_map/all_gather | solution.py:250
  382.3 3.1 fusion.319
  398.0 2.2 fusion.316
  400.2 2.1 convolution_convert_fusion.28
  406.7 2.4 fusion.308
  411.8 2.2 convolution_convert_fusion.19
  415.8 2.2 fusion.309
  418.0 2.1 convolution_convert_fusion.20
  431.6 2.2 fusion.313
  433.8 2.1 convolution_convert_fusion.18
  443.2 2.1 fusion.321
  445.4 2.0 convolution_convert_fusion.24
  455.3 13.3 fusion.324
  468.7 13.4 fusion.325
  482.1 5.4 all-reduce.2
  487.5 5.1 select_reduce_fusion.1
  492.7 2.4 select_reduce_fusion
  495.1 5.6 all-reduce.1
  503.4 10.8 convolution_convert_fusion.30
  514.1 8.8 convolution_convert_fusion.31
  525.1 19.0 %all-reduce.8.cloned.1.call-done = (bf16[96,512]{1,0:T(8,128)(2,1)}, bf16[96,512]{1,0:T(8,128)(2,1)}) async-done(((bf16[96,512]{1,0:T(8,128)(2,1)}, bf16[96,512]{1,0:T(8,128)(2,1)}), (bf16[96,512]{1,0:T(8,128)(2,1)}, bf16[96,512]{1,0:T(8,128)(2,1)})) %all-reduce.8.cloned.1.call-update) | async-done | bytes 196624 | tf_op jit(solution)/shard_map/psum | solution.py:326
  545.6 2.3 scatter_custom_fusion.1
  548.0 2.1 multiply_reduce_fusion.12
  552.6 3.5 fusion.34
  563.6 2.9 convolution_convert_fusion.10
  570.9 2.2 convolution_convert_fusion.16
  592.2 3.0 convolution_convert_fusion.8
  600.2 2.9 convolution_convert_fusion.14
  611.7 3.0 convolution_convert_fusion.6
  620.8 2.2 convolution_convert_fusion.12
  629.8 2.1 multiply_reduce_fusion.11
  641.1 2.4 maximum_add_fusion.3
  644.2 2.8 convolution_bitcast_fusion.2
  651.4 4.2 maximum_add_fusion.2
  656.3 2.2 convolution_bitcast_fusion.7
  662.2 4.0 maximum_add_fusion.1
  667.1 16.4 %fusion.217 = f32[16000,512]{1,0:T(8,128)} fusion(bf16[96,512]{1,0:T(8,128)(2,1)S(1)} %copy-done.197, f32[96,16000]{1,0:T(8,128)} %get-tuple-element.262, f32[96]{0:T(128)S(1)} %copy-done.347, s32[96]{0:T(128)S(1)} %copy-done.302), kind=kOutput, calls=%fused_computation.491 | convolution fusion | flops 1582080000 | bytes 39011072 | tf_op jit(solution)/shard_map/mv,md->vd/dot_general | solution.py:323
  683.6 16.7 %fusion.213 = f32[16000,512]{1,0:T(8,128)} fusion(bf16[96,512]{1,0:T(8,128)(2,1)S(1)} %copy-done.195, f32[96,16000]{1,0:T(8,128)} %get-tuple-element.264, f32[96]{0:T(128)S(1)} %copy-done.349, s32[96]{0:T(128)S(1)} %copy-done.299), kind=kOutput, calls=%fused_computation.487 | convolution fusion | flops 1582080000 | bytes 39011072 | tf_op jit(solution)/shard_map/mv,md->vd/dot_general | solution.py:323
  713.5 5.1 maximum_add_fusion
  719.8 15.7 %fusion.11 = f32[16000,512]{1,0:T(8,128)} fusion(s32[256]{0:T(256)S(1)} %copy-done.316, f32[256,512]{1,0:T(8,128)S(1)} %copy-done.45, f32[256,512]{1,0:T(8,128)S(1)} %copy-done.122, f32[256]{0:T(256)S(1)} %negate_multiply_fusion.2), kind=kOutput, calls=%fused_computation.22 | convolution fusion | flops 4198924288 | bytes 33818624 | tf_op jit(solution)/shard_map/rv,rd->vd/dot_general | solution.py:355
  735.6 15.2 fusion.6
  750.8 16.2 %fusion.9 = f32[16000,512]{1,0:T(8,128)} fusion(s32[256]{0:T(256)S(1)} %bitcast.562, f32[256,512]{1,0:T(8,128)S(1)} %copy-done.39, f32[256,512]{1,0:T(8,128)S(1)} %copy-done.119, f32[256]{0:T(256)S(1)} %negate_multiply_fusion.3), kind=kOutput, calls=%fused_computation.19 | convolution fusion | flops 4198924288 | bytes 33818624 | tf_op jit(solution)/shard_map/rv,rd->vd/dot_general | solution.py:349
  767.0 63.2 %add_add_fusion = f32[16000,512]{1,0:T(8,128)} fusion(f32[16000,512]{1,0:T(8,128)} %fusion.213, f32[16000,512]{1,0:T(8,128)} %fusion.6, f32[16000,512]{1,0:T(8,128)} %fusion.11, f32[16000,512]{1,0:T(8,128)} %fusion.217, f32[16000,512]{1,0:T(8,128)} %fusion.9, s32[256]{0:T(256)S(1)} %copy-done.308, f32[256,512]{1,0:T(8,128)S(1)} %copy-done.42, ...), kind=kOutput, calls=%fused_computation.12 | convolution fusion | flops 4239884288 | bytes 197658624 | tf_op jit(solution)/shard_map/rv,rd->vd/dot_general | solution.py:355
  837.5 89.0 %reduce-scatter.16.cloned.1.call-done = f32[2,128,512]{2,1,0:T(8,128)} async-done(((f32[2,2048,512]{2,1,0:T(8,128)}), f32[2,128,512]{2,1,0:T(8,128)}) %reduce-scatter.16.cloned.1.call-update) | async-done | bytes 524304 | tf_op jit(solution)/shard_map/reduce_scatter | solution.py:379
  928.3 106.5 %reduce-scatter.14.cloned.1.call-done = f32[2,32,2048]{2,1,0:T(8,128)} async-done(((f32[2,512,2048]{2,1,0:T(8,128)}), f32[2,32,2048]{2,1,0:T(8,128)}) %reduce-scatter.14.cloned.1.call-update) | async-done | bytes 524304 | tf_op jit(solution)/shard_map/reduce_scatter | solution.py:378
  1036.6 113.5 %reduce-scatter.10.cloned.1.call-done = f32[3,32,1536]{2,1,0:T(8,128)} async-done(((f32[3,512,1536]{2,1,0:T(8,128)}), f32[3,32,1536]{2,1,0:T(8,128)}) %reduce-scatter.10.cloned.1.call-update) | async-done | bytes 589840 | tf_op jit(solution)/shard_map/reduce_scatter | solution.py:376
  1155.9 326.4 %reduce-scatter.20.cloned.1.call-done = f32[1000,512]{1,0:T(8,128)} async-done(((f32[16000,512]{1,0:T(8,128)}), f32[1000,512]{1,0:T(8,128)}) %reduce-scatter.20.cloned.1.call-update) | async-done | bytes 2048016 | tf_op jit(solution)/shard_map/reduce_scatter | solution.py:382
  1482.3 2.7 multiply_reduce_fusion.6
  1485.7 39.2 %all-reduce = (f32[]{:T(128)}, f32[]{:T(128)}) all-reduce(f32[]{:T(128)S(6)} %div.391, f32[]{:T(128)S(6)} %add.562), channel_id=1, replica_groups=mesh['dp'=16,'vocab'=2] {'dp','vocab'}, use_global_device_ids=true, to_apply=%region_74.75 | all-reduce | flops 2 | bytes 16 | tf_op jit(solution)/shard_map/psum | solution.py:389
  1536.8 2.4 fusion.274
  (1231 shorter events, 195.5 us)
Async XLA Ops:
  7.2 130.8 %all-gather.7.cloned.1.call-start = ((), (), s32[]{:S(2)}) async-start(), calls=%async_computation.7 | async-start | bytes 17408000 | tf_op jit(solution)/shard_map/all_gather | solution.py:253
  10.0 203.7 %all-gather.9.cloned.1.call-start = ((), (), s32[]{:S(2)}) async-start(), calls=%async_computation.8 | async-start | bytes 5013504 | tf_op jit(solution)/shard_map/all_gather | solution.py:247
  10.9 224.6 %all-reduce.10.cloned.1.call-start = ((), (), s32[]{:S(2)}) async-start(), calls=%async_computation.20 | async-start | bytes 2097152 | tf_op jit(solution)/shard_map/psum | solution.py:289
  11.1 148.6 %copy-start.315 = (s32[256]{0:T(256)}, s32[256]{0:T(256)S(1)}, u32[]{:S(2)}) copy-start(s32[256]{0:T(256)S(1)} %select_subtract_fusion.1) | copy-start | bytes 3076
  11.1 138.2 %copy-start.307 = (s32[256]{0:T(256)}, s32[256]{0:T(256)S(1)}, u32[]{:S(2)}) copy-start(s32[256]{0:T(256)S(1)} %select_subtract_fusion) | copy-start | bytes 3076
  11.1 138.2 %copy-start.341 = (s32[1,256]{1,0:T(1,128)}, s32[1,256]{1,0:T(1,128)S(1)}, u32[]{:S(2)}) copy-start(s32[1,256]{1,0:T(1,128)S(1)} %get-tuple-element.211) | copy-start | bytes 3076
  11.1 143.4 %copy-start.339 = (s32[1,256]{1,0:T(1,128)}, s32[1,256]{1,0:T(1,128)S(1)}, u32[]{:S(2)}) copy-start(s32[1,256]{1,0:T(1,128)S(1)} %get-tuple-element.212) | copy-start | bytes 3076
  165.3 112.7 %all-gather.11.cloned.1.call-start = ((), (), s32[]{:S(2)}) async-start(), calls=%async_computation.9 | async-start | bytes 1671168 | tf_op jit(solution)/shard_map/all_gather | solution.py:248
  166.1 164.3 %all-gather.13.cloned.1.call-start = ((), (), s32[]{:S(2)}) async-start(), calls=%async_computation.10 | async-start | bytes 4456448 | tf_op jit(solution)/shard_map/all_gather | solution.py:249
  166.9 215.4 %all-gather.15.cloned.1.call-start = ((), (), s32[]{:S(2)}) async-start(), calls=%async_computation.11 | async-start | bytes 4456448 | tf_op jit(solution)/shard_map/all_gather | solution.py:250
  167.7 376.5 %all-reduce.8.cloned.1.call-start = ((), (), s32[]{:S(2)}) async-start(), calls=%async_computation.19 | async-start | bytes 393216 | tf_op jit(solution)/shard_map/psum | solution.py:326
  167.8 23.8 %copy-start.428 = (s32[96]{0:T(128)}, s32[96]{0:T(128)S(1)}, u32[]{:S(2)}) copy-start(s32[96]{0:T(128)S(1)} %get-tuple-element.201) | copy-start | bytes 1156
  167.8 23.8 %copy-start.429 = (s32[96]{0:T(128)}, s32[96]{0:T(128)S(1)}, u32[]{:S(2)}) copy-start(s32[96]{0:T(128)S(1)} %get-tuple-element.202) | copy-start | bytes 1156
  168.9 49.6 %copy-start.296 = (s32[1,256]{1,0:T(1,128)}, s32[1,256]{1,0:T(1,128)S(1)}, u32[]{:S(2)}) copy-start(s32[1,256]{1,0:T(1,128)S(1)} %get-tuple-element.205) | copy-start | bytes 3076
  168.9 216.9 %copy-start.295 = (s32[1,256]{1,0:T(1,128)}, s32[1,256]{1,0:T(1,128)S(1)}, u32[]{:S(2)}) copy-start(s32[1,256]{1,0:T(1,128)S(1)} %get-tuple-element.206) | copy-start | bytes 3076
  192.2 45.7 %copy-start.305 = (f32[1,512]{1,0:T(1,128)}, f32[1,512]{1,0:T(1,128)S(1)}, u32[]{:S(2)}) copy-start(f32[1,512]{1,0:T(1,128)S(1)} %get-tuple-element.175) | copy-start | bytes 6148
  192.2 88.7 %copy-start.303 = (f32[1,512]{1,0:T(1,128)}, f32[1,512]{1,0:T(1,128)S(1)}, u32[]{:S(2)}) copy-start(f32[1,512]{1,0:T(1,128)S(1)} %get-tuple-element.176) | copy-start | bytes 6148
  212.3 175.6 %copy-start.97 = (bf16[256,512]{0,1:T(8,128)(2,1)}, bf16[256,512]{0,1:T(8,128)(2,1)S(1)}, u32[]{:S(2)}) copy-start(bf16[256,512]{0,1:T(8,128)(2,1)S(1)} %all_gather.27) | copy-start | bytes 786436
  237.0 41.1 %copy-start.31 = (f32[256,512]{1,0:T(8,128)}, f32[256,512]{1,0:T(8,128)S(1)}, u32[]{:S(2)}) copy-start(f32[256,512]{1,0:T(8,128)S(1)} %get-tuple-element.157) | copy-start | bytes 1572868
  237.0 165.4 %copy-start.25 = (f32[256,512]{1,0:T(8,128)}, f32[256,512]{1,0:T(8,128)S(1)}, u32[]{:S(2)}) copy-start(f32[256,512]{1,0:T(8,128)S(1)} %get-tuple-element.161) | copy-start | bytes 1572868
  237.0 174.1 %copy-start.23 = (f32[256,512]{1,0:T(8,128)}, f32[256,512]{1,0:T(8,128)S(1)}, u32[]{:S(2)}) copy-start(f32[256,512]{1,0:T(8,128)S(1)} %get-tuple-element.159) | copy-start | bytes 1572868
  238.2 45.0 %copy-start.113 = (bf16[256,512]{1,0:T(8,128)(2,1)}, bf16[256,512]{1,0:T(8,128)(2,1)S(1)}, u32[]{:S(2)}) copy-start(bf16[256,512]{1,0:T(8,128)(2,1)S(1)} %get-tuple-element.207) | copy-start | bytes 786436
  242.1 38.9 %copy-start.317 = (f32[256]{0:T(256)}, f32[256]{0:T(256)S(1)}, u32[]{:S(2)}) copy-start(f32[256]{0:T(256)S(1)} %broadcast_multiply_fusion.13) | copy-start | bytes 3076
  242.3 37.5 %copy-start.372 = (f32[256]{0:T(256)}, f32[256]{0:T(256)S(1)}, u32[]{:S(2)}) copy-start(f32[256]{0:T(256)S(1)} %multiply_reduce_fusion.51) | copy-start | bytes 3076
  242.3 38.6 %copy-start.320 = (f32[256]{0:T(256)}, f32[256]{0:T(256)S(1)}, u32[]{:S(2)}) copy-start(f32[256]{0:T(256)S(1)} %broadcast_multiply_fusion.6) | copy-start | bytes 3076
  242.5 37.3 %copy-start.374 = (f32[256]{0:T(256)}, f32[256]{0:T(256)S(1)}, u32[]{:S(2)}) copy-start(f32[256]{0:T(256)S(1)} %multiply_reduce_fusion.44) | copy-start | bytes 3076
  246.7 34.5 %copy-start.148 = (bf16[8,64,256]{2,1,0:T(8,128)(2,1)}, bf16[8,64,256]{2,1,0:T(8,128)(2,1)S(1)}, u32[]{:S(2)}) copy-start(bf16[8,64,256]{2,1,0:T(8,128)(2,1)S(1)} %convolution_convert_fusion.26) | copy-start | bytes 786436
  279.6 102.7 %copy-start.12 = (f32[256,512]{1,0:T(8,128)}, f32[256,512]{1,0:T(8,128)S(1)}, u32[]{:S(2)}) copy-start(f32[256,512]{1,0:T(8,128)S(1)} %get-tuple-element.250) | copy-start | bytes 1572868
  279.6 50.7 %copy-start.251 = (f32[256]{0:T(256)}, f32[256]{0:T(256)S(1)}, u32[]{:S(2)}) copy-start(f32[256]{0:T(256)S(1)} %broadcast_multiply_fusion.11) | copy-start | bytes 3076
  279.9 50.4 %copy-start.279 = (f32[256]{0:T(256)}, f32[256]{0:T(256)S(1)}, u32[]{:S(2)}) copy-start(f32[256]{0:T(256)S(1)} %fusion.229) | copy-start | bytes 3076
  334.0 52.3 %copy-start.442 = (f32[8]{0:T(128)S(1)}, f32[8]{0:T(128)}, u32[]{:S(2)}) copy-start(f32[8]{0:T(128)} %convert_reduce_fusion.2) | copy-start | bytes 100
  402.8 44.7 %copy-start.3 = (f32[256,512]{1,0:T(8,128)}, f32[256,512]{1,0:T(8,128)S(1)}, u32[]{:S(2)}) copy-start(f32[256,512]{1,0:T(8,128)S(1)} %get-tuple-element.254) | copy-start | bytes 1572868
  411.5 24.5 %copy-start.5 = (f32[256,512]{1,0:T(8,128)}, f32[256,512]{1,0:T(8,128)S(1)}, u32[]{:S(2)}) copy-start(f32[256,512]{1,0:T(8,128)S(1)} %get-tuple-element.238) | copy-start | bytes 1572868
  523.0 25.0 %copy-start.70 = (f32[256,512]{1,0:T(8,128)S(1)}, f32[256,512]{1,0:T(8,128)}, u32[]{:S(2)}) copy-start(f32[256,512]{1,0:T(8,128)} %copy-done.68) | copy-start | bytes 1572868
  523.0 25.0 %copy-start.72 = (f32[256,512]{1,0:T(8,128)S(1)}, f32[256,512]{1,0:T(8,128)}, u32[]{:S(2)}) copy-start(f32[256,512]{1,0:T(8,128)} %copy-done.71) | copy-start | bytes 1572868
  523.0 27.1 %copy-start.397 = (f32[256]{0:T(256)S(1)}, f32[256]{0:T(256)}, u32[]{:S(2)}) copy-start(f32[256]{0:T(256)} %copy-done.396) | copy-start | bytes 3076
  523.0 27.2 %copy-start.395 = (f32[256]{0:T(256)S(1)}, f32[256]{0:T(256)}, u32[]{:S(2)}) copy-start(f32[256]{0:T(256)} %copy-done.394) | copy-start | bytes 3076
  523.0 27.2 %copy-start.266 = (f32[1,512]{1,0:T(1,128)S(1)}, f32[1,512]{1,0:T(1,128)}, u32[]{:S(2)}) copy-start(f32[1,512]{1,0:T(1,128)} %get-tuple-element.170) | copy-start | bytes 6148
  523.0 27.2 %copy-start.292 = (f32[256]{0:T(256)S(1)}, f32[256]{0:T(256)}, u32[]{:S(2)}) copy-start(f32[256]{0:T(256)} %copy-done.291) | copy-start | bytes 3076
  523.0 27.2 %copy-start.294 = (f32[256]{0:T(256)S(1)}, f32[256]{0:T(256)}, u32[]{:S(2)}) copy-start(f32[256]{0:T(256)} %copy-done.293) | copy-start | bytes 3076
  523.0 27.2 %copy-start.336 = (f32[256]{0:T(256)S(1)}, f32[256]{0:T(256)}, u32[]{:S(2)}) copy-start(f32[256]{0:T(256)} %copy-done.335) | copy-start | bytes 3076
  523.0 27.2 %copy-start.338 = (f32[256]{0:T(256)S(1)}, f32[256]{0:T(256)}, u32[]{:S(2)}) copy-start(f32[256]{0:T(256)} %copy-done.337) | copy-start | bytes 3076
  523.1 309.8 %reduce-scatter.22.cloned.1.call-start = ((), (), s32[]{:S(2)}) async-start(), calls=%async_computation.18 | async-start | bytes 278528
  575.0 31.9 %copy-start.94 = (bf16[8,64,256]{2,1,0:T(8,128)(2,1)}, bf16[8,64,256]{2,1,0:T(8,128)(2,1)S(1)}, u32[]{:S(2)}) copy-start(bf16[8,64,256]{2,1,0:T(8,128)(2,1)S(1)} %fusion.78) | copy-start | bytes 786436
  635.2 199.1 %reduce-scatter.18.cloned.1.call-start = ((), (), s32[]{:S(2)}) async-start(), calls=%async_computation.16 | async-start | bytes 557056 | tf_op jit(solution)/shard_map/reduce_scatter | solution.py:381
  636.4 199.4 %reduce-scatter.12.cloned.1.call-start = ((), (), s32[]{:S(2)}) async-start(), calls=%async_computation.13 | async-start | bytes 3342336 | tf_op jit(solution)/shard_map/reduce_scatter | solution.py:377
  643.6 282.9 %reduce-scatter.16.cloned.1.call-start = ((), (), s32[]{:S(2)}) async-start(), calls=%async_computation.15 | async-start | bytes 8912896 | tf_op jit(solution)/shard_map/reduce_scatter | solution.py:379
  655.7 379.1 %reduce-scatter.14.cloned.1.call-start = ((), (), s32[]{:S(2)}) async-start(), calls=%async_computation.14 | async-start | bytes 8912896 | tf_op jit(solution)/shard_map/reduce_scatter | solution.py:378
  666.3 483.8 %reduce-scatter.10.cloned.1.call-start = ((), (), s32[]{:S(2)}) async-start(), calls=%async_computation.12 | async-start | bytes 10027008 | tf_op jit(solution)/shard_map/reduce_scatter | solution.py:376
  718.6 763.7 %reduce-scatter.20.cloned.1.call-start = ((), (), s32[]{:S(2)}) async-start(), calls=%async_computation.17 | async-start | bytes 34816000 | tf_op jit(solution)/shard_map/reduce_scatter | solution.py:382
  830.3 695.4 %copy-start.345 = (f32[7,32]{1,0:T(8,128)S(1)}, f32[7,32]{1,0:T(8,128)}, u32[]{:S(2)}) copy-start(f32[7,32]{1,0:T(8,128)} %param.35) | copy-start | bytes 2692
  830.3 695.3 %copy-start.419 = (f32[7,32]{1,0:T(8,128)S(1)}, f32[7,32]{1,0:T(8,128)}, u32[]{:S(2)}) copy-start(f32[7,32]{1,0:T(8,128)} %param.42) | copy-start | bytes 2692
  830.3 695.9 %copy-start.418 = (f32[7,32]{1,0:T(8,128)S(1)}, f32[7,32]{1,0:T(8,128)}, u32[]{:S(2)}) copy-start(f32[7,32]{1,0:T(8,128)} %param.49) | copy-start | bytes 2692
  830.3 696.5 %copy-start.245 = (f32[256,32]{0,1:T(8,128)S(1)}, f32[256,32]{0,1:T(8,128)}, u32[]{:S(2)}) copy-start(f32[256,32]{0,1:T(8,128)} %param.36) | copy-start | bytes 98308
  830.3 696.5 %copy-start.264 = (f32[256,32]{0,1:T(8,128)S(1)}, f32[256,32]{0,1:T(8,128)}, u32[]{:S(2)}) copy-start(f32[256,32]{0,1:T(8,128)} %param.43) | copy-start | bytes 98308
  832.2 695.2 %copy-start.263 = (f32[256,32]{0,1:T(8,128)S(1)}, f32[256,32]{0,1:T(8,128)}, u32[]{:S(2)}) copy-start(f32[256,32]{0,1:T(8,128)} %param.50) | copy-start | bytes 98308
  834.3 692.5 %copy-start.246 = (f32[256,32]{0,1:T(8,128)S(1)}, f32[256,32]{0,1:T(8,128)}, u32[]{:S(2)}) copy-start(f32[256,32]{0,1:T(8,128)} %reduce-scatter.18.cloned.1.call-done) | copy-start | bytes 98308
  835.7 692.4 %copy-start.199 = (f32[3,32,512]{2,1,0:T(8,128)S(1)}, f32[3,32,512]{2,1,0:T(8,128)}, u32[]{:S(2)}) copy-start(f32[3,32,512]{2,1,0:T(8,128)} %param.32) | copy-start | bytes 589828
  835.7 692.4 %copy-start.242 = (f32[3,32,512]{2,1,0:T(8,128)S(1)}, f32[3,32,512]{2,1,0:T(8,128)}, u32[]{:S(2)}) copy-start(f32[3,32,512]{2,1,0:T(8,128)} %param.39) | copy-start | bytes 589828
  835.7 692.4 %copy-start.200 = (f32[3,32,512]{2,1,0:T(8,128)S(1)}, f32[3,32,512]{2,1,0:T(8,128)}, u32[]{:S(2)}) copy-start(f32[3,32,512]{2,1,0:T(8,128)} %reduce-scatter.12.cloned.1.call-done) | copy-start | bytes 589828
  1036.6 492.3 %copy-start.241 = (f32[3,32,512]{2,1,0:T(8,128)S(1)}, f32[3,32,512]{2,1,0:T(8,128)}, u32[]{:S(2)}) copy-start(f32[3,32,512]{2,1,0:T(8,128)} %param.46) | copy-start | bytes 589828
  1151.9 377.7 %copy-start.133 = (f32[2,32,2048]{2,1,0:T(8,128)S(1)}, f32[2,32,2048]{2,1,0:T(8,128)}, u32[]{:S(2)}) copy-start(f32[2,32,2048]{2,1,0:T(8,128)} %param.33) | copy-start | bytes 1572868
  1151.9 377.7 %copy-start.137 = (f32[2,32,2048]{2,1,0:T(8,128)S(1)}, f32[2,32,2048]{2,1,0:T(8,128)}, u32[]{:S(2)}) copy-start(f32[2,32,2048]{2,1,0:T(8,128)} %reduce-scatter.14.cloned.1.call-done) | copy-start | bytes 1572868
  1151.9 377.7 %copy-start.210 = (f32[2,32,2048]{2,1,0:T(8,128)S(1)}, f32[2,32,2048]{2,1,0:T(8,128)}, u32[]{:S(2)}) copy-start(f32[2,32,2048]{2,1,0:T(8,128)} %param.40) | copy-start | bytes 1572868
  (400 other events, 1463.0 us)
Sparse Core Ops, SparseCore 0:
  10.9 127.0 all-gather.6
  140.9 51.6 all-gather.8
  196.2 39.1 all-reduce.9
  238.3 39.7 all-gather.10
  280.9 49.4 all-gather.12
  333.2 49.0 all-gather.14
  523.2 20.9 all-reduce.7
  635.3 55.3 reduce-scatter.21
  695.2 54.7 reduce-scatter.17
  753.6 65.1 reduce-scatter.11
  822.9 103.4 reduce-scatter.15
  930.4 104.3 reduce-scatter.13
  1038.9 111.1 reduce-scatter.9
  1154.9 327.3 reduce-scatter.19
where the time goes:
time: 1550 us
  waiting for transfers between devices  923 us (60%)
  matrix products  353 us (23%)
  other arithmetic  87.7 us (6%)
  blocking collectives  87.4 us (6%)
  local copies, waits for them, and re-layouts  67.8 us (4%)
  between operations  29.1 us (2%)
    reduce_scatter x1, waiting for transfers between devices, shards(): lax.psum_scatter(gathered[6], 'dp', scatter_dimension=0, tiled=True)  326 us
    all_gather x1, waiting for transfers between devices, shards(): lax.all_gather(embedding.astype(jnp.bfloat16), 'dp', axis=0, tiled=True)  127 us
    reduce_scatter x1, waiting for transfers between devices, shards(): lax.psum_scatter(gathered[0], 'dp', scatter_dimension=1, tiled=True)  113 us
    reduce_scatter x1, waiting for transfers between devices, shards(): lax.psum_scatter(gathered[2], 'dp', scatter_dimension=1, tiled=True)  107 us
    reduce_scatter x1, waiting for transfers between devices, shards(): lax.psum_scatter(gathered[3], 'dp', scatter_dimension=1, tiled=True)  89 us
    dot_general x2, matrix products, shards(): jnp.einsum('rv,rd->vd', dec_hot, (scale_in * dec_stream).astype(jnp.bfloa...  78.9 us
    all_gather x1, waiting for transfers between devices, shards(): lax.all_gather(ffn_reduce.astype(jnp.bfloat16), 'dp', axis=1, tiled=True)  48.3 us
    all_gather x1, waiting for transfers between devices, shards(): lax.all_gather(ffn_expand.astype(jnp.bfloat16), 'dp', axis=1, tiled=True)  45 us
  transfers between devices with their start and end apart: 14, of which 10 were waited for; matrix products, arithmetic and copies ran while one was open for 17% of the time, Pallas kernels for 0%

commit v1 on v0

v1 whole, which is shorter than its diff:
```python
import math

import jax
import jax.numpy as jnp
from jax import lax
from jax.sharding import Mesh
from jax.sharding import PartitionSpec as P

D = 512
HDIM = 64
LCLS = 256
ROW = 256
SENTS = 8
MASKED = 96
NPARAM = 23858688


HIGHEST = lax.Precision.HIGHEST
EPSILON = 1e-05
MASK_TOKEN = 3
MOMENTUM = 0.9
KEEP = 0.9
CLIP = 0.02
LENGTH_WEIGHT = 0.1
NEGATIVE = -1e30
RATE_SCALE = 0.25
RATE_FACTORS = (1.0, 1.0, 1.0, 1.0, 6.0, 24.0, 1.0)


def layer_norm(stream, gain):
    centred = stream - jnp.mean(stream, axis=-1, keepdims=True)
    spread = jnp.mean(centred * centred, axis=-1, keepdims=True)
    return centred * lax.rsqrt(spread + EPSILON) * gain


def sinusoid(count, width):
    place = jnp.arange(count, dtype=jnp.float32)[:, None]
    index = jnp.arange(width // 2, dtype=jnp.float32)[None, :]
    angle = place * jnp.exp(-math.log(10000.0) * 2.0 * index / width)
    return jnp.concatenate([jnp.sin(angle), jnp.cos(angle)], axis=1)


SWAP = [(0, 1), (1, 0)]


def swap(value, axis):
    return lax.ppermute(value, axis, SWAP)


def shift(value, by):
    count = lax.axis_size("z")
    return lax.ppermute(value, "z", [(i, (i + by) % count) for i in range(count)])


def low(value):
    return value.astype(jnp.bfloat16)


def wide(value):
    return value.astype(jnp.float32)


def ring_gather(value):
    count = lax.axis_size("z")
    if count != 4:
        whole = lax.all_gather(value, "z", axis=0)
        here = lax.axis_index("z")
        return [
            lax.dynamic_index_in_dim(whole, (here - k) % count, 0, False) for k in range(count)
        ]
    half = value.shape[0] // 2
    below = shift(value, 1)
    above = shift(value, -1)
    far = jnp.concatenate([shift(below[:half], 1), shift(above[half:], -1)], axis=0)
    return [value, below, far, above]


def ring_scatter(blocks):
    count = lax.axis_size("z")
    if count != 4:
        here = lax.axis_index("z")
        order = (here - jnp.arange(count)) % count
        stacked = jnp.stack([low(block) for block in blocks])
        whole = jnp.zeros_like(stacked).at[order].set(stacked)
        return wide(lax.psum_scatter(whole, "z", scatter_dimension=0))
    half = blocks[0].shape[0] // 2
    from_above = shift(low(blocks[2][:half]), -1)
    from_below = shift(low(blocks[2][half:]), 1)
    down = jnp.concatenate([wide(blocks[1][:half]) + wide(from_above), wide(blocks[1][half:])])
    up = jnp.concatenate([wide(blocks[3][:half]), wide(blocks[3][half:]) + wide(from_below)])
    from_above = shift(low(down), -1)
    from_below = shift(low(up), 1)
    return wide(blocks[0]) + wide(from_above) + wide(from_below)


def gather_weight(value):
    blocks, rows, columns = value.shape
    count = lax.axis_size("z")
    here, side, core = (lax.axis_index("z"), lax.axis_index("y"), lax.axis_index("core"))
    mine = jnp.stack(ring_gather(value))
    both = jnp.stack([mine, swap(mine, "y")])
    rest = swap(both, "core")
    whole = jnp.zeros((blocks, count, 2, 2, rows, columns), value.dtype)
    for held, at_core in ((both, core), (rest, 1 - core)):
        for j, at_side in ((0, side), (1, 1 - side)):
            for k in range(count):
                whole = lax.dynamic_update_slice(
                    whole,
                    held[j, k][:, None, None, None],
                    (0, (here - k) % count, at_side, at_core, 0, 0),
                )
    return whole.reshape(blocks, count * 4 * rows, columns)


def scatter_weight(grad):
    count = lax.axis_size("z")
    here, side, core = (lax.axis_index("z"), lax.axis_index("y"), lax.axis_index("core"))
    blocks, height, columns = grad.shape
    rows = height // (count * 4)
    parts = grad.reshape(blocks, count, 2, 2, rows, columns)
    mine = lax.dynamic_index_in_dim(parts, core, 3, False)
    theirs = lax.dynamic_index_in_dim(parts, 1 - core, 3, False)
    chip = wide(mine) + wide(swap(low(theirs), "core"))
    mine = lax.dynamic_index_in_dim(chip, side, 2, False)
    theirs = lax.dynamic_index_in_dim(chip, 1 - side, 2, False)
    pair = low(mine + wide(swap(low(theirs), "y")))
    line = ring_scatter(
        [lax.dynamic_index_in_dim(pair, (here - k) % count, 1, False) for k in range(count)]
    )
    half = low(line)
    return wide(half) + wide(swap(half, "vocab"))


def gather_group(value):
    pair = jnp.stack([value, swap(value, "vocab")])
    return jnp.stack(ring_gather(pair))


def scatter_group(parts):
    held = parts[:, 0] + swap(low(parts[:, 1]), "vocab")
    return ring_scatter([held[k] for k in range(parts.shape[0])])


def butterfly(value, join, axes):
    for axis in axes:
        count = lax.axis_size(axis)
        step = 1
        while step < count:
            pairs = [(i, i ^ step) for i in range(count)]
            value = join(value, lax.ppermute(value, axis, pairs))
            step *= 2
    return value


def join_totals(left, right):
    peak = jnp.maximum(left[0], right[0])
    return jnp.stack(
        [peak, left[1] * jnp.exp(left[0] - peak) + right[1] * jnp.exp(right[0] - peak)]
    )


def turn(value):
    count = lax.axis_size("z")
    here, half = (lax.axis_index("z"), lax.axis_index("vocab"))
    value = jnp.where(half == 0, value, value[:, ::-1])
    backward = value[::-1]
    twice = jnp.concatenate([backward, backward])
    return lax.dynamic_slice_in_dim(twice, count - 1 - here, count, 0)


def heads_of(value):
    return value.reshape(value.shape[0], -1, HDIM)


def dot(left, right):
    return jnp.dot(left, right, preferred_element_type=jnp.float32)


def dot_left(left, right):
    return jnp.einsum("rd,re->de", left, right, preferred_element_type=jnp.float32)


def dot_right(left, right):
    return jnp.einsum("re,de->rd", left, right, preferred_element_type=jnp.float32)


def attend_fwd(a_query, a_memory, w, allowed):
    count, width = a_query.shape
    low_query = low(a_query)
    low_memory = low(a_memory)
    query = heads_of(low(dot(low_query, w[0])))
    keys = heads_of(low(dot(low_memory, w[1])))
    values = heads_of(low(dot(low_memory, w[2])))
    scores = jnp.einsum("qhd,khd->hqk", query, keys, preferred_element_type=jnp.float32) * HDIM ** (
        -0.5
    )
    scores = jnp.where(allowed[None], scores, NEGATIVE)
    expo = jnp.exp(scores - jnp.max(scores, axis=-1, keepdims=True))
    probs = expo / jnp.sum(expo, axis=-1, keepdims=True)
    low_probs = low(probs)
    mixed = low(
        jnp.einsum("hqk,khd->qhd", low_probs, values, preferred_element_type=jnp.float32)
    ).reshape(count, width)
    branch = dot(mixed, w[3])
    return (branch, (low_query, low_memory, query, keys, values, probs, low_probs, mixed))


def attend_bwd(grad_out, cache, w):
    low_query, low_memory, query, keys, values, probs, low_probs, mixed = cache
    count, width = mixed.shape
    scale = HDIM ** (-0.5)
    grad_low = low(grad_out)
    grad_wout = dot_left(mixed, grad_low)
    grad_mixed = heads_of(low(dot_right(grad_low, w[3])))
    grad_probs = jnp.einsum("qhd,khd->hqk", grad_mixed, values, preferred_element_type=jnp.float32)
    grad_scores = low(probs * (grad_probs - jnp.sum(probs * grad_probs, axis=-1, keepdims=True)))
    grad_query = low(
        jnp.einsum("hqk,khd->qhd", grad_scores, keys, preferred_element_type=jnp.float32) * scale
    ).reshape(count, width)
    grad_keys = low(
        jnp.einsum("hqk,qhd->khd", grad_scores, query, preferred_element_type=jnp.float32) * scale
    ).reshape(-1, width)
    grad_values = low(
        jnp.einsum("hqk,qhd->khd", low_probs, grad_mixed, preferred_element_type=jnp.float32)
    ).reshape(-1, width)
    grads = jnp.stack(
        [
            dot_left(low_query, grad_query),
            dot_left(low_memory, grad_keys),
            dot_left(low_memory, grad_values),
            grad_wout,
        ]
    )
    grad_aq = dot_right(grad_query, w[0])
    grad_am = dot_right(grad_keys, w[1]) + dot_right(grad_values, w[2])
    return (grad_aq, grad_am, grads)


def ffn_fwd(normed, w):
    low_normed = low(normed)
    hidden = [dot(low_normed, w[j]) for j in range(4)]
    active = [low(jax.nn.gelu(part)) for part in hidden]
    branch = sum(dot(active[j], w[4 + j]) for j in range(4))
    return (branch, (low_normed, hidden, active))


def ffn_bwd(grad_out, cache, w):
    low_normed, hidden, active = cache
    grad_low = low(grad_out)
    grad_down = [dot_left(part, grad_low) for part in active]
    grad_hidden = []
    for j in range(4):
        _, gelu_back = jax.vjp(jax.nn.gelu, hidden[j])
        grad_hidden.append(low(gelu_back(dot_right(grad_low, w[4 + j]))[0]))
    grad_up = [dot_left(low_normed, part) for part in grad_hidden]
    grad_normed = sum(dot_right(grad_hidden[j], w[j]) for j in range(4))
    return (grad_normed, jnp.stack(grad_up + grad_down))


def layer_fwd(stream, weights, depth, allowed, memory, cross_allowed):
    w_attn, w_ffn, gain = weights
    base = 3 * depth
    records = []
    normed, norm_back = jax.vjp(layer_norm, stream, gain[base])
    branch, cache = attend_fwd(normed, normed, w_attn[depth], allowed)
    records.append((norm_back, cache))
    stream = stream + branch
    if memory is not None:
        base = base + 1
        normed, norm_back = jax.vjp(layer_norm, stream, gain[base])
        branch, cache = attend_fwd(normed, memory, w_attn[2], cross_allowed)
        records.append((norm_back, cache))
        stream = stream + branch
    normed, norm_back = jax.vjp(layer_norm, stream, gain[base + 1])
    branch, cache = ffn_fwd(normed, w_ffn[depth])
    records.append((norm_back, cache))
    stream = stream + branch
    top, final_back = jax.vjp(layer_norm, stream, gain[base + 2])
    return (top, (records, final_back))


def layer_bwd(grad_top, kept, weights, depth):
    w_attn, w_ffn, gain = weights
    records, final_back = kept
    grad_stream, final_gain = final_back(grad_top)
    ffn_back, ffn_cache = records[-1]
    grad_normed, ffn_grads = ffn_bwd(grad_stream, ffn_cache, w_ffn[depth])
    extra, ffn_gain = ffn_back(grad_normed)
    grad_stream = grad_stream + extra
    gain_grads = [ffn_gain, final_gain]
    attn_grads = {}
    memory_grad = None
    for place in range(len(records) - 2, -1, -1):
        attn_back, attn_cache = records[place]
        index = depth if place == 0 else 2
        grad_aq, grad_am, attn_grads[index] = attend_bwd(grad_stream, attn_cache, w_attn[index])
        if place == 0:
            grad_aq = grad_aq + grad_am
        else:
            memory_grad = grad_am
        extra, attn_gain = attn_back(grad_aq)
        grad_stream = grad_stream + extra
        gain_grads.insert(0, attn_gain)
    return (grad_stream, memory_grad, gain_grads, attn_grads, ffn_grads)


def pack_attn(project, output):
    width = output.shape[1]
    return jnp.stack([project[:, j * width : (j + 1) * width] for j in range(3)] + [output])


def pack_ffn(expand, reduce):
    rows, width = (expand.shape[0], reduce.shape[1])
    up = expand.reshape(rows, width // rows, 4, rows).transpose(2, 0, 1, 3)
    return jnp.concatenate([up.reshape(4, rows, width), reduce.reshape(4, rows, width)])


def unpack_attn(pack):
    return (jnp.concatenate([pack[0], pack[1], pack[2]], axis=1), pack[3])


def unpack_ffn(pack):
    rows, width = pack.shape[1:]
    up = pack[:4].reshape(4, rows, width // rows, rows).transpose(1, 2, 0, 3)
    return (up.reshape(rows, 4 * width), pack[4:].reshape(4 * rows, width))


def shards(
    src_tokens,
    tgt_tokens,
    src_segments,
    tgt_lengths,
    mask_order,
    attn_project,
    attn_output,
    ffn_expand,
    ffn_reduce,
    norm_gains,
    length_table,
    embedding,
    momentum_attn_project,
    momentum_attn_output,
    momentum_ffn_expand,
    momentum_ffn_reduce,
    momentum_norm_gains,
    momentum_length_table,
    momentum_embedding,
    average_attn_project,
    average_attn_output,
    average_ffn_expand,
    average_ffn_reduce,
    average_norm_gains,
    average_length_table,
    average_embedding,
):
    masters = (
        attn_project,
        attn_output,
        ffn_expand,
        ffn_reduce,
        norm_gains,
        length_table,
        embedding,
    )
    moments = (
        momentum_attn_project,
        momentum_attn_output,
        momentum_ffn_expand,
        momentum_ffn_reduce,
        momentum_norm_gains,
        momentum_length_table,
        momentum_embedding,
    )
    averages = (
        average_attn_project,
        average_attn_output,
        average_ffn_expand,
        average_ffn_reduce,
        average_norm_gains,
        average_length_table,
        average_embedding,
    )
    count_z = lax.axis_size("z")
    here, side, core, half = (
        lax.axis_index("z"),
        lax.axis_index("y"),
        lax.axis_index("core"),
        lax.axis_index("vocab"),
    )
    rows_here = src_tokens.shape[0]
    count_dp = count_z * 4
    inverse = 1.0 / (SENTS * rows_here * count_dp)
    source, target, segments, lengths, order = (
        lax.dynamic_index_in_dim(array, half, 0, False)
        for array in (src_tokens, tgt_tokens, src_segments, tgt_lengths, mask_order)
    )
    shuffled = target[order]
    bounds = jnp.cumsum(lengths)
    tsegs = jnp.sum((order[:, None] >= bounds[None, :]).astype(jnp.int32), axis=1)
    src_allowed = segments[:, None] == segments[None, :]
    tgt_allowed = tsegs[:, None] == tsegs[None, :]
    cross_allowed = tsegs[:, None] == segments[None, :]
    position = sinusoid(ROW, D)
    dec_position = position[order]

    own_rows = low(embedding)
    shard = own_rows.shape[0]
    far_rows = swap(own_rows, "y")
    near = jnp.concatenate([own_rows, swap(own_rows, "core")])
    away = jnp.concatenate([far_rows, swap(far_rows, "core")])
    first = half * count_dp + here * 4
    ids = jnp.arange(shard, dtype=jnp.int32)
    block_ids = jnp.concatenate(
        [
            ids + (first + at_side * 2 + at_core) * shard
            for at_side in (side, 1 - side)
            for at_core in (core, 1 - core)
        ]
    )
    near_ids, away_ids = (block_ids[: 2 * shard], block_ids[2 * shard :])
    block_rows = jnp.concatenate([near, away])

    few = ROW - MASKED + 16
    extra = jnp.where(jnp.arange(16) == 0, MASK_TOKEN, -1).astype(jnp.int32)
    numbers = gather_group(jnp.concatenate([source, shuffled, extra]))
    numbers = numbers.reshape(count_z * 2, 2 * ROW + 16)
    src_ids = numbers[:, :ROW].reshape(-1)
    goal_ids = numbers[:, ROW : ROW + MASKED].reshape(-1)
    dec_ids = numbers[:, ROW + MASKED :].reshape(-1)

    def look_up(tokens):
        near_hot = low(tokens[:, None] == near_ids[None, :])
        away_hot = low(tokens[:, None] == away_ids[None, :])
        rows = low(dot(near_hot, near) + dot(away_hot, away))
        return scatter_group(rows.reshape(count_z, 2, -1, D))

    blanks = jnp.zeros((1, length_table.shape[1], D - LCLS - 7), jnp.bfloat16)
    misc = jnp.concatenate([low(length_table).T[None], low(norm_gains).T[None], blanks], axis=2)
    enc_pack = gather_weight(
        jnp.concatenate(
            [
                low(pack_attn(attn_project[0], attn_output[0])),
                misc,
                low(pack_ffn(ffn_expand[0], ffn_reduce[0])),
            ]
        )
    )
    dec_pack = gather_weight(
        jnp.concatenate(
            [
                low(pack_attn(attn_project[1], attn_output[1])),
                low(pack_attn(attn_project[2], attn_output[2])),
            ]
        )
    )
    dec_wide = gather_weight(low(pack_ffn(ffn_expand[1], ffn_reduce[1])))
    table = enc_pack[4, :, :LCLS].T
    gain = enc_pack[4, :, LCLS : LCLS + 7].T.astype(jnp.float32)
    weights = ((enc_pack[:4], dec_pack[:4], dec_pack[4:]), (enc_pack[5:], dec_wide), gain)
    scale_in = math.sqrt(D)
    class_ids = jnp.arange(LCLS, dtype=jnp.int32)
    sentence_ids = jnp.arange(SENTS, dtype=jnp.int32)

    src_emb = look_up(src_ids)
    dec_rows = look_up(dec_ids)
    dec_emb = jnp.concatenate(
        [
            jnp.broadcast_to(dec_rows[ROW - MASKED][None], (MASKED, D)),
            dec_rows[: ROW - MASKED],
        ]
    )
    enc_top, enc_kept = layer_fwd(
        scale_in * src_emb + position, weights, 0, src_allowed, None, None
    )
    dec_top, dec_kept = layer_fwd(
        scale_in * dec_emb + dec_position, weights, 1, tgt_allowed, enc_top, cross_allowed
    )

    tops = gather_group(low(dec_top[:MASKED])).reshape(-1, D)
    logits = dot_right(tops, block_rows)
    goal_hot = goal_ids[:, None] == block_ids[None, :]
    picked = jnp.sum(jnp.where(goal_hot, logits, 0.0))
    peak = jnp.max(logits, axis=1)
    total = jnp.sum(jnp.exp(logits - peak[:, None]), axis=1)
    totals = jnp.stack([turn(part.reshape(count_z, 2, MASKED)) for part in (peak, total)])
    totals = butterfly(totals, join_totals, ("vocab", "z"))
    log_total = turn(totals[0] + jnp.log(totals[1])).reshape(-1)
    grad_logits = low(
        (jnp.exp(logits - log_total[:, None]) - goal_hot.astype(jnp.float32)) * inverse
    )
    grad_rows = scatter_group(low(dot(grad_logits, block_rows)).reshape(count_z, 2, MASKED, D))
    grad_top = jnp.concatenate([grad_rows, jnp.zeros((ROW - MASKED, D), jnp.float32)])
    grad_block = dot_left(grad_logits, tops)

    member = (segments[None, :] == sentence_ids[:, None]).astype(jnp.float32)
    members = jnp.sum(member, axis=1, keepdims=True)
    pooled_low = low(jnp.dot(member, enc_top, precision=HIGHEST) / members)
    length_logits = jnp.einsum("sd,cd->sc", pooled_low, table, preferred_element_type=jnp.float32)
    length_total = jax.nn.logsumexp(length_logits, axis=1)
    class_hot = (lengths[:, None] - 1 == class_ids[None, :]).astype(jnp.float32)
    length_loss = length_total - jnp.sum(length_logits * class_hot, axis=1)
    loss_local = jnp.sum(log_total[:MASKED]) - picked + LENGTH_WEIGHT * jnp.sum(length_loss)
    grad_length = low(
        (jnp.exp(length_logits - length_total[:, None]) - class_hot) * (LENGTH_WEIGHT * inverse)
    )
    grad_table = jnp.einsum("sc,sd->dc", grad_length, pooled_low, preferred_element_type=jnp.float32)
    grad_pooled = jnp.einsum("sc,cd->sd", grad_length, table, preferred_element_type=jnp.float32)
    grad_enc = jnp.dot(member.T, grad_pooled / members, precision=HIGHEST)

    dec_stream, memory_grad, dec_gains, dec_attn, dec_ffn = layer_bwd(
        grad_top, dec_kept, weights, 1
    )
    sent = wide(low(scale_in * dec_stream))
    blank_sum = jnp.sum(sent[:MASKED], axis=0, keepdims=True)
    blank_high = low(blank_sum)
    blank_rest = low(blank_sum - wide(blank_high))
    sent = jnp.concatenate(
        [low(sent[MASKED:]), blank_high, blank_rest, jnp.zeros((14, D), jnp.bfloat16)]
    )
    again = jnp.where(jnp.arange(few) == ROW - MASKED + 1, MASK_TOKEN, 0).astype(jnp.int32)
    dec_sent = gather_group(sent).reshape(-1, D)
    back_ids = jnp.where(again[None] > 0, again[None], dec_ids.reshape(-1, few)).reshape(-1)
    dec_hot = low(back_ids[:, None] == block_ids[None, :])
    grad_block = grad_block + dot_left(dec_hot, dec_sent)
    enc_stream, _, enc_gains, enc_attn, enc_ffn = layer_bwd(
        grad_enc + memory_grad, enc_kept, weights, 0
    )
    src_sent = gather_group(low(scale_in * enc_stream)).reshape(-1, D)
    src_hot = low(src_ids[:, None] == block_ids[None, :])
    grad_block = grad_block + dot_left(src_hot, src_sent)
    blocks = grad_block.reshape(2, 2, shard, D)
    chip = blocks[:, 0] + wide(swap(low(blocks[:, 1]), "core"))
    grad_embed = chip[0] + wide(swap(low(chip[1]), "y"))

    grad_gain = jnp.stack(enc_gains + dec_gains).T
    grad_misc = jnp.concatenate(
        [grad_table, grad_gain, jnp.zeros((D, D - LCLS - 7), jnp.float32)], axis=1
    )
    sum_dec_ffn = scatter_weight(dec_ffn)
    sum_dec_attn = scatter_weight(jnp.concatenate([dec_attn[1], dec_attn[2]]))
    sum_enc_ffn = scatter_weight(enc_ffn)
    sum_enc_attn = scatter_weight(jnp.concatenate([enc_attn[0], grad_misc[None]]))
    attn = [unpack_attn(part) for part in (sum_enc_attn[:4], sum_dec_attn[:4], sum_dec_attn[4:])]
    ffn = [unpack_ffn(part) for part in (sum_enc_ffn, sum_dec_ffn)]
    reduced = (
        jnp.stack([part[0] for part in attn]),
        jnp.stack([part[1] for part in attn]),
        jnp.stack([part[0] for part in ffn]),
        jnp.stack([part[1] for part in ffn]),
        sum_enc_attn[4, :, LCLS : LCLS + 7].T,
        sum_enc_attn[4, :, :LCLS].T,
        grad_embed,
    )
    layer_squares = jnp.zeros((), jnp.float32)
    for grad in reduced[:6]:
        layer_squares = layer_squares + jnp.sum(grad * grad)
    table_squares = jnp.sum(reduced[6] * reduced[6])
    vocab_count = lax.axis_size("vocab")
    totals = butterfly(
        jnp.stack([layer_squares / vocab_count + table_squares, loss_local]),
        jnp.add,
        ("core", "vocab", "y", "z"),
    )
    squares, loss_sum = (totals[0], totals[1])
    grad_norm = jnp.sqrt(squares)
    factor = jnp.minimum(1.0, CLIP / grad_norm)
    rate = RATE_SCALE * math.sqrt(NPARAM / D) / CLIP
    fresh, moved, smooth, copies = ([], [], [], [])
    for weight, grad, moment, average, boost in zip(
        masters, reduced, moments, averages, RATE_FACTORS
    ):
        clipped = grad * factor
        moment = MOMENTUM * moment + clipped
        weight = weight - boost * rate * (clipped + MOMENTUM * moment)
        average = KEEP * average + (1.0 - KEEP) * weight
        fresh.append(weight)
        moved.append(moment)
        smooth.append(average)
        copies.append(weight.astype(jnp.bfloat16))
    return (loss_sum, grad_norm) + tuple(fresh) + tuple(moved) + tuple(smooth) + tuple(copies)


def solution(mesh):
    vocab = mesh.shape["vocab"]
    grid = Mesh(mesh.devices.reshape(-1, 2, 2, vocab), ("z", "y", "core", "vocab"))
    dp = ("z", "y", "core")
    return jax.shard_map(
        shards,
        mesh=grid,
        in_specs=(
            P(dp, None),
            P(dp, None),
            P(dp, None),
            P(dp, None),
            P(dp, None),
            P(None, dp, None),
            P(None, dp, None),
            P(None, dp, None),
            P(None, dp, None),
            P(None, dp),
            P(None, dp),
            P(("vocab",) + dp, None),
            P(None, dp, None),
            P(None, dp, None),
            P(None, dp, None),
            P(None, dp, None),
            P(None, dp),
            P(None, dp),
            P(("vocab",) + dp, None),
            P(None, dp, None),
            P(None, dp, None),
            P(None, dp, None),
            P(None, dp, None),
            P(None, dp),
            P(None, dp),
            P(("vocab",) + dp, None),
        ),
        out_specs=(
            P(),
            P(),
            P(None, dp, None),
            P(None, dp, None),
            P(None, dp, None),
            P(None, dp, None),
            P(None, dp),
            P(None, dp),
            P(("vocab",) + dp, None),
            P(None, dp, None),
            P(None, dp, None),
            P(None, dp, None),
            P(None, dp, None),
            P(None, dp),
            P(None, dp),
            P(("vocab",) + dp, None),
            P(None, dp, None),
            P(None, dp, None),
            P(None, dp, None),
            P(None, dp, None),
            P(None, dp),
            P(None, dp),
            P(("vocab",) + dp, None),
            P(None, dp, None),
            P(None, dp, None),
            P(None, dp, None),
            P(None, dp, None),
            P(None, dp),
            P(None, dp),
            P(("vocab",) + dp, None),
        ),
        check_vma=False,
    )
```

time: 1550 us -> 854 us (0.55)
  waiting for transfers between devices: 923 us -> 247 us
  matrix products: 353 us -> 159 us
  starting transfers between devices: 0.97 us -> 141 us
  local copies, waits for them, and re-layouts: 67.8 us -> 164 us
  blocking collectives: 87.4 us -> 0 us
  other arithmetic: 87.7 us -> 118 us
    reduce_scatter x6 -> x0, waiting for transfers between devices: 635 us -> none  [the longest x1 326 us: shards(): lax.psum_scatter(gathered[6], 'dp', scatter_dimension=0, tiled=True)]
    all_gather x5 -> x0, waiting for transfers between devices: 251 us -> none  [the longest x1 127 us: shards(): lax.all_gather(embedding.astype(jnp.bfloat16), 'dp', axis=0, tiled=True)]
    ppermute x0 -> x94, waiting for transfers between devices: none -> 247 us  [the longest x56 138 us: shift(): lax.ppermute(value, 'z', [(i, (i + by) % count) for i in range(count)])]
    dot_general x96 -> x95, matrix products: 295 us -> 128 us  [the longest x33 53.1 us: dot(): return jnp.dot(left, right, preferred_element_type=jnp.float32)]
    ppermute x0 -> x94, starting transfers between devices: none -> 141 us  [the longest x56 111 us: shift(): lax.ppermute(value, 'z', [(i, (i + by) % count) for i in range(count)])]
    psum x2 -> x0, blocking collectives: 44.7 us -> none  [the longest x1 39.2 us: shards(): lax.psum((layer_squares / vocab_count + table_squares, loss_local / vocab...]
    all_gather x2 -> x0, blocking collectives: 37.2 us -> none  [the longest x1 18.8 us: shards(): lax.all_gather(norm_gains.astype(jnp.bfloat16), 'dp', axis=1, tiled=True)]
    psum x2 -> x0, waiting for transfers between devices: 36 us -> none  [the longest x1 19 us: shards(): lax.psum(jnp.einsum('mv,vd->md', grad_logits, embed, preferred_element_ty...]
  transfers between devices with their start and end apart: 14 -> 94, of which waited for: 10 -> 45; matrix products, arithmetic and copies ran while one was open for 17% -> 28% of each run, Pallas kernels for 0% -> 0%
where the time goes in v1:
time: 854 us; the launch traced here: 844 us
  waiting for transfers between devices  247 us (29%)
  local copies, waits for them, and re-layouts  164 us (19%)
  matrix products  159 us (19%)
  starting transfers between devices  141 us (17%)
  other arithmetic  118 us (14%)
  between operations  15.2 us (2%)
    ppermute x56, waiting for transfers between devices, shift(): lax.ppermute(value, 'z', [(i, (i + by) % count) for i in range(count)])  138 us
    ppermute x56, starting transfers between devices, shift(): lax.ppermute(value, 'z', [(i, (i + by) % count) for i in range(count)])  111 us
    ppermute x30, waiting for transfers between devices, swap(): return lax.ppermute(value, axis, SWAP)  91.1 us
    dot_general x33, matrix products, dot(): return jnp.dot(left, right, preferred_element_type=jnp.float32)  53.1 us
    dot_general x31, matrix products, dot_left(): jnp.einsum('rd,re->de', left, right, preferred_element_type=jnp.float32)  49.1 us
    unnamed x604, local copies, waits for them, and re-layouts  47.8 us
    convert_element_type x23, local copies, waits for them, and re-layouts, low(): return value.astype(jnp.bfloat16)  27.5 us
    dot_general x29, matrix products, dot_right(): jnp.einsum('re,de->rd', left, right, preferred_element_type=jnp.float32)  24.3 us
  transfers between devices with their start and end apart: 94, of which 45 were waited for; matrix products, arithmetic and copies ran while one was open for 28% of the time, Pallas kernels for 0%

profile of v1, /device:TPU:0, one launch (start us, length us, event | category | flops | bytes accessed | tf_op | source)
XLA Modules:
  0.0 844.5 jit_solution(12732006529834259350)
XLA Ops:
  45.9 3.9 collective-permute-start.4
  57.4 7.0 collective-permute-done.32
  70.1 4.7 collective-permute-done.31
  76.6 12.2 %collective-permute-done.33 = bf16[4,32,512]{2,1,0:T(8,128)(2,1)S(1)} collective-permute-done((bf16[4,32,512]{2,1,0:T(8,128)(2,1)S(1)}, bf16[4,32,512]{2,1,0:T(8,128)(2,1)S(1)}, u32[]{:S(2)}, u32[]{:S(2)}) %collective-permute-start.33) | collective-permute-done | bytes 131104 | tf_op jit(solution)/shard_map/ppermute | solution.py:52
  100.5 7.2 collective-permute-done.14
  112.2 3.6 collective-permute-done.6
  117.1 4.5 fusion.21
  121.6 7.4 fusion.11
  128.9 9.2 %collective-permute-done.28 = bf16[4,8,32,512]{3,2,1,0:T(8,128)(2,1)S(1)} collective-permute-done((bf16[4,8,32,512]{3,2,1,0:T(8,128)(2,1)S(1)}, bf16[4,8,32,512]{3,2,1,0:T(8,128)(2,1)S(1)}, u32[]{:S(2)}, u32[]{:S(2)}) %collective-permute-start.28) | collective-permute-done | bytes 1048608 | tf_op jit(solution)/shard_map/ppermute | solution.py:47
  139.8 20.9 %collective-permute-done.34 = bf16[4,8,32,512]{3,2,1,0:T(8,128)(2,1)S(1)} collective-permute-done((bf16[4,8,32,512]{3,2,1,0:T(8,128)(2,1)}, bf16[4,8,32,512]{3,2,1,0:T(8,128)(2,1)S(1)}, u32[]{:S(2)}, u32[]{:S(2)}) %collective-permute-start.34) | collective-permute-done | bytes 1048608 | tf_op jit(solution)/shard_map/ppermute | solution.py:47
  162.5 7.9 add_convert_fusion
  171.1 3.5 fusion.40
  176.3 12.5 %collective-permute-done.17 = bf16[4,13,32,512]{3,2,1,0:T(8,128)(2,1)S(1)} collective-permute-done((bf16[4,13,32,512]{3,2,1,0:T(8,128)(2,1)S(1)}, bf16[4,13,32,512]{3,2,1,0:T(8,128)(2,1)S(1)}, u32[]{:S(2)}, u32[]{:S(2)}) %collective-permute-start.17) | collective-permute-done | bytes 1703968 | tf_op jit(solution)/shard_map/ppermute | solution.py:47
  188.9 5.6 collective-permute-done.19
  194.7 15.5 %collective-permute-start.20 = (bf16[88,512]{1,0:T(8,128)(2,1)S(1)}, bf16[88,512]{1,0:T(8,128)(2,1)S(1)}, u32[]{:S(2)}, u32[]{:S(2)}) collective-permute-start(bf16[88,512]{1,0:T(8,128)(2,1)S(1)} %get-tuple-element.344), channel_id=1, source_target_pairs={{0,24},{8,0},{16,8},{24,16},{1,25},{9,1},{17,9},{25,17},{2,26},{10... | collective-permute-start | bytes 270344 | tf_op jit(solution)/shard_map/ppermute | solution.py:52
  212.3 4.4 collective-permute-done.22
  216.9 3.8 collective-permute-start.9
  229.2 11.9 %collective-permute-start.12 = (bf16[256,512]{1,0:T(8,128)(2,1)S(1)}, bf16[256,512]{1,0:T(8,128)(2,1)S(1)}, u32[]{:S(2)}, u32[]{:S(2)}) collective-permute-start(bf16[256,512]{1,0:T(8,128)(2,1)S(1)} %pad_maximum_fusion.21), channel_id=1, source_target_pairs={{0,8},{8,16},{16,24},{24,0},{1,9},{9,17},{17,25},{25,1},{2,10},{10... | collective-permute-start | bytes 786440 | tf_op jit(solution)/shard_map/ppermute | solution.py:52
  243.8 5.5 collective-permute-done.12
  267.0 4.2 fusion.350
  319.9 3.2 fusion.358
  328.5 3.2 fusion.363
  339.3 4.1 collective-permute-done.36
  343.5 3.8 collective-permute-start.39
  347.7 5.2 collective-permute-done.37
  353.0 4.3 collective-permute-start.40
  359.7 9.6 %fusion.366 = (f32[768]{0:T(1024)S(1)}, f32[768,4000]{0,1:T(8,128)}) fusion(bf16[768,512]{1,0:T(8,128)(2,1)S(1)} %bitcast.1343, bf16[1000,512]{1,0:T(8,128)(2,1)S(1)} %copy-done.176, bf16[1000,512]{1,0:T(8,128)(2,1)} %collective-permute-done.6, bf16[1000,512]{1,0:T(8,128)(2,1)} %collective-permute-done.5, bf16[1000,512]{1,0:T(8,128)(2,1)S(1)} %copy-done.174), kind=kOutput, calls=%fused_computation.882 | convolution fusion | flops 3165183232 | bytes 17173504 | tf_op jit(solution)/shard_map/re,de->rd/dot_general | solution.py:184
  369.5 8.6 %fusion.16 = (f32[]{:T(128)}, f32[768]{0:T(1024)S(1)}) fusion(f32[768,4000]{0,1:T(8,128)} %get-tuple-element.415, s32[768]{0:T(1024)} %eq.286, s32[4000]{0:T(1024)S(1)} %concatenate.202, f32[768]{0:T(1024)S(1)} %get-tuple-element.414), kind=kLoop, calls=%fused_computation.20 | loop fusion | flops 15359231 | bytes 12313220 | tf_op jit(solution)/shard_map/reduce_sum | solution.py:482
  379.0 3.1 collective-permute-done.41
  394.6 10.9 %convolution_convert_fusion = bf16[768,512]{1,0:T(8,128)(2,1)S(1)} fusion(bf16[1000,512]{1,0:T(8,128)(2,1)} %copy-done.175, bf16[1000,512]{1,0:T(8,128)(2,1)} %collective-permute-done.6, bf16[1000,512]{1,0:T(8,128)(2,1)} %collective-permute-done.5, bf16[1000,512]{1,0:T(8,128)(2,1)} %convert_element_type.756, f32[768,4000]{0,1:T(8,128)} %get-tuple-element.415, ...), kind=kOutput, calls=%fused_computation.96 | convolution fusion | flops 3180937216 | bytes 17192576 | tf_op jit(solution)/shard_map/dot_general | solution.py:176
  409.0 4.4 collective-permute-done.44
  415.6 9.0 %fusion.324 = f32[4000,512]{1,0:T(8,128)} fusion(bf16[768,512]{1,0:T(8,128)(2,1)S(1)} %bitcast.1344, f32[768,4000]{0,1:T(8,128)} %get-tuple-element.415, s32[768]{0:T(1024)} %eq.286, f32[768]{0:T(1024)} %copy-done.278, s32[4000]{0:T(1024)} %copy-done.205), kind=kOutput, calls=%fused_computation.847 | convolution fusion | flops 3164160000 | bytes 21288576 | tf_op jit(solution)/shard_map/rd,re->de/dot_general | solution.py:180
  425.3 3.2 collective-permute-start.46
  432.0 4.1 collective-permute-done.48
  500.3 3.3 copy-done.26
  525.3 3.8 fusion.43
  530.2 3.8 collective-permute-start.80
  535.9 3.8 collective-permute-start.85
  539.7 3.5 collective-permute-done.78
  543.3 5.9 collective-permute-done.80
  553.0 24.4 %collective-permute-done.79 = bf16[1,176,512]{2,1,0:T(8,128)(2,1)S(1)} collective-permute-done((bf16[1,176,512]{2,1,0:T(8,128)(2,1)S(1)}, bf16[1,176,512]{2,1,0:T(8,128)(2,1)S(1)}, u32[]{:S(2)}, u32[]{:S(2)}) %collective-permute-start.79) | collective-permute-done | bytes 180256 | tf_op jit(solution)/shard_map/ppermute | solution.py:52
  579.4 3.9 collective-permute-start.86
  583.2 9.2 %fusion.5 = f32[4000,512]{1,0:T(8,128)} fusion(bf16[1408,512]{1,0:T(8,128)(2,1)S(1)} %bitcast.1311, s32[4000]{0:T(1024)S(1)} %copy-done.206, s32[1408]{0:T(1024)S(1)} %copy-done.274), kind=kOutput, calls=%fused_computation.7 | convolution fusion | flops 5772800000 | bytes 9655424 | tf_op jit(solution)/shard_map/rd,re->de/dot_general | solution.py:180
  597.4 14.4 %add_add_fusion = f32[4000,512]{1,0:T(8,128)S(1)} fusion(f32[4000,512]{1,0:T(8,128)} %fusion.324, f32[4000,512]{1,0:T(8,128)} %fusion.5, bf16[2048,512]{1,0:T(8,128)(2,1)S(1)} %bitcast.1293, s32[4000]{0:T(1024)S(1)} %copy-done.206, s32[2048]{0:T(1024)S(1)} %bitcast.1397), kind=kOutput, calls=%fused_computation.32 | convolution fusion | flops 8400896000 | bytes 26697344 | tf_op jit(solution)/shard_map/rd,re->de/dot_general | solution.py:180
  615.7 3.7 copy.607
  622.0 4.0 fusion.33
  629.6 6.2 collective-permute-done.51
  638.9 9.6 %collective-permute-done.53 = bf16[3,32,512]{1,2,0:T(8,128)(2,1)S(1)} collective-permute-done((bf16[3,32,512]{1,2,0:T(8,128)(2,1)}, bf16[3,32,512]{1,2,0:T(8,128)(2,1)S(1)}, u32[]{:S(2)}, u32[]{:S(2)}) %collective-permute-start.53) | collective-permute-done | bytes 98336 | tf_op jit(solution)/shard_map/ppermute | solution.py:52
  651.9 3.6 bitcast_add_fusion.1
  658.3 3.6 bitcast_add_fusion.2
  672.1 3.6 bitcast_add_fusion.3
  682.2 3.6 fusion.34
  693.5 13.2 %collective-permute-done.64 = bf16[8,4,32,512]{3,2,1,0:T(8,128)(2,1)} collective-permute-done((bf16[8,4,32,512]{3,2,1,0:T(8,128)(2,1)}, bf16[8,4,32,512]{3,2,1,0:T(8,128)(2,1)}, u32[]{:S(2)}, u32[]{:S(2)}) %collective-permute-start.64) | collective-permute-done | bytes 1048608 | tf_op jit(solution)/shard_map/ppermute | solution.py:47
  711.5 17.7 %collective-permute-done.57 = bf16[8,4,32,512]{3,2,1,0:T(8,128)(2,1)} collective-permute-done((bf16[8,4,32,512]{3,2,1,0:T(8,128)(2,1)}, bf16[8,4,32,512]{3,2,1,0:T(8,128)(2,1)}, u32[]{:S(2)}, u32[]{:S(2)}) %collective-permute-start.57) | collective-permute-done | bytes 1048608 | tf_op jit(solution)/shard_map/ppermute | solution.py:47
  731.0 3.9 collective-permute-start.58
  735.0 3.9 collective-permute-start.73
  739.1 4.0 collective-permute-start.66
  744.2 4.8 collective-permute-done.73
  755.7 4.1 collective-permute-done.66
  760.3 5.6 collective-permute-done.68
  767.9 4.9 collective-permute-done.61
  793.8 3.0 multiply_reduce_fusion.3
  802.9 3.0 collective-permute-done.91
  833.0 4.0 fusion.327
  (1242 shorter events, 411.5 us)
Async XLA Ops:
  9.6 58.5 %collective-permute-start.24 = (bf16[8,32,512]{2,1,0:T(8,128)(2,1)}, bf16[8,32,512]{2,1,0:T(8,128)(2,1)}, u32[]{:S(2)}, u32[]{:S(2)}) collective-permute-start(bf16[8,32,512]{2,1,0:T(8,128)(2,1)} %get-tuple-element.381), channel_id=1, source_target_pairs={{0,8},{8,16},{16,24},{24,0},{1,9},{9,17},{17,25},{25,1},{2,10},{10... | collective-permute-start | bytes 786440 | tf_op jit(solution)/shard_map/ppermute | solution.py:52
  12.6 56.4 %collective-permute-start.26 = (bf16[8,32,512]{2,1,0:T(8,128)(2,1)}, bf16[8,32,512]{2,1,0:T(8,128)(2,1)}, u32[]{:S(2)}, u32[]{:S(2)}) collective-permute-start(bf16[8,32,512]{2,1,0:T(8,128)(2,1)} %get-tuple-element.381), channel_id=1, source_target_pairs={{0,24},{8,0},{16,8},{24,16},{1,25},{9,1},{17,9},{25,17},{2,26},{10... | collective-permute-start | bytes 786440 | tf_op jit(solution)/shard_map/ppermute | solution.py:52
  18.6 21.1 %collective-permute-start = (s32[528]{0:T(1024)S(1)}, s32[528]{0:T(1024)}, u32[]{:S(2)}, u32[]{:S(2)}) collective-permute-start(s32[528]{0:T(1024)S(1)} %pad_add_fusion.4), channel_id=1, source_target_pairs={{0,1},{1,0},{2,3},{3,2},{4,5},{5,4},{6,7},{7,6},{8,9},{9,8},{10,11... | collective-permute-start | bytes 6344 | tf_op jit(solution)/shard_map/ppermute | solution.py:47
  25.6 29.7 %collective-permute-start.30 = (bf16[8,32,512]{2,1,0:T(8,128)(2,1)}, bf16[8,32,512]{2,1,0:T(8,128)(2,1)S(1)}, u32[]{:S(2)}, u32[]{:S(2)}) collective-permute-start(bf16[8,32,512]{2,1,0:T(8,128)(2,1)} %pad_maximum_fusion.22), channel_id=1, source_target_pairs={{0,8},{8,16},{16,24},{24,0},{1,9},{9,17},{17,25},{25,1},{2,10},{10... | collective-permute-start | bytes 786440 | tf_op jit(solution)/shard_map/ppermute | solution.py:52
  55.2 42.8 %collective-permute-start.15 = (bf16[13,32,512]{2,1,0:T(8,128)(2,1)}, bf16[13,32,512]{2,1,0:T(8,128)(2,1)S(1)}, u32[]{:S(2)}, u32[]{:S(2)}) collective-permute-start(bf16[13,32,512]{2,1,0:T(8,128)(2,1)} %constant_dynamic-update-slice_fusion.2), channel_id=1, source_target_pairs={{0,24},{8,0},{16,8},{24,16},{1,25},{9,1},{17,9},{25,17},{2,26},{10... | collective-permute-start | bytes 1277960 | tf_op jit(solution)/shard_map/ppermute | solution.py:52
  55.4 19.3 %collective-permute-start.31 = (bf16[4,32,512]{2,1,0:T(8,128)(2,1)S(1)}, bf16[4,32,512]{2,1,0:T(8,128)(2,1)S(1)}, u32[]{:S(2)}, u32[]{:S(2)}) collective-permute-start(bf16[4,32,512]{2,1,0:T(8,128)(2,1)S(1)} %slice.1177), channel_id=1, source_target_pairs={{0,8},{8,16},{16,24},{24,0},{1,9},{9,17},{17,25},{25,1},{2,10},{10... | collective-permute-start | bytes 393224 | tf_op jit(solution)/shard_map/ppermute | solution.py:52
  64.4 24.4 %collective-permute-start.33 = (bf16[4,32,512]{2,1,0:T(8,128)(2,1)S(1)}, bf16[4,32,512]{2,1,0:T(8,128)(2,1)S(1)}, u32[]{:S(2)}, u32[]{:S(2)}) collective-permute-start(bf16[4,32,512]{2,1,0:T(8,128)(2,1)S(1)} %slice.1178), channel_id=1, source_target_pairs={{0,24},{8,0},{16,8},{24,16},{1,25},{9,1},{17,9},{25,17},{2,26},{10... | collective-permute-start | bytes 393224 | tf_op jit(solution)/shard_map/ppermute | solution.py:52
  68.1 31.7 %collective-permute-start.13 = (bf16[13,32,512]{2,1,0:T(8,128)(2,1)}, bf16[13,32,512]{2,1,0:T(8,128)(2,1)S(1)}, u32[]{:S(2)}, u32[]{:S(2)}) collective-permute-start(bf16[13,32,512]{2,1,0:T(8,128)(2,1)} %constant_dynamic-update-slice_fusion.2), channel_id=1, source_target_pairs={{0,8},{8,16},{16,24},{24,0},{1,9},{9,17},{17,25},{25,1},{2,10},{10... | collective-permute-start | bytes 1277960 | tf_op jit(solution)/shard_map/ppermute | solution.py:52
  69.1 48.0 %collective-permute-start.5 = (bf16[1000,512]{1,0:T(8,128)(2,1)}, bf16[1000,512]{1,0:T(8,128)(2,1)}, u32[]{:S(2)}, u32[]{:S(2)}) collective-permute-start(bf16[1000,512]{1,0:T(8,128)(2,1)} %convert_element_type.756), channel_id=1, source_target_pairs={{0,2},{2,0},{1,3},{3,1},{4,6},{6,4},{5,7},{7,5},{8,10},{10,8},{9,1... | collective-permute-start | bytes 3072008 | tf_op jit(solution)/shard_map/ppermute | solution.py:47
  74.7 15.4 %collective-permute-start.25 = (bf16[4,32,512]{2,1,0:T(8,128)(2,1)S(1)}, bf16[4,32,512]{2,1,0:T(8,128)(2,1)S(1)}, u32[]{:S(2)}, u32[]{:S(2)}) collective-permute-start(bf16[4,32,512]{2,1,0:T(8,128)(2,1)S(1)} %slice.1149), channel_id=1, source_target_pairs={{0,8},{8,16},{16,24},{24,0},{1,9},{9,17},{17,25},{25,1},{2,10},{10... | collective-permute-start | bytes 393224 | tf_op jit(solution)/shard_map/ppermute | solution.py:52
  90.1 25.7 %collective-permute-start.6 = (bf16[1000,512]{1,0:T(8,128)(2,1)S(1)}, bf16[1000,512]{1,0:T(8,128)(2,1)}, u32[]{:S(2)}, u32[]{:S(2)}) collective-permute-start(bf16[1000,512]{1,0:T(8,128)(2,1)S(1)} %copy-done.173), channel_id=1, source_target_pairs={{0,4},{4,0},{1,5},{5,1},{2,6},{6,2},{3,7},{7,3},{8,12},{12,8},{9,1... | collective-permute-start | bytes 3072008 | tf_op jit(solution)/shard_map/ppermute | solution.py:47
  95.1 43.0 %collective-permute-start.28 = (bf16[4,8,32,512]{3,2,1,0:T(8,128)(2,1)S(1)}, bf16[4,8,32,512]{3,2,1,0:T(8,128)(2,1)S(1)}, u32[]{:S(2)}, u32[]{:S(2)}) collective-permute-start(bf16[4,8,32,512]{3,2,1,0:T(8,128)(2,1)S(1)} %get-tuple-element.340), channel_id=1, source_target_pairs={{0,4},{4,0},{1,5},{5,1},{2,6},{6,2},{3,7},{7,3},{8,12},{12,8},{9,1... | collective-permute-start | bytes 3145736 | tf_op jit(solution)/shard_map/ppermute | solution.py:47
  98.0 10.2 %collective-permute-start.16 = (bf16[7,32,512]{2,1,0:T(8,128)(2,1)S(1)}, bf16[7,32,512]{2,1,0:T(8,128)(2,1)S(1)}, u32[]{:S(2)}, u32[]{:S(2)}) collective-permute-start(bf16[7,32,512]{2,1,0:T(8,128)(2,1)S(1)} %slice.1094), channel_id=1, source_target_pairs={{0,24},{8,0},{16,8},{24,16},{1,25},{9,1},{17,9},{25,17},{2,26},{10... | collective-permute-start | bytes 688136 | tf_op jit(solution)/shard_map/ppermute | solution.py:52
  107.7 53.0 %collective-permute-start.34 = (bf16[4,8,32,512]{3,2,1,0:T(8,128)(2,1)}, bf16[4,8,32,512]{3,2,1,0:T(8,128)(2,1)S(1)}, u32[]{:S(2)}, u32[]{:S(2)}) collective-permute-start(bf16[4,8,32,512]{3,2,1,0:T(8,128)(2,1)} %pad_maximum_fusion.11), channel_id=1, source_target_pairs={{0,4},{4,0},{1,5},{5,1},{2,6},{6,2},{3,7},{7,3},{8,12},{12,8},{9,1... | collective-permute-start | bytes 3145736 | tf_op jit(solution)/shard_map/ppermute | solution.py:47
  109.5 79.3 %collective-permute-start.17 = (bf16[4,13,32,512]{3,2,1,0:T(8,128)(2,1)S(1)}, bf16[4,13,32,512]{3,2,1,0:T(8,128)(2,1)S(1)}, u32[]{:S(2)}, u32[]{:S(2)}) collective-permute-start(bf16[4,13,32,512]{3,2,1,0:T(8,128)(2,1)S(1)} %get-tuple-element.312), channel_id=1, source_target_pairs={{0,4},{4,0},{1,5},{5,1},{2,6},{6,2},{3,7},{7,3},{8,12},{12,8},{9,1... | collective-permute-start | bytes 5111816 | tf_op jit(solution)/shard_map/ppermute | solution.py:47
  115.8 46.6 %collective-permute-start.7 = (bf16[1000,512]{1,0:T(8,128)(2,1)}, bf16[1000,512]{1,0:T(8,128)(2,1)S(1)}, u32[]{:S(2)}, u32[]{:S(2)}) collective-permute-start(bf16[1000,512]{1,0:T(8,128)(2,1)} %collective-permute-done.6), channel_id=1, source_target_pairs={{0,2},{2,0},{1,3},{3,1},{4,6},{6,4},{5,7},{7,5},{8,10},{10,8},{9,1... | collective-permute-start | bytes 3072008 | tf_op jit(solution)/shard_map/ppermute | solution.py:47
  139.6 113.6 %collective-permute-start.29 = (bf16[2,4,8,32,512]{4,3,2,1,0:T(8,128)(2,1)}, bf16[2,4,8,32,512]{4,3,2,1,0:T(8,128)(2,1)S(1)}, u32[]{:S(2)}, u32[]{:S(2)}) collective-permute-start(bf16[2,4,8,32,512]{4,3,2,1,0:T(8,128)(2,1)} %pad_maximum_fusion.2), channel_id=1, source_target_pairs={{0,2},{2,0},{1,3},{3,1},{4,6},{6,4},{5,7},{7,5},{8,10},{10,8},{9,1... | collective-permute-start | bytes 6291464 | tf_op jit(solution)/shard_map/ppermute | solution.py:47
  170.5 46.2 %collective-permute-start.8 = (bf16[4,256,512]{2,1,0:T(8,128)(2,1)S(1)}, bf16[4,256,512]{2,1,0:T(8,128)(2,1)S(1)}, u32[]{:S(2)}, u32[]{:S(2)}) collective-permute-start(bf16[4,256,512]{2,1,0:T(8,128)(2,1)S(1)} %slice_bitcast_fusion.1), channel_id=1, source_target_pairs={{0,1},{1,0},{2,3},{3,2},{4,5},{5,4},{6,7},{7,6},{8,9},{9,8},{10,11... | collective-permute-start | bytes 3145736 | tf_op jit(solution)/shard_map/ppermute | solution.py:47
  174.7 19.8 %collective-permute-start.19 = (bf16[4,176,512]{2,1,0:T(8,128)(2,1)S(1)}, bf16[4,176,512]{2,1,0:T(8,128)(2,1)S(1)}, u32[]{:S(2)}, u32[]{:S(2)}) collective-permute-start(bf16[4,176,512]{2,1,0:T(8,128)(2,1)S(1)} %slice_bitcast_fusion.3), channel_id=1, source_target_pairs={{0,1},{1,0},{2,3},{3,2},{4,5},{5,4},{6,7},{7,6},{8,9},{9,8},{10,11... | collective-permute-start | bytes 2162696 | tf_op jit(solution)/shard_map/ppermute | solution.py:47
  194.7 17.6 %collective-permute-start.20 = (bf16[88,512]{1,0:T(8,128)(2,1)S(1)}, bf16[88,512]{1,0:T(8,128)(2,1)S(1)}, u32[]{:S(2)}, u32[]{:S(2)}) collective-permute-start(bf16[88,512]{1,0:T(8,128)(2,1)S(1)} %get-tuple-element.344), channel_id=1, source_target_pairs={{0,24},{8,0},{16,8},{24,16},{1,25},{9,1},{17,9},{25,17},{2,26},{10... | collective-permute-start | bytes 270344 | tf_op jit(solution)/shard_map/ppermute | solution.py:52
  216.9 9.8 %collective-permute-start.9 = (bf16[128,512]{1,0:T(8,128)(2,1)S(1)}, bf16[128,512]{1,0:T(8,128)(2,1)S(1)}, u32[]{:S(2)}, u32[]{:S(2)}) collective-permute-start(bf16[128,512]{1,0:T(8,128)(2,1)S(1)} %get-tuple-element.336), channel_id=1, source_target_pairs={{0,24},{8,0},{16,8},{24,16},{1,25},{9,1},{17,9},{25,17},{2,26},{10... | collective-permute-start | bytes 393224 | tf_op jit(solution)/shard_map/ppermute | solution.py:52
  220.8 22.4 %collective-permute-start.21 = (bf16[176,512]{1,0:T(8,128)(2,1)S(1)}, bf16[176,512]{1,0:T(8,128)(2,1)S(1)}, u32[]{:S(2)}, u32[]{:S(2)}) collective-permute-start(bf16[176,512]{1,0:T(8,128)(2,1)S(1)} %pad_maximum_fusion.31), channel_id=1, source_target_pairs={{0,24},{8,0},{16,8},{24,16},{1,25},{9,1},{17,9},{25,17},{2,26},{10... | collective-permute-start | bytes 540680 | tf_op jit(solution)/shard_map/ppermute | solution.py:52
  220.9 22.3 %collective-permute-start.23 = (bf16[176,512]{1,0:T(8,128)(2,1)S(1)}, bf16[176,512]{1,0:T(8,128)(2,1)S(1)}, u32[]{:S(2)}, u32[]{:S(2)}) collective-permute-start(bf16[176,512]{1,0:T(8,128)(2,1)S(1)} %pad_maximum_fusion.32), channel_id=1, source_target_pairs={{0,8},{8,16},{16,24},{24,0},{1,9},{9,17},{17,25},{25,1},{2,10},{10... | collective-permute-start | bytes 540680 | tf_op jit(solution)/shard_map/ppermute | solution.py:52
  226.9 16.9 %collective-permute-start.10 = (bf16[256,512]{1,0:T(8,128)(2,1)S(1)}, bf16[256,512]{1,0:T(8,128)(2,1)S(1)}, u32[]{:S(2)}, u32[]{:S(2)}) collective-permute-start(bf16[256,512]{1,0:T(8,128)(2,1)S(1)} %pad_maximum_fusion.20), channel_id=1, source_target_pairs={{0,24},{8,0},{16,8},{24,16},{1,25},{9,1},{17,9},{25,17},{2,26},{10... | collective-permute-start | bytes 786440 | tf_op jit(solution)/shard_map/ppermute | solution.py:52
  229.2 20.1 %collective-permute-start.12 = (bf16[256,512]{1,0:T(8,128)(2,1)S(1)}, bf16[256,512]{1,0:T(8,128)(2,1)S(1)}, u32[]{:S(2)}, u32[]{:S(2)}) collective-permute-start(bf16[256,512]{1,0:T(8,128)(2,1)S(1)} %pad_maximum_fusion.21), channel_id=1, source_target_pairs={{0,8},{8,16},{16,24},{24,0},{1,9},{9,17},{17,25},{25,1},{2,10},{10... | collective-permute-start | bytes 786440 | tf_op jit(solution)/shard_map/ppermute | solution.py:52
  243.2 13.1 %collective-permute-start.35 = (bf16[2,4,8,32,512]{4,3,2,1,0:T(8,128)(2,1)}, bf16[2,4,8,32,512]{4,3,2,1,0:T(8,128)(2,1)}, u32[]{:S(2)}, u32[]{:S(2)}) collective-permute-start(bf16[2,4,8,32,512]{4,3,2,1,0:T(8,128)(2,1)} %pad_maximum_fusion.3), channel_id=1, source_target_pairs={{0,2},{2,0},{1,3},{3,1},{4,6},{6,4},{5,7},{7,5},{8,10},{10,8},{9,1... | collective-permute-start | bytes 6291464 | tf_op jit(solution)/shard_map/ppermute | solution.py:47
  243.2 30.2 %collective-permute-start.18 = (bf16[2,4,13,32,512]{4,3,2,1,0:T(8,128)(2,1)}, bf16[2,4,13,32,512]{4,3,2,1,0:T(8,128)(2,1)}, u32[]{:S(2)}, u32[]{:S(2)}) collective-permute-start(bf16[2,4,13,32,512]{4,3,2,1,0:T(8,128)(2,1)} %pad_maximum_fusion.1), channel_id=1, source_target_pairs={{0,2},{2,0},{1,3},{3,1},{4,6},{6,4},{5,7},{7,5},{8,10},{10,8},{9,1... | collective-permute-start | bytes 10223624 | tf_op jit(solution)/shard_map/ppermute | solution.py:47
  343.5 9.5 %collective-permute-start.39 = (bf16[2,96,512]{2,1,0:T(8,128)(2,1)S(1)}, bf16[2,96,512]{2,1,0:T(8,128)(2,1)S(1)}, u32[]{:S(2)}, u32[]{:S(2)}) collective-permute-start(bf16[2,96,512]{2,1,0:T(8,128)(2,1)S(1)} %get-tuple-element.380), channel_id=1, source_target_pairs={{0,24},{8,0},{16,8},{24,16},{1,25},{9,1},{17,9},{25,17},{2,26},{10... | collective-permute-start | bytes 589832 | tf_op jit(solution)/shard_map/ppermute | solution.py:52
  413.4 11.2 %collective-permute-start.45 = (bf16[48,512]{1,0:T(8,128)(2,1)S(1)}, bf16[48,512]{1,0:T(8,128)(2,1)S(1)}, u32[]{:S(2)}, u32[]{:S(2)}) collective-permute-start(bf16[48,512]{1,0:T(8,128)(2,1)S(1)} %get-tuple-element.373), channel_id=1, source_target_pairs={{0,24},{8,0},{16,8},{24,16},{1,25},{9,1},{17,9},{25,17},{2,26},{10... | collective-permute-start | bytes 147464 | tf_op jit(solution)/shard_map/ppermute | solution.py:52
  415.0 9.7 %collective-permute-start.47 = (bf16[48,512]{1,0:T(8,128)(2,1)S(1)}, bf16[48,512]{1,0:T(8,128)(2,1)S(1)}, u32[]{:S(2)}, u32[]{:S(2)}) collective-permute-start(bf16[48,512]{1,0:T(8,128)(2,1)S(1)} %get-tuple-element.374), channel_id=1, source_target_pairs={{0,8},{8,16},{16,24},{24,0},{1,9},{9,17},{17,25},{25,1},{2,10},{10... | collective-permute-start | bytes 147464 | tf_op jit(solution)/shard_map/ppermute | solution.py:52
  497.4 36.9 %collective-permute-start.82 = (bf16[256,512]{1,0:T(8,128)(2,1)}, bf16[256,512]{1,0:T(8,128)(2,1)}, u32[]{:S(2)}, u32[]{:S(2)}) collective-permute-start(bf16[256,512]{1,0:T(8,128)(2,1)} %multiply_convert_fusion.3), channel_id=1, source_target_pairs={{0,1},{1,0},{2,3},{3,2},{4,5},{5,4},{6,7},{7,6},{8,9},{9,8},{10,11... | collective-permute-start | bytes 786440 | tf_op jit(solution)/shard_map/ppermute | solution.py:47
  498.0 31.2 %collective-permute-start.77 = (bf16[176,512]{1,0:T(8,128)(2,1)}, bf16[176,512]{1,0:T(8,128)(2,1)}, u32[]{:S(2)}, u32[]{:S(2)}) collective-permute-start(bf16[176,512]{1,0:T(8,128)(2,1)} %maximum_maximum_fusion.1), channel_id=1, source_target_pairs={{0,1},{1,0},{2,3},{3,2},{4,5},{5,4},{6,7},{7,6},{8,9},{9,8},{10,11... | collective-permute-start | bytes 540680 | tf_op jit(solution)/shard_map/ppermute | solution.py:47
  505.2 145.6 %collective-permute-start.70 = (bf16[8,4,2,32,512]{4,3,2,1,0:T(8,128)(2,1)}, bf16[8,4,2,32,512]{4,3,2,1,0:T(8,128)(2,1)}, u32[]{:S(2)}, u32[]{:S(2)}) collective-permute-start(bf16[8,4,2,32,512]{4,3,2,1,0:T(8,128)(2,1)} %fusion.44), channel_id=1, source_target_pairs={{0,2},{2,0},{1,3},{3,1},{4,6},{6,4},{5,7},{7,5},{8,10},{10,8},{9,1... | collective-permute-start | bytes 6291464 | tf_op jit(solution)/shard_map/ppermute | solution.py:47
  530.1 13.1 %collective-permute-start.78 = (bf16[2,176,512]{2,1,0:T(8,128)(2,1)S(1)}, bf16[2,176,512]{2,1,0:T(8,128)(2,1)S(1)}, u32[]{:S(2)}, u32[]{:S(2)}) collective-permute-start(bf16[2,176,512]{2,1,0:T(8,128)(2,1)S(1)} %get-tuple-element.378), channel_id=1, source_target_pairs={{0,8},{8,16},{16,24},{24,0},{1,9},{9,17},{17,25},{25,1},{2,10},{10... | collective-permute-start | bytes 1081352 | tf_op jit(solution)/shard_map/ppermute | solution.py:52
  530.2 19.0 %collective-permute-start.80 = (bf16[2,176,512]{2,1,0:T(8,128)(2,1)S(1)}, bf16[2,176,512]{2,1,0:T(8,128)(2,1)S(1)}, u32[]{:S(2)}, u32[]{:S(2)}) collective-permute-start(bf16[2,176,512]{2,1,0:T(8,128)(2,1)S(1)} %get-tuple-element.378), channel_id=1, source_target_pairs={{0,24},{8,0},{16,8},{24,16},{1,25},{9,1},{17,9},{25,17},{2,26},{10... | collective-permute-start | bytes 1081352 | tf_op jit(solution)/shard_map/ppermute | solution.py:52
  535.8 43.4 %collective-permute-start.83 = (bf16[2,256,512]{2,1,0:T(8,128)(2,1)S(1)}, bf16[2,256,512]{2,1,0:T(8,128)(2,1)S(1)}, u32[]{:S(2)}, u32[]{:S(2)}) collective-permute-start(bf16[2,256,512]{2,1,0:T(8,128)(2,1)S(1)} %get-tuple-element.353), channel_id=1, source_target_pairs={{0,8},{8,16},{16,24},{24,0},{1,9},{9,17},{17,25},{25,1},{2,10},{10... | collective-permute-start | bytes 1572872 | tf_op jit(solution)/shard_map/ppermute | solution.py:52
  535.9 43.4 %collective-permute-start.85 = (bf16[2,256,512]{2,1,0:T(8,128)(2,1)S(1)}, bf16[2,256,512]{2,1,0:T(8,128)(2,1)S(1)}, u32[]{:S(2)}, u32[]{:S(2)}) collective-permute-start(bf16[2,256,512]{2,1,0:T(8,128)(2,1)S(1)} %get-tuple-element.353), channel_id=1, source_target_pairs={{0,24},{8,0},{16,8},{24,16},{1,25},{9,1},{17,9},{25,17},{2,26},{10... | collective-permute-start | bytes 1572872 | tf_op jit(solution)/shard_map/ppermute | solution.py:52
  543.3 34.1 %collective-permute-start.79 = (bf16[1,176,512]{2,1,0:T(8,128)(2,1)S(1)}, bf16[1,176,512]{2,1,0:T(8,128)(2,1)S(1)}, u32[]{:S(2)}, u32[]{:S(2)}) collective-permute-start(bf16[1,176,512]{2,1,0:T(8,128)(2,1)S(1)} %slice.1245), channel_id=1, source_target_pairs={{0,8},{8,16},{16,24},{24,0},{1,9},{9,17},{17,25},{25,1},{2,10},{10... | collective-permute-start | bytes 540680 | tf_op jit(solution)/shard_map/ppermute | solution.py:52
  549.2 29.8 %collective-permute-start.81 = (bf16[1,176,512]{2,1,0:T(8,128)(2,1)S(1)}, bf16[1,176,512]{2,1,0:T(8,128)(2,1)S(1)}, u32[]{:S(2)}, u32[]{:S(2)}) collective-permute-start(bf16[1,176,512]{2,1,0:T(8,128)(2,1)S(1)} %slice.1246), channel_id=1, source_target_pairs={{0,24},{8,0},{16,8},{24,16},{1,25},{9,1},{17,9},{25,17},{2,26},{10... | collective-permute-start | bytes 540680 | tf_op jit(solution)/shard_map/ppermute | solution.py:52
  577.4 79.4 %collective-permute-start.63 = (bf16[8,4,2,32,512]{4,3,2,1,0:T(8,128)(2,1)}, bf16[8,4,2,32,512]{4,3,2,1,0:T(8,128)(2,1)}, u32[]{:S(2)}, u32[]{:S(2)}) collective-permute-start(bf16[8,4,2,32,512]{4,3,2,1,0:T(8,128)(2,1)} %fusion.43), channel_id=1, source_target_pairs={{0,2},{2,0},{1,3},{3,1},{4,6},{6,4},{5,7},{7,5},{8,10},{10,8},{9,1... | collective-permute-start | bytes 6291464 | tf_op jit(solution)/shard_map/ppermute | solution.py:47
  579.0 16.0 %collective-permute-start.49 = (bf16[5,4,2,32,512]{4,3,2,1,0:T(8,128)(2,1)S(1)}, bf16[5,4,2,32,512]{4,3,2,1,0:T(8,128)(2,1)S(1)}, u32[]{:S(2)}, u32[]{:S(2)}) collective-permute-start(bf16[5,4,2,32,512]{4,3,2,1,0:T(8,128)(2,1)S(1)} %fusion.66), channel_id=1, source_target_pairs={{0,2},{2,0},{1,3},{3,1},{4,6},{6,4},{5,7},{7,5},{8,10},{10,8},{9,1... | collective-permute-start | bytes 3932168 | tf_op jit(solution)/shard_map/ppermute | solution.py:47
  579.3 13.2 %collective-permute-start.84 = (bf16[1,256,512]{2,1,0:T(8,128)(2,1)S(1)}, bf16[1,256,512]{2,1,0:T(8,128)(2,1)S(1)}, u32[]{:S(2)}, u32[]{:S(2)}) collective-permute-start(bf16[1,256,512]{2,1,0:T(8,128)(2,1)S(1)} %slice.1247), channel_id=1, source_target_pairs={{0,8},{8,16},{16,24},{24,0},{1,9},{9,17},{17,25},{25,1},{2,10},{10... | collective-permute-start | bytes 786440 | tf_op jit(solution)/shard_map/ppermute | solution.py:52
  579.4 15.3 %collective-permute-start.86 = (bf16[1,256,512]{2,1,0:T(8,128)(2,1)S(1)}, bf16[1,256,512]{2,1,0:T(8,128)(2,1)S(1)}, u32[]{:S(2)}, u32[]{:S(2)}) collective-permute-start(bf16[1,256,512]{2,1,0:T(8,128)(2,1)S(1)} %slice.1248), channel_id=1, source_target_pairs={{0,24},{8,0},{16,8},{24,16},{1,25},{9,1},{17,9},{25,17},{2,26},{10... | collective-permute-start | bytes 786440 | tf_op jit(solution)/shard_map/ppermute | solution.py:52
  592.5 79.6 %collective-permute-start.56 = (bf16[8,4,2,32,512]{4,3,2,1,0:T(8,128)(2,1)}, bf16[8,4,2,32,512]{4,3,2,1,0:T(8,128)(2,1)}, u32[]{:S(2)}, u32[]{:S(2)}) collective-permute-start(bf16[8,4,2,32,512]{4,3,2,1,0:T(8,128)(2,1)} %fusion.45), channel_id=1, source_target_pairs={{0,2},{2,0},{1,3},{3,1},{4,6},{6,4},{5,7},{7,5},{8,10},{10,8},{9,1... | collective-permute-start | bytes 6291464 | tf_op jit(solution)/shard_map/ppermute | solution.py:47
  595.8 23.7 %collective-permute-start.50 = (bf16[5,4,32,512]{3,2,1,0:T(8,128)(2,1)S(1)}, bf16[5,4,32,512]{3,2,1,0:T(8,128)(2,1)S(1)}, u32[]{:S(2)}, u32[]{:S(2)}) collective-permute-start(bf16[5,4,32,512]{3,2,1,0:T(8,128)(2,1)S(1)} %fusion.97), channel_id=1, source_target_pairs={{0,4},{4,0},{1,5},{5,1},{2,6},{6,2},{3,7},{7,3},{8,12},{12,8},{9,1... | collective-permute-start | bytes 1966088 | tf_op jit(solution)/shard_map/ppermute | solution.py:47
  615.6 66.6 %collective-permute-start.87 = (bf16[2,1000,512]{2,1,0:T(8,128)(2,1)}, bf16[2,1000,512]{2,1,0:T(8,128)(2,1)}, u32[]{:S(2)}, u32[]{:S(2)}) collective-permute-start(bf16[2,1000,512]{2,1,0:T(8,128)(2,1)} %fusion.49), channel_id=1, source_target_pairs={{0,2},{2,0},{1,3},{3,1},{4,6},{6,4},{5,7},{7,5},{8,10},{10,8},{9,1... | collective-permute-start | bytes 6144008 | tf_op jit(solution)/shard_map/ppermute | solution.py:47
  635.8 12.8 %collective-permute-start.53 = (bf16[3,32,512]{1,2,0:T(8,128)(2,1)}, bf16[3,32,512]{1,2,0:T(8,128)(2,1)S(1)}, u32[]{:S(2)}, u32[]{:S(2)}) collective-permute-start(bf16[3,32,512]{1,2,0:T(8,128)(2,1)} %get-tuple-element.311), channel_id=1, source_target_pairs={{0,8},{8,16},{16,24},{24,0},{1,9},{9,17},{17,25},{25,1},{2,10},{10... | collective-permute-start | bytes 294920 | tf_op jit(solution)/shard_map/ppermute | solution.py:52
  648.5 16.5 %collective-permute-start.52 = (bf16[5,32,512]{2,1,0:T(8,128)(2,1)}, bf16[5,32,512]{2,1,0:T(8,128)(2,1)}, u32[]{:S(2)}, u32[]{:S(2)}) collective-permute-start(bf16[5,32,512]{2,1,0:T(8,128)(2,1)} %pad_maximum_fusion.33), channel_id=1, source_target_pairs={{0,24},{8,0},{16,8},{24,16},{1,25},{9,1},{17,9},{25,17},{2,26},{10... | collective-permute-start | bytes 491528 | tf_op jit(solution)/shard_map/ppermute | solution.py:52
  650.8 17.7 %collective-permute-start.54 = (bf16[5,32,512]{2,1,0:T(8,128)(2,1)S(1)}, bf16[5,32,512]{2,1,0:T(8,128)(2,1)S(1)}, u32[]{:S(2)}, u32[]{:S(2)}) collective-permute-start(bf16[5,32,512]{2,1,0:T(8,128)(2,1)S(1)} %pad_maximum_fusion.34), channel_id=1, source_target_pairs={{0,8},{8,16},{16,24},{24,0},{1,9},{9,17},{17,25},{25,1},{2,10},{10... | collective-permute-start | bytes 491528 | tf_op jit(solution)/shard_map/ppermute | solution.py:52
  657.8 30.6 %collective-permute-start.71 = (bf16[8,4,32,512]{3,2,1,0:T(8,128)(2,1)}, bf16[8,4,32,512]{3,2,1,0:T(8,128)(2,1)}, u32[]{:S(2)}, u32[]{:S(2)}) collective-permute-start(bf16[8,4,32,512]{3,2,1,0:T(8,128)(2,1)} %fusion.82), channel_id=1, source_target_pairs={{0,4},{4,0},{1,5},{5,1},{2,6},{6,2},{3,7},{7,3},{8,12},{12,8},{9,1... | collective-permute-start | bytes 3145736 | tf_op jit(solution)/shard_map/ppermute | solution.py:47
  665.0 41.7 %collective-permute-start.64 = (bf16[8,4,32,512]{3,2,1,0:T(8,128)(2,1)}, bf16[8,4,32,512]{3,2,1,0:T(8,128)(2,1)}, u32[]{:S(2)}, u32[]{:S(2)}) collective-permute-start(bf16[8,4,32,512]{3,2,1,0:T(8,128)(2,1)} %fusion.81), channel_id=1, source_target_pairs={{0,4},{4,0},{1,5},{5,1},{2,6},{6,2},{3,7},{7,3},{8,12},{12,8},{9,1... | collective-permute-start | bytes 3145736 | tf_op jit(solution)/shard_map/ppermute | solution.py:47
  678.7 50.4 %collective-permute-start.57 = (bf16[8,4,32,512]{3,2,1,0:T(8,128)(2,1)}, bf16[8,4,32,512]{3,2,1,0:T(8,128)(2,1)}, u32[]{:S(2)}, u32[]{:S(2)}) collective-permute-start(bf16[8,4,32,512]{3,2,1,0:T(8,128)(2,1)} %fusion.80), channel_id=1, source_target_pairs={{0,4},{4,0},{1,5},{5,1},{2,6},{6,2},{3,7},{7,3},{8,12},{12,8},{9,1... | collective-permute-start | bytes 3145736 | tf_op jit(solution)/shard_map/ppermute | solution.py:47
  686.9 106.9 %collective-permute-start.88 = (bf16[1000,512]{1,0:T(8,128)(2,1)}, bf16[1000,512]{1,0:T(8,128)(2,1)}, u32[]{:S(2)}, u32[]{:S(2)}) collective-permute-start(bf16[1000,512]{1,0:T(8,128)(2,1)} %fusion.93), channel_id=1, source_target_pairs={{0,4},{4,0},{1,5},{5,1},{2,6},{6,2},{3,7},{7,3},{8,12},{12,8},{9,1... | collective-permute-start | bytes 3072008 | tf_op jit(solution)/shard_map/ppermute | solution.py:47
  690.5 40.4 %collective-permute-start.72 = (bf16[4,32,512]{2,1,0:T(8,128)(2,1)S(1)}, bf16[4,32,512]{2,1,0:T(8,128)(2,1)S(1)}, u32[]{:S(2)}, u32[]{:S(2)}) collective-permute-start(bf16[4,32,512]{2,1,0:T(8,128)(2,1)S(1)} %get-tuple-element.320), channel_id=1, source_target_pairs={{0,24},{8,0},{16,8},{24,16},{1,25},{9,1},{17,9},{25,17},{2,26},{10... | collective-permute-start | bytes 393224 | tf_op jit(solution)/shard_map/ppermute | solution.py:52
  693.5 41.3 %collective-permute-start.74 = (bf16[4,32,512]{2,1,0:T(8,128)(2,1)S(1)}, bf16[4,32,512]{2,1,0:T(8,128)(2,1)S(1)}, u32[]{:S(2)}, u32[]{:S(2)}) collective-permute-start(bf16[4,32,512]{2,1,0:T(8,128)(2,1)S(1)} %get-tuple-element.322), channel_id=1, source_target_pairs={{0,8},{8,16},{16,24},{24,0},{1,9},{9,17},{17,25},{25,1},{2,10},{10... | collective-permute-start | bytes 393224 | tf_op jit(solution)/shard_map/ppermute | solution.py:52
  708.4 26.6 %collective-permute-start.65 = (bf16[4,32,512]{2,1,0:T(8,128)(2,1)S(1)}, bf16[4,32,512]{2,1,0:T(8,128)(2,1)S(1)}, u32[]{:S(2)}, u32[]{:S(2)}) collective-permute-start(bf16[4,32,512]{2,1,0:T(8,128)(2,1)S(1)} %get-tuple-element.325), channel_id=1, source_target_pairs={{0,24},{8,0},{16,8},{24,16},{1,25},{9,1},{17,9},{25,17},{2,26},{10... | collective-permute-start | bytes 393224 | tf_op jit(solution)/shard_map/ppermute | solution.py:52
  729.2 9.7 %collective-permute-start.67 = (bf16[4,32,512]{2,1,0:T(8,128)(2,1)S(1)}, bf16[4,32,512]{2,1,0:T(8,128)(2,1)S(1)}, u32[]{:S(2)}, u32[]{:S(2)}) collective-permute-start(bf16[4,32,512]{2,1,0:T(8,128)(2,1)S(1)} %get-tuple-element.327), channel_id=1, source_target_pairs={{0,8},{8,16},{16,24},{24,0},{1,9},{9,17},{17,25},{25,1},{2,10},{10... | collective-permute-start | bytes 393224 | tf_op jit(solution)/shard_map/ppermute | solution.py:52
  735.0 14.0 %collective-permute-start.73 = (bf16[8,32,512]{2,1,0:T(8,128)(2,1)S(1)}, bf16[8,32,512]{2,1,0:T(8,128)(2,1)S(1)}, u32[]{:S(2)}, u32[]{:S(2)}) collective-permute-start(bf16[8,32,512]{2,1,0:T(8,128)(2,1)S(1)} %pad_maximum_fusion.27), channel_id=1, source_target_pairs={{0,24},{8,0},{16,8},{24,16},{1,25},{9,1},{17,9},{25,17},{2,26},{10... | collective-permute-start | bytes 786440 | tf_op jit(solution)/shard_map/ppermute | solution.py:52
  738.9 15.7 %collective-permute-start.75 = (bf16[8,32,512]{2,1,0:T(8,128)(2,1)S(1)}, bf16[8,32,512]{2,1,0:T(8,128)(2,1)S(1)}, u32[]{:S(2)}, u32[]{:S(2)}) collective-permute-start(bf16[8,32,512]{2,1,0:T(8,128)(2,1)S(1)} %pad_maximum_fusion.28), channel_id=1, source_target_pairs={{0,8},{8,16},{16,24},{24,0},{1,9},{9,17},{17,25},{25,1},{2,10},{10... | collective-permute-start | bytes 786440 | tf_op jit(solution)/shard_map/ppermute | solution.py:52
  739.1 20.7 %collective-permute-start.66 = (bf16[8,32,512]{2,1,0:T(8,128)(2,1)S(1)}, bf16[8,32,512]{2,1,0:T(8,128)(2,1)S(1)}, u32[]{:S(2)}, u32[]{:S(2)}) collective-permute-start(bf16[8,32,512]{2,1,0:T(8,128)(2,1)S(1)} %pad_maximum_fusion.25), channel_id=1, source_target_pairs={{0,24},{8,0},{16,8},{24,16},{1,25},{9,1},{17,9},{25,17},{2,26},{10... | collective-permute-start | bytes 786440 | tf_op jit(solution)/shard_map/ppermute | solution.py:52
  743.3 22.6 %collective-permute-start.68 = (bf16[8,32,512]{2,1,0:T(8,128)(2,1)S(1)}, bf16[8,32,512]{2,1,0:T(8,128)(2,1)S(1)}, u32[]{:S(2)}, u32[]{:S(2)}) collective-permute-start(bf16[8,32,512]{2,1,0:T(8,128)(2,1)S(1)} %pad_maximum_fusion.26), channel_id=1, source_target_pairs={{0,8},{8,16},{16,24},{24,0},{1,9},{9,17},{17,25},{25,1},{2,10},{10... | collective-permute-start | bytes 786440 | tf_op jit(solution)/shard_map/ppermute | solution.py:52
  749.0 18.9 %collective-permute-start.59 = (bf16[8,32,512]{2,1,0:T(8,128)(2,1)S(1)}, bf16[8,32,512]{2,1,0:T(8,128)(2,1)S(1)}, u32[]{:S(2)}, u32[]{:S(2)}) collective-permute-start(bf16[8,32,512]{2,1,0:T(8,128)(2,1)S(1)} %pad_maximum_fusion.23), channel_id=1, source_target_pairs={{0,24},{8,0},{16,8},{24,16},{1,25},{9,1},{17,9},{25,17},{2,26},{10... | collective-permute-start | bytes 786440 | tf_op jit(solution)/shard_map/ppermute | solution.py:52
  754.6 18.1 %collective-permute-start.61 = (bf16[8,32,512]{2,1,0:T(8,128)(2,1)S(1)}, bf16[8,32,512]{2,1,0:T(8,128)(2,1)S(1)}, u32[]{:S(2)}, u32[]{:S(2)}) collective-permute-start(bf16[8,32,512]{2,1,0:T(8,128)(2,1)S(1)} %pad_maximum_fusion.24), channel_id=1, source_target_pairs={{0,8},{8,16},{16,24},{24,0},{1,9},{9,17},{17,25},{25,1},{2,10},{10... | collective-permute-start | bytes 786440 | tf_op jit(solution)/shard_map/ppermute | solution.py:52
  759.8 14.3 %collective-permute-start.76 = (bf16[8,32,512]{2,1,0:T(8,128)(2,1)S(1)}, bf16[8,32,512]{2,1,0:T(8,128)(2,1)S(1)}, u32[]{:S(2)}, u32[]{:S(2)}) collective-permute-start(bf16[8,32,512]{2,1,0:T(8,128)(2,1)S(1)} %fusion.160), channel_id=1, source_target_pairs={{0,1},{1,0},{2,3},{3,2},{4,5},{5,4},{6,7},{7,6},{8,9},{9,8},{10,11... | collective-permute-start | bytes 786440 | tf_op jit(solution)/shard_map/ppermute | solution.py:47
  (314 other events, 2913.8 us)

commit v2 on v1

v2 whole, which is shorter than its diff:
```python
import functools
import math

import jax
import jax.numpy as jnp
from jax import lax
from jax.experimental import pallas as pl
from jax.experimental.pallas import tpu as pltpu
from jax.sharding import Mesh
from jax.sharding import PartitionSpec as P

D = 512
HDIM = 64
LCLS = 256
ROW = 256
SENTS = 8
MASKED = 96
NPARAM = 23858688


HIGHEST = lax.Precision.HIGHEST
EPSILON = 1e-05
MASK_TOKEN = 3
MOMENTUM = 0.9
KEEP = 0.9
CLIP = 0.02
LENGTH_WEIGHT = 0.1
NEGATIVE = -1e30
RATE_SCALE = 0.25
RATE_FACTORS = (1.0, 1.0, 1.0, 1.0, 6.0, 24.0, 1.0)


def sinusoid(count, width):
    place = jnp.arange(count, dtype=jnp.float32)[:, None]
    index = jnp.arange(width // 2, dtype=jnp.float32)[None, :]
    angle = place * jnp.exp(-math.log(10000.0) * 2.0 * index / width)
    return jnp.concatenate([jnp.sin(angle), jnp.cos(angle)], axis=1)


SWAP = [(0, 1), (1, 0)]


def swap(value, axis):
    return lax.ppermute(value, axis, SWAP)


def shift(value, by):
    count = lax.axis_size("z")
    return lax.ppermute(value, "z", [(i, (i + by) % count) for i in range(count)])


def low(value):
    return value.astype(jnp.bfloat16)


def wide(value):
    return value.astype(jnp.float32)


def ring_first(value):
    if lax.axis_size("z") != 4:
        return value, value
    return shift(value, 1), shift(value, -1)


def ring_second(value, below, above):
    count = lax.axis_size("z")
    if count != 4:
        whole = lax.all_gather(value, "z", axis=0)
        here = lax.axis_index("z")
        return [lax.dynamic_index_in_dim(whole, (here - k) % count, 0, False) for k in range(count)]
    half = value.shape[0] // 2
    return [value, below, shift(below[:half], 1), shift(above[half:], -1), above]


def ring_gather(value):
    return ring_second(value, *ring_first(value))


def ring_scatter(blocks):
    count = lax.axis_size("z")
    if count != 4:
        here = lax.axis_index("z")
        order = (here - jnp.arange(count)) % count
        stacked = jnp.stack([low(block) for block in blocks])
        whole = jnp.zeros_like(stacked).at[order].set(stacked)
        return wide(lax.psum_scatter(whole, "z", scatter_dimension=0))
    half = blocks[0].shape[0] // 2
    from_above = shift(low(blocks[2][:half]), -1)
    from_below = shift(low(blocks[2][half:]), 1)
    down = jnp.concatenate([wide(blocks[1][:half]) + wide(from_above), wide(blocks[1][half:])])
    up = jnp.concatenate([wide(blocks[3][:half]), wide(blocks[3][half:]) + wide(from_below)])
    from_above = shift(low(down), -1)
    from_below = shift(low(up), 1)
    return wide(blocks[0]) + wide(from_above) + wide(from_below)


def gather_weight(value):
    return lax.all_gather(value, ("z", "y", "core"), axis=1, tiled=True)


def take(value, index, axis):
    return lax.dynamic_index_in_dim(value, index, axis, False)


def add_swap(value):
    mine = low(value)
    return wide(mine) + wide(swap(mine, "vocab"))


def by_core(grads):
    core = lax.axis_index("core")
    count = lax.axis_size("z")
    parts = grads.reshape(grads.shape[0], count, 2, 2, -1, grads.shape[2])
    parts = parts.transpose(0, 3, 2, 1, 4, 5).reshape(grads.shape[0], 2, -1, grads.shape[2])
    return take(parts, core, 1), take(parts, 1 - core, 1)


def swap_core(mine, theirs):
    if lax.axis_size("z") != 4:
        mine, theirs = by_core(jnp.concatenate([mine, theirs], axis=1))
    return mine, swap(theirs, "core")


def low_sum(*refs):
    return low(sum(wide(ref[...]) for ref in refs))


def sums_kernel(at_ref, *refs):
    count = len(refs) // 3
    for k in range(count):
        refs[2 * count + k][...] = low_sum(refs[2 * k], refs[2 * k + 1])


def line_kernel(at_ref, *refs):
    own, down, far, up = (low_sum(refs[2 * k], refs[2 * k + 1]) for k in range(4))
    own_ref, down_ref, far_down_ref, far_up_ref, up_ref = refs[8:]
    own_ref[...] = own
    down_ref[...] = down
    up_ref[...] = up
    half = far.shape[2] // 2
    far_down_ref[...] = far[:, :, :half]
    far_up_ref[...] = far[:, :, half:]


def pass_kernel(down_ref, up_ref, above_ref, below_ref, down_out, up_out):
    half = above_ref.shape[2]
    down_out[:, :, :half] = low(wide(down_ref[:, :, :half]) + wide(above_ref[...]))
    down_out[:, :, half:] = down_ref[:, :, half:]
    up_out[:, :, :half] = up_ref[:, :, :half]
    up_out[:, :, half:] = low(wide(up_ref[:, :, half:]) + wide(below_ref[...]))


def three_kernel(one_ref, two_ref, three_ref, out_ref):
    out_ref[...] = low_sum(one_ref, two_ref, three_ref)


def two_kernel(one_ref, two_ref, out_ref, square_ref):
    total = wide(one_ref[...]) + wide(two_ref[...])
    out_ref[...] = total
    square_ref[0, 0] = jnp.sum(total * total)


def both_kernel(at_ref, mine_ref, theirs_ref, out_ref, square_ref):
    size = mine_ref.shape[0]
    mine, theirs = (wide(mine_ref[...]), wide(theirs_ref[...]))
    out_ref[pl.ds(at_ref[0] * size, size)] = mine
    out_ref[pl.ds((1 - at_ref[0]) * size, size)] = theirs
    square_ref[0, 0] = jnp.sum(mine * mine) + jnp.sum(theirs * theirs)


def staged(kernel, at, steps, block, mine, theirs, places, outs, out_place):
    def spec(place):
        return pl.BlockSpec(block, lambda i, at: place(i, at[0]))

    def out_spec(shape):
        return pl.BlockSpec(block[:2] + shape[2:], lambda i, at: out_place(i))

    return pl.pallas_call(
        kernel,
        grid_spec=pltpu.PrefetchScalarGridSpec(
            num_scalar_prefetch=1,
            grid=(steps,),
            in_specs=[spec(place) for place in places for _ in (0, 1)],
            out_specs=[out_spec(shape) for shape in outs],
        ),
        out_shape=[jax.ShapeDtypeStruct(shape, jnp.bfloat16) for shape in outs],
        compiler_params=pltpu.CompilerParams(vmem_limit_bytes=VMEM_BYTES),
    )(at[None].astype(jnp.int32), *([mine, theirs] * len(places)))


def add_vocab_parts(mine, theirs):
    blocks, rows, columns = mine.shape
    kept = (blocks // 2, rows, columns)
    steps = 2
    return staged(
        sums_kernel, lax.axis_index("vocab"), steps, (blocks // 2 // steps, rows, columns),
        mine, theirs,
        (lambda i, at: (at * steps + i, 0, 0), lambda i, at: ((1 - at) * steps + i, 0, 0)),
        (kept, kept), lambda i: (i, 0, 0),
    )


def add_side_parts(mine, theirs):
    blocks, rows, columns = mine.shape
    kept = (blocks, rows // 2, columns)
    steps = 2
    return staged(
        sums_kernel, lax.axis_index("y"), steps, (blocks, rows // 2 // steps, columns),
        mine, theirs,
        (lambda i, at: (0, at * steps + i, 0), lambda i, at: (0, (1 - at) * steps + i, 0)),
        (kept, kept), lambda i: (0, i, 0),
    )


def line_parts(mine, theirs):
    here, count = (lax.axis_index("z"), lax.axis_size("z"))
    blocks, rows, columns = mine.shape
    if count != 4:
        return low(wide(mine) + wide(theirs)).reshape(blocks, count, -1, columns)
    part = (blocks, rows // 4, columns)
    half = (blocks, rows // 4, columns // 2)
    places = [lambda i, at, k=k: (0, lax.rem(at - k + 4, 4), 0) for k in range(4)]
    return staged(
        line_kernel, here, 1, part, mine, theirs, places, (part, part, half, half, part),
        lambda i: (0, 0, 0),
    )


def line_first(parts):
    if lax.axis_size("z") != 4:
        return parts
    return shift(parts[2], -1), shift(parts[3], 1)


def line_second(parts, near):
    if lax.axis_size("z") != 4:
        return low(lax.psum_scatter(near, "z", scatter_dimension=1))
    own, down, _, _, up = parts
    down, up = run(pass_kernel, (down, up), down, up, *near)
    return run(three_kernel, (own,), own, shift(down, -1), shift(up, 1))[0]


SQUARE = jax.ShapeDtypeStruct((1, 1), jnp.float32)


def add_vocab_last(part):
    out = jax.ShapeDtypeStruct(part.shape, jnp.float32)
    total, square = run(two_kernel, (out, SQUARE), part, swap(part, "vocab"))
    return total, square[0, 0]


def join_vocab(part):
    out = jax.ShapeDtypeStruct((2 * part.shape[0],) + part.shape[1:], jnp.float32)
    half = lax.axis_index("vocab")[None].astype(jnp.int32)
    total, square = run(both_kernel, (out, SQUARE), half, part, swap(part, "vocab"))
    return total, square[0, 0]


def after(value, *others):
    return lax.optimization_barrier((value,) + others)[0]


def pair_vocab(value):
    return jnp.stack([value, swap(value, "vocab")])


def gather_group(value):
    pieces = ring_gather(pair_vocab(value))
    return jnp.concatenate([piece.reshape(-1, value.shape[-1]) for piece in pieces])


def add_vocab(parts):
    return parts[..., 0, :, :] + swap(low(parts[..., 1, :, :]), "vocab")


def scatter_line(parts):
    return ring_scatter([parts[k] for k in range(parts.shape[0])])


def scatter_group(parts):
    return scatter_line(add_vocab(parts))


def butterfly(value, join, axes):
    for axis in axes:
        count = lax.axis_size(axis)
        step = 1
        while step < count:
            pairs = [(i, i ^ step) for i in range(count)]
            value = join(value, lax.ppermute(value, axis, pairs))
            step *= 2
    return value


def join_totals(left, right):
    peak = jnp.maximum(left[0], right[0])
    return jnp.stack(
        [peak, left[1] * jnp.exp(left[0] - peak) + right[1] * jnp.exp(right[0] - peak)]
    )


def turn(value):
    count = lax.axis_size("z")
    here, half = (lax.axis_index("z"), lax.axis_index("vocab"))
    value = jnp.where(half == 0, value, value[:, ::-1])
    backward = value[::-1]
    twice = jnp.concatenate([backward, backward])
    return lax.dynamic_slice_in_dim(twice, count - 1 - here, count, 0)


SCALE = HDIM ** (-0.5)
GELU_A = math.sqrt(2.0 / math.pi)
GELU_B = 0.044715


def dot(left, right):
    return jnp.dot(left, right, preferred_element_type=jnp.float32)


def dot_left(left, right):
    return lax.dot_general(left, right, (((0,), (0,)), ((), ())), preferred_element_type=jnp.float32)


def dot_right(left, right):
    return lax.dot_general(left, right, (((1,), (1,)), ((), ())), preferred_element_type=jnp.float32)


def norm_parts(stream):
    centred = stream - jnp.mean(stream, axis=-1, keepdims=True)
    inverse = lax.rsqrt(jnp.mean(centred * centred, axis=-1, keepdims=True) + EPSILON)
    return centred * inverse, inverse


def norm_back(grad, stream, gain):
    normed, inverse = norm_parts(stream)
    scaled = grad * gain
    through = scaled - jnp.mean(scaled, axis=-1, keepdims=True)
    through = through - normed * jnp.mean(scaled * normed, axis=-1, keepdims=True)
    return through * inverse, jnp.sum(grad * normed, axis=0, keepdims=True)


def gelu_parts(hidden):
    bend = jnp.tanh(GELU_A * (hidden + GELU_B * hidden * hidden * hidden))
    return bend, 0.5 * (1.0 + bend)


def lane_halves(kind):
    first = lax.broadcasted_iota(jnp.int32, (1, 2 * HDIM), 1) < HDIM
    ones = first.astype(jnp.float32)
    return first, (ones.astype(kind), (1.0 - ones).astype(kind))


def softmax_of(query, keys, allowed):
    scores = jnp.where(allowed, dot_right(query, keys) * SCALE, NEGATIVE)
    expo = jnp.exp(scores - jnp.max(scores, axis=-1, keepdims=True))
    return expo / jnp.sum(expo, axis=-1, keepdims=True)


def attend_inside(low_query, low_memory, w, allowed, q_ref, k_ref, v_ref, o_ref):
    q_ref[...] = low(dot(low_query, w[0]))
    k_ref[...] = low(dot(low_memory, w[1]))
    v_ref[...] = low(dot(low_memory, w[2]))
    first, keeps = lane_halves(jnp.bfloat16)
    for tile in range(0, D, 2 * HDIM):
        lanes = slice(tile, tile + 2 * HDIM)
        query, keys, values = (q_ref[:, lanes], k_ref[:, lanes], v_ref[:, lanes])
        outs = [
            dot(low(softmax_of(query * keep, keys, allowed)), values) for keep in keeps
        ]
        o_ref[:, lanes] = low(jnp.where(first, outs[0], outs[1]))
    return dot(o_ref[...], w[3])


def down_blocks(w, plain, wd_ref):
    if plain:
        return [w[4 + j] for j in range(4)]
    rows = D // 16
    for place in range(16):
        for j in range(4):
            start = (place % 4) * 4 * rows + j * rows
            wd_ref[place // 4, start : start + rows] = w[4 + j, place * rows : (place + 1) * rows]
    return [wd_ref[j] for j in range(4)]


def ffn_inside(normed, w, plain, h_ref, wd_ref):
    branch = None
    down = down_blocks(w, plain, wd_ref)
    for j in range(4):
        hidden = dot(normed, w[j])
        h_ref[j] = hidden
        part = dot(low(hidden * gelu_parts(hidden)[1]), down[j])
        branch = part if branch is None else branch + part
    return branch


def store_split(core_ref, mine_ref, theirs_ref, j, value):
    value = low(value)
    count = core_ref.shape[0]
    step = D // (4 * count)
    if count != 4:
        mine_ref[j] = value[: D // 2]
        theirs_ref[j] = value[D // 2 :]
        return
    upper, lower = (
        jnp.concatenate(
            [
                value[((z * 2 + y) * 2 + c) * step : ((z * 2 + y) * 2 + c + 1) * step]
                for y in (0, 1)
                for z in range(count)
            ]
        )
        for c in (0, 1)
    )
    first = core_ref[0] == 0
    mine_ref[j] = jnp.where(first, upper, lower)
    theirs_ref[j] = jnp.where(first, lower, upper)


def enc_fwd_kernel(plain, x_ref, gain_ref, wa_ref, wf_ref, sc_ref, sr_ref, x1_ref, x2_ref, top_ref, q_ref, k_ref, v_ref, o_ref, h_ref, *wd):
    allowed = sc_ref[...] == sr_ref[...]
    stream = x_ref[...]
    normed = low(norm_parts(stream)[0] * gain_ref[0:1])
    stream = stream + attend_inside(normed, normed, wa_ref, allowed, q_ref, k_ref, v_ref, o_ref)
    x1_ref[...] = stream
    normed = low(norm_parts(stream)[0] * gain_ref[1:2])
    stream = stream + ffn_inside(normed, wf_ref, plain, h_ref, *wd)
    x2_ref[...] = stream
    top_ref[...] = norm_parts(stream)[0] * gain_ref[2:3]


def dec_self_kernel(x_ref, gain_ref, w_ref, tc_ref, tr_ref, y1_ref, q_ref, k_ref, v_ref, o_ref):
    stream = x_ref[...]
    normed = low(norm_parts(stream)[0] * gain_ref[3:4])
    branch = attend_inside(
        normed, normed, w_ref, tc_ref[...] == tr_ref[...], q_ref, k_ref, v_ref, o_ref
    )
    y1_ref[...] = stream + branch


def dec_rest_kernel(plain, y1_ref, mem_ref, gain_ref, wa_ref, wf_ref, tc_ref, sr_ref, y2_ref, y3_ref, top_ref, q_ref, k_ref, v_ref, o_ref, h_ref, *wd):
    stream = y1_ref[...]
    normed = low(norm_parts(stream)[0] * gain_ref[4:5])
    memory = low(mem_ref[...])
    stream = stream + attend_inside(
        normed, memory, wa_ref, tc_ref[...] == sr_ref[...], q_ref, k_ref, v_ref, o_ref
    )
    y2_ref[...] = stream
    normed = low(norm_parts(stream)[0] * gain_ref[5:6])
    stream = stream + ffn_inside(normed, wf_ref, plain, h_ref, *wd)
    y3_ref[...] = stream
    top_ref[...] = norm_parts(stream)[0] * gain_ref[6:7]


def store_down(core_ref, mine_ref, theirs_ref, j, value):
    if core_ref.shape[0] != 4:
        store_split(core_ref, mine_ref, theirs_ref, 4 + j, value)
        return
    value = low(value)
    first = core_ref[0] == 0
    rows = D // 16
    for y in (0, 1):
        for part in range(4):
            upper, lower = (
                value[start : start + rows]
                for start in ((y * 2 + c) * 4 * rows + part * rows for c in (0, 1))
            )
            to = slice((y * 4 + j) * rows, (y * 4 + j + 1) * rows)
            mine_ref[4 + part, to] = jnp.where(first, upper, lower)
            theirs_ref[4 + part, to] = jnp.where(first, lower, upper)


def ffn_back_kernel(place, plain, grad_ref, end_ref, mid_ref, h_ref, gain_ref, w_ref, core_ref, out_ref, mine_ref, theirs_ref, dg_ref, *wd):
    grad_stream, end_gain = norm_back(grad_ref[...], end_ref[...], gain_ref[place + 1 : place + 2])
    grad_low = low(grad_stream)
    gain = gain_ref[place : place + 1]
    normed = low(norm_parts(mid_ref[...])[0] * gain)
    total = None
    down = down_blocks(w_ref, plain, *(wd or (None,)))
    for j in range(4):
        hidden = h_ref[j]
        bend, half = gelu_parts(hidden)
        store_down(core_ref, mine_ref, theirs_ref, j, dot_left(low(hidden * half), grad_low))
        slope = half + 0.5 * hidden * (1.0 - bend * bend) * GELU_A * (
            1.0 + 3.0 * GELU_B * hidden * hidden
        )
        grad_hidden = low(dot_right(grad_low, down[j]) * slope)
        store_split(core_ref, mine_ref, theirs_ref, j, dot_left(normed, grad_hidden))
        part = dot_right(grad_hidden, w_ref[j])
        total = part if total is None else total + part
    extra, mid_gain = norm_back(total, mid_ref[...], gain)
    out_ref[...] = grad_stream + extra
    dg_ref[...] = jnp.concatenate([mid_gain, end_gain], axis=0)


def attn_back_inside(grad_low, normed, memory, refs, w, allowed, dw_refs, scratch):
    q_ref, k_ref, v_ref, o_ref = refs
    do_ref, dq_ref, dk_ref, dv_ref = scratch
    store_split(*dw_refs, 3, dot_left(o_ref[...], grad_low))
    do_ref[...] = low(dot_right(grad_low, w[3]))
    first, keeps = lane_halves(jnp.bfloat16)
    for tile in range(0, D, 2 * HDIM):
        lanes = slice(tile, tile + 2 * HDIM)
        query, keys, values, grad_mixed = (
            ref[:, lanes] for ref in (q_ref, k_ref, v_ref, do_ref)
        )
        found = []
        for keep in keeps:
            probs = softmax_of(query * keep, keys, allowed)
            grad_probs = dot_right(grad_mixed * keep, values)
            inner = jnp.sum(probs * grad_probs, axis=-1, keepdims=True)
            grad_scores = low(probs * (grad_probs - inner))
            found.append(
                (
                    dot(grad_scores, keys),
                    dot_left(grad_scores, query),
                    dot_left(low(probs), grad_mixed),
                )
            )
        dq_ref[:, lanes] = low(jnp.where(first, found[0][0], found[1][0]) * SCALE)
        dk_ref[:, lanes] = low(jnp.where(first, found[0][1], found[1][1]) * SCALE)
        dv_ref[:, lanes] = low(jnp.where(first, found[0][2], found[1][2]))
    store_split(*dw_refs, 0, dot_left(normed, dq_ref[...]))
    store_split(*dw_refs, 1, dot_left(memory, dk_ref[...]))
    store_split(*dw_refs, 2, dot_left(memory, dv_ref[...]))
    grad_query = dot_right(dq_ref[...], w[0])
    grad_memory = dot_right(dk_ref[...], w[1]) + dot_right(dv_ref[...], w[2])
    return grad_query, grad_memory


def self_back_kernel(place, grad_ref, x_ref, q_ref, k_ref, v_ref, o_ref, gain_ref, w_ref, sc_ref, sr_ref, core_ref, held_ref, kept_ref, out_ref, mine_ref, theirs_ref, dg_ref, *scratch):
    gain = gain_ref[place : place + 1]
    normed = low(norm_parts(x_ref[...])[0] * gain)
    grad_query, grad_memory = attn_back_inside(
        low(grad_ref[...]), normed, normed, (q_ref, k_ref, v_ref, o_ref), w_ref,
        sc_ref[...] == sr_ref[...], (core_ref, mine_ref, theirs_ref), scratch,
    )
    extra, dg_ref[...] = norm_back(grad_query + grad_memory, x_ref[...], gain)
    out_ref[...] = grad_ref[...] + extra


def cross_back_kernel(place, grad_ref, x_ref, mem_ref, q_ref, k_ref, v_ref, o_ref, gain_ref, w_ref, sc_ref, sr_ref, core_ref, held_ref, kept_ref, out_ref, dmem_ref, mine_ref, theirs_ref, dg_ref, *scratch):
    gain = gain_ref[place : place + 1]
    normed = low(norm_parts(x_ref[...])[0] * gain)
    grad_query, dmem_ref[...] = attn_back_inside(
        low(grad_ref[...]), normed, low(mem_ref[...]), (q_ref, k_ref, v_ref, o_ref), w_ref,
        sc_ref[...] == sr_ref[...], (core_ref, mine_ref, theirs_ref), scratch,
    )
    extra, dg_ref[...] = norm_back(grad_query, x_ref[...], gain)
    out_ref[...] = grad_ref[...] + extra


def ids_along(first_ref, j, count, dim):
    shape = (1, count) if dim else (count, 1)
    return first_ref[j] + lax.broadcasted_iota(jnp.int32, shape, dim)


def head_fwd_kernel(top_ref, goal_ref, first_ref, *refs):
    blocks, (peak_ref, total_ref, pick_ref) = (refs[:4], refs[4:])
    peak_ref[...] = jnp.full(peak_ref.shape, NEGATIVE, jnp.float32)
    total_ref[...] = jnp.zeros(total_ref.shape, jnp.float32)
    pick_ref[...] = jnp.zeros(pick_ref.shape, jnp.float32)
    for j, block_ref in enumerate(blocks):
        logits = dot_right(top_ref[...], block_ref[...])
        hot = goal_ref[...] == ids_along(first_ref, j, block_ref.shape[0], 1)
        pick_ref[...] += jnp.sum(jnp.where(hot, logits, 0.0), axis=1, keepdims=True)
        peak = peak_ref[...]
        higher = jnp.maximum(peak, jnp.max(logits, axis=1, keepdims=True))
        total_ref[...] = total_ref[...] * jnp.exp(peak - higher) + jnp.sum(
            jnp.exp(logits - higher), axis=1, keepdims=True
        )
        peak_ref[...] = higher


def head_back_kernel(inverse, top_ref, goal_ref, log_ref, first_ref, *refs):
    blocks, (rows_ref, *grads_out, sum_ref) = (refs[:4], refs[4:])
    for j, block_ref in enumerate(blocks):
        logits = dot_right(top_ref[...], block_ref[...])
        hot = goal_ref[...] == ids_along(first_ref, j, block_ref.shape[0], 1)
        grads = low((jnp.exp(logits - log_ref[...]) - hot.astype(jnp.float32)) * inverse)
        rows = dot(grads, block_ref[...])
        sum_ref[...] = rows if j == 0 else sum_ref[...] + rows
        grads_out[j][...] = dot_left(grads, top_ref[...])
    rows_ref[...] = low(sum_ref[...])


def spread_kernel(picks, pieces, first_ref, ids_ref, *refs):
    count = len(picks)
    rows_refs, refs = (refs[:pieces], refs[pieces:])
    for j, base_ref, out_ref in zip(picks, refs[:count], refs[count:]):
        total = base_ref[...]
        start = 0
        for rows_ref in rows_refs:
            stop = start + rows_ref.shape[0]
            hot = ids_along(first_ref, j, base_ref.shape[0], 0) == ids_ref[:, start:stop]
            total = total + dot(hot.astype(jnp.bfloat16), rows_ref[...])
            start = stop
        out_ref[...] = total.astype(out_ref.dtype)


VMEM_BYTES = 48 * 2**20
FULL = jax.ShapeDtypeStruct((ROW, D), jnp.float32)
HALF = jax.ShapeDtypeStruct((ROW, D), jnp.bfloat16)
HIDDEN = jax.ShapeDtypeStruct((4, ROW, D), jnp.float32)


def halves_of(count):
    return jax.ShapeDtypeStruct((count, D // 2, D), jnp.bfloat16)


def gains_of(count):
    return jax.ShapeDtypeStruct((count, D), jnp.float32)


def spec_of(item):
    if item is None:
        return pl.BlockSpec(memory_space=pl.ANY)
    if isinstance(item, tuple):
        array, size, index = item
        shape, place = ((size,) + array.shape[1:], index)
    else:
        shape, place = (item.shape, 0)
    if len(shape) == 1 or shape == (1, 1):
        return pl.BlockSpec(memory_space=pltpu.SMEM)
    return pl.BlockSpec(shape, lambda i: (place,) + (0,) * (len(shape) - 1))


def run(kernel, outs, *operands, held=(), scratch=0, down=0, total=0, flops=0):
    arrays = [item[0] if isinstance(item, tuple) else item for item in operands]
    in_specs = [spec_of(item) for item in operands]
    shapes = [item[0] if isinstance(item, tuple) else item for item in outs]
    shapes = [jax.ShapeDtypeStruct(item.shape, item.dtype) for item in shapes]
    aliases = {}
    for array, place in held:
        aliases[len(arrays)] = place
        arrays.append(array)
        in_specs.append(spec_of(None))
    moved = sum(math.prod(x.shape) * x.dtype.itemsize for x in arrays + shapes)
    return pl.pallas_call(
        kernel,
        grid=(1,),
        out_shape=shapes,
        in_specs=in_specs,
        out_specs=[spec_of(item) for item in outs],
        input_output_aliases=aliases,
        scratch_shapes=[pltpu.VMEM((ROW, D), jnp.bfloat16)] * scratch
        + [pltpu.VMEM((4, D, D), jnp.bfloat16)] * down
        + [pltpu.VMEM((total, D), jnp.float32)] * (total > 0),
        compiler_params=pltpu.CompilerParams(vmem_limit_bytes=VMEM_BYTES),
        cost_estimate=pl.CostEstimate(flops=flops, bytes_accessed=moved, transcendentals=0),
    )(*arrays)


def spread(picks, kinds, ids, pieces, first_ids, bases):
    pieces = [piece.reshape(-1, D) for piece in pieces]
    return run(
        functools.partial(spread_kernel, picks, len(pieces)),
        [jax.ShapeDtypeStruct(base.shape, kind) for base, kind in zip(bases, kinds)],
        first_ids, ids[None], *pieces, *bases,
        flops=2 * len(picks) * ids.shape[0] * D * bases[0].shape[0],
    )


def pack_attn(project, output):
    width = output.shape[1]
    return jnp.stack([project[:, j * width : (j + 1) * width] for j in range(3)] + [output])


def pack_ffn(expand, reduce):
    rows, width = (expand.shape[0], reduce.shape[1])
    up = [expand[:, j * width : (j + 1) * width] for j in range(4)]
    return jnp.concatenate([jnp.stack(up), reduce.reshape(4, rows, width)])


def down_in_order(pack, count):
    parts = pack[4:8].reshape(4, count, -1, D).transpose(1, 0, 2, 3).reshape(4, D, D)
    return jnp.concatenate([pack[:4], parts])


def down_in_packs(grads, count):
    parts = grads[4:8].reshape(count, 4, -1, D).transpose(1, 0, 2, 3).reshape(4, D, D)
    return jnp.concatenate([grads[:4], parts])


def update_kernel(boosts, scalar_ref, dec_ref, enc_ref, *refs):
    factor = scalar_ref[0]
    packs = ((enc_ref, 8, 0), (dec_ref, 0, 8), (dec_ref, 4, None))
    rate = RATE_SCALE * math.sqrt(NPARAM / D) / CLIP

    def write(which, place, grad):
        weight, moment, average = (refs[3 * which + k][place] for k in range(3))
        outs = refs[12 + 4 * which : 16 + 4 * which]
        clipped = grad * factor
        moment = MOMENTUM * moment + clipped
        weight = weight - boosts[which] * rate * (clipped + MOMENTUM * moment)
        outs[0][place] = weight
        outs[1][place] = moment
        outs[2][place] = KEEP * average + (1.0 - KEEP) * weight
        outs[3][place] = low(weight)

    rows = enc_ref.shape[1]
    for layer, (pack_ref, attn, ffn) in enumerate(packs):
        for j in range(3):
            write(0, (layer, slice(None), slice(j * D, (j + 1) * D)), pack_ref[attn + j])
        write(1, (layer,), pack_ref[attn + 3])
        if ffn is None:
            continue
        for j in range(4):
            write(2, (layer, slice(None), slice(j * D, (j + 1) * D)), pack_ref[ffn + j])
            write(3, (layer, slice(j * rows, (j + 1) * rows)), pack_ref[ffn + 4 + j])


def shards(
    src_tokens,
    tgt_tokens,
    src_segments,
    tgt_lengths,
    mask_order,
    attn_project,
    attn_output,
    ffn_expand,
    ffn_reduce,
    norm_gains,
    length_table,
    embedding,
    momentum_attn_project,
    momentum_attn_output,
    momentum_ffn_expand,
    momentum_ffn_reduce,
    momentum_norm_gains,
    momentum_length_table,
    momentum_embedding,
    average_attn_project,
    average_attn_output,
    average_ffn_expand,
    average_ffn_reduce,
    average_norm_gains,
    average_length_table,
    average_embedding,
):
    masters = (
        attn_project,
        attn_output,
        ffn_expand,
        ffn_reduce,
        norm_gains,
        length_table,
        embedding,
    )
    moments = (
        momentum_attn_project,
        momentum_attn_output,
        momentum_ffn_expand,
        momentum_ffn_reduce,
        momentum_norm_gains,
        momentum_length_table,
        momentum_embedding,
    )
    averages = (
        average_attn_project,
        average_attn_output,
        average_ffn_expand,
        average_ffn_reduce,
        average_norm_gains,
        average_length_table,
        average_embedding,
    )
    count_z = lax.axis_size("z")
    here, side, core, half = (
        lax.axis_index("z"),
        lax.axis_index("y"),
        lax.axis_index("core"),
        lax.axis_index("vocab"),
    )
    rows_here = src_tokens.shape[0]
    count_dp = count_z * 4
    inverse = 1.0 / (SENTS * rows_here * count_dp)
    source, target, segments, lengths, order = (
        lax.dynamic_index_in_dim(array, half, 0, False)
        for array in (src_tokens, tgt_tokens, src_segments, tgt_lengths, mask_order)
    )
    shuffled = target[order]
    bounds = jnp.cumsum(lengths)
    tsegs = jnp.sum((order[:, None] >= bounds[None, :]).astype(jnp.int32), axis=1)
    position = sinusoid(ROW, D)
    dec_position = position[order]

    own_rows = low(embedding)
    shard = own_rows.shape[0]
    far_rows = swap(own_rows, "y")
    near = (own_rows, swap(own_rows, "core"))
    place = half * count_dp + here * 4
    firsts = [
        (place + at_side * 2 + at_core) * shard
        for at_side in (side, 1 - side)
        for at_core in (core, 1 - core)
    ]
    first_ids = jnp.stack(firsts).astype(jnp.int32)
    offsets = jnp.arange(shard, dtype=jnp.int32)

    few = ROW - MASKED + 16
    extra = jnp.where(jnp.arange(16) == 0, MASK_TOKEN, -1).astype(jnp.int32)
    group = count_z * 2
    numbers = jnp.concatenate([source, shuffled, extra])
    numbers = lax.all_to_all(
        jnp.broadcast_to(numbers[None], (group, 2 * ROW + 16)), ("z", "vocab"), 0, 0, tiled=True
    )
    numbers = turn(numbers.reshape(count_z, 2, -1)).reshape(group, -1)
    src_ids = numbers[:, :ROW].reshape(-1)
    goal_ids = numbers[:, ROW : ROW + MASKED].reshape(-1)
    dec_ids = numbers[:, ROW + MASKED :].reshape(-1)

    def look_up(tokens, blocks, starts):
        return sum(
            dot(low(tokens[:, None] == (offsets + start)[None, :]), rows)
            for rows, start in zip(blocks, starts)
        )

    near_src, near_dec = (look_up(ids, near, firsts[:2]) for ids in (src_ids, dec_ids))
    far_rows, near_src, near_dec = lax.optimization_barrier((far_rows, near_src, near_dec))
    away = (far_rows, swap(far_rows, "core"))
    src_rows, dec_rows = (
        low(found + look_up(ids, away, firsts[2:])).reshape(count_z, 2, -1, D)
        for ids, found in ((src_ids, near_src), (dec_ids, near_dec))
    )
    table_blocks = near + away

    blanks = jnp.zeros((1, length_table.shape[1], D - LCLS - 7), jnp.bfloat16)
    misc = jnp.concatenate([low(length_table).T[None], low(norm_gains).T[None], blanks], axis=2)
    enc_pack = gather_weight(
        jnp.concatenate(
            [
                low(pack_ffn(ffn_expand[0], ffn_reduce[0])),
                low(pack_attn(attn_project[0], attn_output[0])),
                misc,
            ]
        )
    )
    dec_pack = gather_weight(
        jnp.concatenate(
            [
                low(pack_attn(attn_project[1], attn_output[1])),
                low(pack_attn(attn_project[2], attn_output[2])),
                low(pack_ffn(ffn_expand[1], ffn_reduce[1])),
            ]
        )
    )
    plain = count_z != 4
    enc_ffn, dec_ffn = ((enc_pack, 8, 0), (dec_pack, 8, 1))
    if plain:
        enc_ffn = down_in_order(enc_pack, count_dp)
        dec_ffn = down_in_order(dec_pack[8:], count_dp)
    table = enc_pack[12, :, :LCLS].T
    gain = enc_pack[12, :, LCLS : LCLS + 7].T.astype(jnp.float32)
    scale_in = math.sqrt(D)
    class_ids = jnp.arange(LCLS, dtype=jnp.int32)
    sentence_ids = jnp.arange(SENTS, dtype=jnp.int32)

    src_part = add_vocab(src_rows)
    dec_part = scatter_line(dec_rows)
    src_part, dec_part = lax.optimization_barrier((src_part, dec_part))
    src_emb = scatter_line(src_part)
    dec_rows = add_vocab(dec_part)
    dec_emb = jnp.concatenate(
        [
            jnp.broadcast_to(dec_rows[ROW - MASKED][None], (MASKED, D)),
            dec_rows[: ROW - MASKED],
        ]
    )
    src_column, src_row = (segments[:, None], segments[None, :])
    tgt_column, tgt_row = (tsegs[:, None], tsegs[None, :])
    mega = 10**6
    x0 = scale_in * src_emb + position
    x1, x2, enc_top, *enc_attn_kept, enc_hidden = run(
        functools.partial(enc_fwd_kernel, plain), (FULL, FULL, FULL, HALF, HALF, HALF, HALF, HIDDEN),
        x0, gain, (enc_pack, 4, 2), enc_ffn, src_column, src_row, down=1, flops=1800 * mega,
    )
    y0 = scale_in * dec_emb + dec_position
    y1, *self_kept = run(
        dec_self_kernel, (FULL, HALF, HALF, HALF, HALF),
        y0, gain, (dec_pack, 4, 0), tgt_column, tgt_row, flops=700 * mega,
    )
    y2, y3, dec_top, *cross_kept, dec_hidden = run(
        functools.partial(dec_rest_kernel, plain), (FULL, FULL, FULL, HALF, HALF, HALF, HALF, HIDDEN),
        y1, enc_top, gain, (dec_pack, 4, 1), dec_ffn, tgt_column, src_row, down=1, flops=1800 * mega,
    )

    tops = gather_group(low(dec_top[:MASKED]))
    many = tops.shape[0]

    def rows_of(kind):
        return jax.ShapeDtypeStruct((shard, D), kind)

    column = jax.ShapeDtypeStruct((many, 1), jnp.float32)
    goal_column = goal_ids[:, None]
    peak, total, picked = run(
        head_fwd_kernel, (column, column, column),
        tops, goal_column, first_ids, *table_blocks, flops=8 * many * D * shard,
    )
    totals = jnp.stack([turn(part.reshape(count_z, 2, MASKED)) for part in (peak, total)])
    totals = butterfly(totals, join_totals, ("vocab", "z"))
    log_total = turn(totals[0] + jnp.log(totals[1])).reshape(-1)
    grad_rows, *grad_blocks = run(
        functools.partial(head_back_kernel, inverse),
        [jax.ShapeDtypeStruct((many, D), jnp.bfloat16)] + [rows_of(jnp.float32)] * 4,
        tops, goal_column, log_total[:, None], first_ids, *table_blocks,
        total=many, flops=24 * many * D * shard,
    )
    grad_rows = scatter_group(grad_rows.reshape(count_z, 2, MASKED, D))
    grad_top = jnp.concatenate([grad_rows, jnp.zeros((ROW - MASKED, D), jnp.float32)])

    member = (segments[None, :] == sentence_ids[:, None]).astype(jnp.float32)
    members = jnp.sum(member, axis=1, keepdims=True)
    pooled_low = low(jnp.dot(member, enc_top, precision=HIGHEST) / members)
    length_logits = jnp.einsum("sd,cd->sc", pooled_low, table, preferred_element_type=jnp.float32)
    length_total = jax.nn.logsumexp(length_logits, axis=1)
    class_hot = (lengths[:, None] - 1 == class_ids[None, :]).astype(jnp.float32)
    length_loss = length_total - jnp.sum(length_logits * class_hot, axis=1)
    loss_local = jnp.sum(log_total[:MASKED]) - jnp.sum(picked) + LENGTH_WEIGHT * jnp.sum(length_loss)
    grad_length = low(
        (jnp.exp(length_logits - length_total[:, None]) - class_hot) * (LENGTH_WEIGHT * inverse)
    )
    grad_table = jnp.einsum("sc,sd->dc", grad_length, pooled_low, preferred_element_type=jnp.float32)
    grad_pooled = jnp.einsum("sc,cd->sd", grad_length, table, preferred_element_type=jnp.float32)
    grad_enc = jnp.dot(member.T, grad_pooled / members, precision=HIGHEST)

    core_only = jnp.full((count_z,), core, jnp.int32)
    grad_stream, mine_dec, theirs_dec, dec_ffn_gain = run(
        functools.partial(ffn_back_kernel, 5, plain),
        (FULL, (halves_of(16), 8, 1), (halves_of(16), 8, 1), gains_of(2)),
        grad_top, y3, y2, dec_hidden, gain, dec_ffn, core_only, down=1, flops=2200 * mega,
    )
    grad_stream, memory_grad, mine_dec, theirs_dec, cross_gain = run(
        functools.partial(cross_back_kernel, 4),
        (FULL, FULL, (halves_of(16), 4, 1), (halves_of(16), 4, 1), gains_of(1)),
        grad_stream, y1, enc_top, *cross_kept, gain, (dec_pack, 4, 1), tgt_column, src_row,
        core_only, held=((mine_dec, 2), (theirs_dec, 3)), scratch=4, flops=1500 * mega,
    )
    dec_stream, mine_dec, theirs_dec, self_gain = run(
        functools.partial(self_back_kernel, 3),
        (FULL, (halves_of(16), 4, 0), (halves_of(16), 4, 0), gains_of(1)),
        grad_stream, y0, *self_kept, gain, (dec_pack, 4, 0), tgt_column, tgt_row,
        core_only, held=((mine_dec, 1), (theirs_dec, 2)), scratch=4, flops=1500 * mega,
    )
    sent = wide(low(scale_in * dec_stream))
    blank_sum = jnp.sum(sent[:MASKED], axis=0, keepdims=True)
    blank_high = low(blank_sum)
    blank_rest = low(blank_sum - wide(blank_high))
    sent = jnp.concatenate(
        [low(sent[MASKED:]), blank_high, blank_rest, jnp.zeros((14, D), jnp.bfloat16)]
    )
    again = jnp.where(jnp.arange(few) == ROW - MASKED + 1, MASK_TOKEN, 0).astype(jnp.int32)
    back_ids = jnp.where(again[None] > 0, again[None], dec_ids.reshape(-1, few)).reshape(-1)
    hold = lax.optimization_barrier
    if plain:
        whole = jnp.concatenate([mine_dec, theirs_dec], axis=1)
        whole = jnp.concatenate([whole[:8], down_in_packs(whole[8:], count_dp)])
        mine_dec, theirs_dec = jnp.split(whole, 2, axis=1)
    mine_dec, theirs_dec = swap_core(mine_dec, theirs_dec)
    dec_pair = pair_vocab(sent)
    grad_stream, mine_enc, theirs_enc, enc_ffn_gain = run(
        functools.partial(ffn_back_kernel, 1, plain),
        (FULL, (halves_of(13), 8, 0), (halves_of(13), 8, 0), gains_of(2)),
        grad_enc + memory_grad, x2, x1, enc_hidden, gain, enc_ffn, core_only,
        down=1, flops=2200 * mega,
    )
    grad_stream, dec_pair, mine_dec, theirs_dec = hold(
        (grad_stream, dec_pair, mine_dec, theirs_dec)
    )
    mine_dec, theirs_dec = add_vocab_parts(mine_dec, theirs_dec)
    dec_near = ring_first(dec_pair)
    enc_stream, mine_enc, theirs_enc, enc_attn_gain = run(
        functools.partial(self_back_kernel, 0),
        (FULL, (halves_of(13), 4, 2), (halves_of(13), 4, 2), gains_of(1)),
        grad_stream, x0, *enc_attn_kept, gain, (enc_pack, 4, 2), src_column, src_row,
        core_only, held=((mine_enc, 1), (theirs_enc, 2)), scratch=4, flops=1500 * mega,
    )
    grad_gain = jnp.concatenate(
        [enc_attn_gain, enc_ffn_gain, self_gain, cross_gain, dec_ffn_gain]
    ).T
    grad_misc = jnp.concatenate(
        [grad_table, grad_gain, jnp.zeros((D, D - LCLS - 7), jnp.float32)], axis=1
    )
    misc_parts = by_core(low(grad_misc)[None])
    if count_z != 4:
        misc_parts = jnp.split(low(grad_misc)[None], 2, axis=1)
    mine_enc, theirs_enc = (
        lax.dynamic_update_slice(part, misc_part, (12, 0, 0))
        for part, misc_part in zip((mine_enc, theirs_enc), misc_parts)
    )
    if plain:
        whole = jnp.concatenate([mine_enc, theirs_enc], axis=1)
        whole = jnp.concatenate([down_in_packs(whole[:8], count_dp), whole[8:]])
        mine_enc, theirs_enc = jnp.split(whole, 2, axis=1)
    mine_enc, theirs_enc = swap_core(mine_enc, theirs_enc)
    src_pair = pair_vocab(low(scale_in * enc_stream))
    dec_near, mine_enc, theirs_enc, src_pair, mine_dec, theirs_dec = hold(
        (dec_near, mine_enc, theirs_enc, src_pair, mine_dec, theirs_dec)
    )
    mine_enc, theirs_enc = add_side_parts(mine_enc, theirs_enc)
    dec_sent = ring_second(dec_pair, *dec_near)
    mine_enc, theirs_enc, dec_sent, src_pair, mine_dec, theirs_dec = hold(
        (mine_enc, theirs_enc, dec_sent, src_pair, mine_dec, theirs_dec)
    )
    theirs_dec = swap(theirs_dec, "vocab")
    theirs_enc = swap(theirs_enc, "y")
    src_near = ring_first(src_pair)
    grad_blocks = spread(
        (0, 1, 2, 3), [jnp.float32] * 4, back_ids, dec_sent, first_ids, grad_blocks
    )
    src_near, grad_blocks = hold((src_near, grad_blocks))
    src_sent = ring_second(src_pair, *src_near)
    mine_dec, theirs_dec, mine_enc, theirs_enc, src_sent, grad_blocks = hold(
        (mine_dec, theirs_dec, mine_enc, theirs_enc, src_sent, grad_blocks)
    )
    mine_dec, theirs_dec = add_side_parts(mine_dec, theirs_dec)
    theirs_dec = swap(theirs_dec, "y")
    enc_parts = line_parts(mine_enc, theirs_enc)
    enc_far = line_first(enc_parts)
    kinds = (jnp.float32, jnp.bfloat16)
    far_chip, far_sent = spread((2, 3), kinds, src_ids, src_sent, first_ids, grad_blocks[2:])
    far_back = swap(far_sent, "core")
    near_chip, near_sent = spread((0, 1), kinds, src_ids, src_sent, first_ids, grad_blocks[:2])
    near_back = swap(near_sent, "core")
    mine_dec, theirs_dec, far_back, near_back, enc_parts, enc_far = hold(
        (mine_dec, theirs_dec, far_back, near_back, enc_parts, enc_far)
    )
    far_chip = swap(low(far_chip + wide(far_back)), "y")
    dec_parts = line_parts(mine_dec, theirs_dec)
    dec_far = line_first(dec_parts)
    enc_line = line_second(enc_parts, enc_far)
    enc_line, dec_parts, dec_far, far_chip = hold((enc_line, dec_parts, dec_far, far_chip))
    dec_line = line_second(dec_parts, dec_far)
    sum_enc, enc_square = add_vocab_last(enc_line)
    dec_line, sum_enc, far_chip = hold((dec_line, sum_enc, far_chip))
    sum_dec, dec_square = join_vocab(dec_line)
    grad_embed = near_chip + wide(near_back) + wide(far_chip)
    layer_squares = dec_square + enc_square
    table_squares = jnp.sum(grad_embed * grad_embed)
    vocab_count = lax.axis_size("vocab")
    totals = butterfly(
        jnp.stack([layer_squares / vocab_count + table_squares, loss_local]),
        jnp.add,
        ("core", "vocab", "y", "z"),
    )
    squares, loss_sum = (totals[0], totals[1])
    grad_norm = jnp.sqrt(squares)
    factor = jnp.minimum(1.0, CLIP / grad_norm)
    rate = RATE_SCALE * math.sqrt(NPARAM / D) / CLIP
    layers = [
        item for k in range(4) for item in (masters[k], moments[k], averages[k])
    ]
    kinds = (jnp.float32, jnp.float32, jnp.float32, jnp.bfloat16)
    updated = run(
        functools.partial(update_kernel, RATE_FACTORS[:4]),
        [jax.ShapeDtypeStruct(masters[k].shape, kind) for k in range(4) for kind in kinds],
        factor[None], sum_dec, sum_enc, *layers,
    )
    results = [tuple(updated[4 * k : 4 * k + 4]) for k in range(4)]
    misc_sum = sum_enc[12]
    for k, grad in (
        (4, misc_sum[:, LCLS : LCLS + 7].T),
        (5, misc_sum[:, :LCLS].T),
        (6, grad_embed),
    ):
        clipped = grad * factor
        moment = MOMENTUM * moments[k] + clipped
        weight = masters[k] - RATE_FACTORS[k] * rate * (clipped + MOMENTUM * moment)
        average = KEEP * averages[k] + (1.0 - KEEP) * weight
        results.append((weight, moment, average, low(weight)))
    return (loss_sum, grad_norm) + tuple(result[k] for k in range(4) for result in results)


def solution(mesh):
    vocab = mesh.shape["vocab"]
    grid = Mesh(mesh.devices.reshape(-1, 2, 2, vocab), ("z", "y", "core", "vocab"))
    dp = ("z", "y", "core")
    return jax.shard_map(
        shards,
        mesh=grid,
        in_specs=(
            P(dp, None),
            P(dp, None),
            P(dp, None),
            P(dp, None),
            P(dp, None),
            P(None, dp, None),
            P(None, dp, None),
            P(None, dp, None),
            P(None, dp, None),
            P(None, dp),
            P(None, dp),
            P(("vocab",) + dp, None),
            P(None, dp, None),
            P(None, dp, None),
            P(None, dp, None),
            P(None, dp, None),
            P(None, dp),
            P(None, dp),
            P(("vocab",) + dp, None),
            P(None, dp, None),
            P(None, dp, None),
            P(None, dp, None),
            P(None, dp, None),
            P(None, dp),
            P(None, dp),
            P(("vocab",) + dp, None),
        ),
        out_specs=(
            P(),
            P(),
            P(None, dp, None),
            P(None, dp, None),
            P(None, dp, None),
            P(None, dp, None),
            P(None, dp),
            P(None, dp),
            P(("vocab",) + dp, None),
            P(None, dp, None),
            P(None, dp, None),
            P(None, dp, None),
            P(None, dp, None),
            P(None, dp),
            P(None, dp),
            P(("vocab",) + dp, None),
            P(None, dp, None),
            P(None, dp, None),
            P(None, dp, None),
            P(None, dp, None),
            P(None, dp),
            P(None, dp),
            P(("vocab",) + dp, None),
            P(None, dp, None),
            P(None, dp, None),
            P(None, dp, None),
            P(None, dp, None),
            P(None, dp),
            P(None, dp),
            P(("vocab",) + dp, None),
        ),
        check_vma=False,
    )
```

time: 854 us -> 588 us (0.69)
  matrix products: 159 us -> 23.9 us
  Pallas kernels: 0 us -> 133 us
  local copies, waits for them, and re-layouts: 164 us -> 66.7 us
  other arithmetic: 118 us -> 38.3 us
  starting transfers between devices: 141 us -> 79.9 us
  waiting for transfers between devices: 247 us -> 215 us
    pallas_call x0 -> x25, Pallas kernels: none -> 133 us  [the longest x20 121 us: run(): pl.pallas_call(kernel, grid=(1,), out_shape=shapes, in_specs=in_specs, ou...]
    dot_general x75 -> x0, matrix products: 92.5 us -> none  [the longest x31 49.1 us: dot_left(): jnp.einsum('rd,re->de', left, right, preferred_element_type=jnp.float32)]
    ppermute x30 -> x19, waiting for transfers between devices: 91.1 us -> 17.1 us  [swap(): return lax.ppermute(value, axis, SWAP)]
    ppermute x56 -> x32, starting transfers between devices: 111 us -> 48.1 us  [shift(): lax.ppermute(value, 'z', [(i, (i + by) % count) for i in range(count)])]
    dot_general x33 -> x8, matrix products: 53.1 us -> 19.9 us  [dot(): return jnp.dot(left, right, preferred_element_type=jnp.float32)]
    all_gather x0 -> x2, waiting for transfers between devices: none -> 28.2 us  [gather_weight(): return lax.all_gather(value, ('z', 'y', 'core'), axis=1, tiled=True)]
    convert_element_type x23 -> x2, local copies, waits for them, and re-layouts: 27.5 us -> 0.13 us  [low(): return value.astype(jnp.bfloat16)]
    reduce_sum x26 -> x3, other arithmetic: 25.9 us -> 3.69 us  [the longest x1 2.38 us: shards(): table_squares = jnp.sum(grad_embed * grad_embed)]
  transfers between devices with their start and end apart: 94 -> 62, of which waited for: 45 -> 43; matrix products, arithmetic and copies ran while one was open for 28% -> 10% of each run, Pallas kernels for 0% -> 10%
where the time goes in v2:
time: 588 us; the launch traced here: 579 us
  waiting for transfers between devices  215 us (37%)
  Pallas kernels  133 us (23%)
  starting transfers between devices  79.9 us (14%)
  local copies, waits for them, and re-layouts  66.7 us (11%)
  other arithmetic  38.3 us (7%)
  matrix products  23.9 us (4%)
  between operations  22 us (4%)
    ppermute x32, waiting for transfers between devices, shift(): lax.ppermute(value, 'z', [(i, (i + by) % count) for i in range(count)])  142 us
    pallas_call x20, Pallas kernels, run(): pl.pallas_call(kernel, grid=(1,), out_shape=shapes, in_specs=in_specs, ou...  121 us
    unnamed x272, local copies, waits for them, and re-layouts  50.8 us
    ppermute x32, starting transfers between devices, shift(): lax.ppermute(value, 'z', [(i, (i + by) % count) for i in range(count)])  48.1 us
    all_gather x2, waiting for transfers between devices, gather_weight(): return lax.all_gather(value, ('z', 'y', 'core'), axis=1, tiled=True)  28.2 us
    ppermute x8, waiting for transfers between devices, butterfly(): value = join(value, lax.ppermute(value, axis, pairs))  20.7 us
    dot_general x8, matrix products, dot(): return jnp.dot(left, right, preferred_element_type=jnp.float32)  19.9 us
    ppermute x19, starting transfers between devices, swap(): return lax.ppermute(value, axis, SWAP)  18.4 us
  transfers between devices with their start and end apart: 62, of which 43 were waited for; matrix products, arithmetic and copies ran while one was open for 10% of the time, Pallas kernels for 10%

profile of v2, /device:TPU:0, one launch (start us, length us, event | category | flops | bytes accessed | tf_op | source)
XLA Modules:
  0.0 579.2 jit_solution(11370524901268722093)
XLA Ops:
  14.9 2.6 collective-permute-start
  20.2 5.8 %all-to-all-start = ((s32[8,1,528]{2,1,0:T(1,128)}), s32[8,1,528]{2,1,0:T(1,128)S(1)}, u32[]{:S(2)}, u32[]{:S(2)}) async-start(s32[8,1,528]{2,1,0:T(1,128)} %broadcast_in_dim.68), calls=%async_computation | async-start | bytes 40960 | tf_op jit(solution)/shard_map/all_to_all | solution.py:805
  26.1 6.8 %all-to-all-done = s32[8,1,528]{2,1,0:T(1,128)S(1)} async-done(((s32[8,1,528]{2,1,0:T(1,128)}), s32[8,1,528]{2,1,0:T(1,128)S(1)}, u32[]{:S(2)}, u32[]{:S(2)}) %all-to-all-start) | async-done | bytes 16928 | tf_op jit(solution)/shard_map/all_to_all | solution.py:805
  35.2 2.5 fusion.6
  37.6 3.4 fusion.24
  41.0 4.1 fusion.30
  45.4 2.4 fusion.2
  52.4 3.9 collective-permute-start.4
  56.3 2.4 fusion
  62.9 6.3 %collective-permute-done.4 = bf16[1,176,512]{2,1,0:T(8,128)(2,1)S(1)} collective-permute-done((bf16[1,176,512]{2,1,0:T(8,128)(2,1)S(1)}, bf16[1,176,512]{2,1,0:T(8,128)(2,1)S(1)}, u32[]{:S(2)}, u32[]{:S(2)}) %collective-permute-start.4) | collective-permute-done | bytes 180256 | tf_op jit(solution)/shard_map/ppermute | solution.py:49
  69.1 4.3 collective-permute-done.6
  82.1 13.3 %collective-permute-done.7 = bf16[2,176,512]{2,1,0:T(8,128)(2,1)} collective-permute-done((bf16[2,176,512]{2,1,0:T(8,128)(2,1)}, bf16[2,176,512]{2,1,0:T(8,128)(2,1)}, u32[]{:S(2)}, u32[]{:S(2)}) %collective-permute-start.7) | collective-permute-done | bytes 360480 | tf_op jit(solution)/shard_map/ppermute | solution.py:49
  95.4 6.9 %collective-permute-done.5 = bf16[2,176,512]{2,1,0:T(8,128)(2,1)} collective-permute-done((bf16[2,176,512]{2,1,0:T(8,128)(2,1)}, bf16[2,176,512]{2,1,0:T(8,128)(2,1)}, u32[]{:S(2)}, u32[]{:S(2)}) %collective-permute-start.5) | collective-permute-done | bytes 360480 | tf_op jit(solution)/shard_map/ppermute | solution.py:49
  105.2 2.4 collective-permute-start.8
  111.5 4.0 collective-permute-done.10
  116.3 2.5 collective-permute-start.11
  122.0 11.2 %collective-permute-done.11 = bf16[256,512]{1,0:T(8,128)(2,1)} collective-permute-done((bf16[256,512]{1,0:T(8,128)(2,1)}, bf16[256,512]{1,0:T(8,128)(2,1)}, u32[]{:S(2)}, u32[]{:S(2)}) %collective-permute-start.11) | collective-permute-done | bytes 262176 | tf_op jit(solution)/shard_map/ppermute | solution.py:49
  133.2 9.8 %collective-permute-done.9 = bf16[256,512]{1,0:T(8,128)(2,1)S(1)} collective-permute-done((bf16[256,512]{1,0:T(8,128)(2,1)}, bf16[256,512]{1,0:T(8,128)(2,1)S(1)}, u32[]{:S(2)}, u32[]{:S(2)}) %collective-permute-start.9) | collective-permute-done | bytes 262176 | tf_op jit(solution)/shard_map/ppermute | solution.py:49
  147.4 7.8 %shard_map.481 = (f32[256,512]{1,0:T(8,128)S(1)}, f32[256,512]{1,0:T(8,128)S(1)}, f32[256,512]{1,0:T(8,128)S(1)}, bf16[256,512]{1,0:T(8,128)(2,1)S(1)}, bf16[256...) custom-call(f32[256,512]{1,0:T(8,128)S(1)} %get-tuple-element.538.x_, ...), custom_call_target="tpu_custom_call" | custom-call | flops 1800000000 | bytes 18890752 | tf_op jit(solution)/shard_map/pallas_call | solution.py:639
  161.0 28.1 %all-gather.5.cloned.1.call-done.w_ref.wa_ref.wf_ref = bf16[16,512,512]{2,1,0:T(8,128)(2,1)} async-done(((bf16[16,32,512]{2,1,0:T(8,128)(2,1)}), bf16[16,512,512]{2,1,0:T(8,128)(2,1)}) %all-gather.5.cloned.1.call-update) | async-done | bytes 8388624 | tf_op jit(solution)/shard_map/all_gather | solution.py:99
  189.1 3.8 shard_map.482
  195.8 7.2 %shard_map.483 = (f32[256,512]{1,0:T(8,128)S(1)}, f32[256,512]{1,0:T(8,128)S(1)}, f32[256,512]{1,0:T(8,128)S(1)}, bf16[256,512]{1,0:T(8,128)(2,1)S(1)}, bf16[256...) custom-call(f32[256,512]{1,0:T(8,128)S(1)} %get-tuple-element.198.y1, ...), custom_call_target="tpu_custom_call" | custom-call | flops 1800000000 | bytes 22560768 | tf_op jit(solution)/shard_map/pallas_call | solution.py:639
  210.2 3.5 collective-permute-done.13
  218.5 3.2 collective-permute-done.16
  222.5 4.3 collective-permute-start.17
  229.6 5.5 collective-permute-done.15
  239.5 9.5 %shard_map.484 = (f32[768,1]{1,0:T(8,128)S(1)}, f32[768,1]{1,0:T(8,128)S(1)}, f32[768,1]{1,0:T(8,128)S(1)}) custom-call(bf16[768,512]{1,0:T(8,128)(2,1)S(1)} %constant_dynamic-update-slice_fusion.23.top_ref, s32[768,1]{1,0:T(8,128)S(1)} %copy-done.36, s32[4]{0:T(128)S(1)} %pad_add_fusion.1.first_ref, bf16[1000,512]{1,0:T(8,128)(2,1)S(1)} %convert_element_type.252.refs_0_, ...), custom_call_target="tpu_custom_call" | custom-call | flops 3145728000 | bytes 4894736 | tf_op jit(solution)/shard_map/pallas_call | solution.py:639
  257.7 3.6 collective-permute-done.19
  261.5 4.5 collective-permute-done.20
  272.7 14.5 %shard_map.485 = (bf16[768,512]{1,0:T(8,128)(2,1)S(1)}, f32[1000,512]{1,0:T(8,128)}, f32[1000,512]{1,0:T(8,128)}, f32[1000,512]{1,0:T(8,128)}, f32[1000,512]{1,0:T(8,128)}) custom-call(bf16[768,512]{1,0:T(8,128)(2,1)S(1)} %copy-done.76, s32[768,1]{1,0:T(8,128)S(1)} %copy-done.37, f32[768,1]{1,0:T(8,128)S(1)} %copy-done.38, s32[4]{0:T(128)S(1)} %pad_add_fusion.1.first_ref, ...), custom_call_target="tpu_custom_call" | custom-call | flops 9437184000 | bytes 13867024 | tf_op jit(solution)/shard_map/pallas_call | solution.py:639
  288.7 6.3 %collective-permute-done.21 = bf16[4,96,512]{2,1,0:T(8,128)(2,1)S(1)} collective-permute-done((bf16[4,96,512]{2,1,0:T(8,128)(2,1)S(1)}, bf16[4,96,512]{2,1,0:T(8,128)(2,1)S(1)}, u32[]{:S(2)}, u32[]{:S(2)}) %collective-permute-start.21) | collective-permute-done | bytes 393248 | tf_op jit(solution)/shard_map/ppermute | solution.py:44
  297.2 2.5 collective-permute-done.22
  301.4 3.7 collective-permute-start.23
  305.1 2.5 collective-permute-done.25
  307.8 8.1 %shard_map.486 = (f32[256,512]{1,0:T(8,128)S(1)}, bf16[16,256,512]{2,1,0:T(8,128)(2,1)}, bf16[16,256,512]{2,1,0:T(8,128)(2,1)}, f32[2,512]{1,0:T(2,128)S(1)}) custom-call(f32[256,512]{1,0:T(8,128)S(1)} %concatenate.105.grad_ref, f32[256,512]{1,0:T(8,128)S(1)} %copy-done.28, f32[256,512]{1,0:T(8,128)S(1)} %copy-done.26, f32[4,256,512]{2,1,0:T(8,128)S(1)} %copy-done.12, ...), custom_call_target="tpu_custom_call" | custom-call | flops 2200000000 | bytes 20989968 | tf_op jit(solution)/shard_map/pallas_call | solution.py:639
  316.0 8.4 %shard_map.487 = (f32[256,512]{1,0:T(8,128)S(1)}, f32[256,512]{1,0:T(8,128)S(1)}, bf16[16,256,512]{2,1,0:T(8,128)(2,1)}, bf16[16,256,512]{2,1,0:T(8,128)(2,1)}, f32[1,512]{1,0:T(1,128)S(1)}) custom-call(f32[256,512]{1,0:T(8,128)S(1)} %get-tuple-element.206.grad_ref, ...), custom_call_target="tpu_custom_call", output_to_operand_aliasing={{2}: (12, {}), {3}: (13, {})} | custom-call | flops 1500000000 | bytes 28854288 | tf_op jit(solution)/shard_map/pallas_call | solution.py:639
  324.4 8.8 %shard_map.489 = (f32[256,512]{1,0:T(8,128)S(1)}, bf16[16,256,512]{2,1,0:T(8,128)(2,1)}, bf16[16,256,512]{2,1,0:T(8,128)(2,1)}, f32[1,512]{1,0:T(1,128)S(1)}) custom-call(f32[256,512]{1,0:T(8,128)S(1)} %get-tuple-element.218.grad_ref, f32[256,512]{1,0:T(8,128)S(1)} %fusion.44.x_ref, ...), custom_call_target="tpu_custom_call", output_to_operand_aliasing={{1}: (11, {}), {2}: (12, {})} | custom-call | flops 1500000000 | bytes 27805712 | tf_op jit(solution)/shard_map/pallas_call | solution.py:639
  342.8 8.0 %shard_map.488 = (f32[256,512]{1,0:T(8,128)S(1)}, bf16[13,256,512]{2,1,0:T(8,128)(2,1)}, bf16[13,256,512]{2,1,0:T(8,128)(2,1)}, f32[2,512]{1,0:T(2,128)S(1)}) custom-call(f32[256,512]{1,0:T(8,128)S(1)} %convolution_add_fusion.grad_ref, f32[256,512]{1,0:T(8,128)S(1)} %copy-done.33, f32[256,512]{1,0:T(8,128)S(1)} %copy-done.31, f32[4,256,512]{2,1,0:T(8,128)S(1)} %copy-done.10, ...), custom_call_target="tpu_custom_call" | custom-call | flops 2200000000 | bytes 17844240 | tf_op jit(solution)/shard_map/pallas_call | solution.py:639
  353.1 8.2 %shard_map.490 = (f32[256,512]{1,0:T(8,128)S(1)}, bf16[13,256,512]{2,1,0:T(8,128)(2,1)S(1)}, bf16[13,256,512]{2,1,0:T(8,128)(2,1)}, f32[1,512]{1,0:T(1,128)S(1)}) custom-call(f32[256,512]{1,0:T(8,128)S(1)} %get-tuple-element.229.grad_ref, f32[256,512]{1,0:T(8,128)S(1)} %get-tuple-element.538.x_ref, ...), custom_call_target="tpu_custom_call", output_to_operand_aliasing={{1}: (11, {}), {2}: (12, {})} | custom-call | flops 1500000000 | bytes 23087120 | tf_op jit(solution)/shard_map/pallas_call | solution.py:639
  365.2 3.9 collective-permute-start.29
  369.1 4.9 shard_map.491
  375.0 2.9 collective-permute-done.29
  378.0 7.5 %collective-permute-done.28 = bf16[2,176,512]{2,1,0:T(8,128)(2,1)S(1)} collective-permute-done((bf16[2,176,512]{2,1,0:T(8,128)(2,1)S(1)}, bf16[2,176,512]{2,1,0:T(8,128)(2,1)S(1)}, u32[]{:S(2)}, u32[]{:S(2)}) %collective-permute-start.28) | collective-permute-done | bytes 360480 | tf_op jit(solution)/shard_map/ppermute | solution.py:49
  388.3 4.4 shard_map.492
  392.7 3.4 collective-permute-done.33
  406.4 13.7 %shard_map.493 = (f32[1000,512]{1,0:T(8,128)S(1)}, f32[1000,512]{1,0:T(8,128)S(1)}, f32[1000,512]{1,0:T(8,128)}, f32[1000,512]{1,0:T(8,128)}) custom-call(s32[4]{0:T(128)S(1)} %pad_add_fusion.1.first_ref, s32[1,1408]{1,0:T(1,128)S(1)} %broadcast_in_dim_reshape.10.ids_ref, bf16[352,512]{1,0:T(8,128)(2,1)S(1)} %bitcast.358, bf16[352,512]{1,0:T(8,128)(2,1)S(1)} %bitcast.364, ...), custom_call_target="tpu_custom_call" | custom-call | flops 5767168000 | bytes 17831440 | tf_op jit(solution)/shard_map/pallas_call | solution.py:639
  421.5 3.8 collective-permute-done.36
  427.6 6.2 %collective-permute-done.39 = bf16[1,256,512]{2,1,0:T(8,128)(2,1)S(1)} collective-permute-done((bf16[1,256,512]{2,1,0:T(8,128)(2,1)S(1)}, bf16[1,256,512]{2,1,0:T(8,128)(2,1)S(1)}, u32[]{:S(2)}, u32[]{:S(2)}) %collective-permute-start.39) | collective-permute-done | bytes 262176 | tf_op jit(solution)/shard_map/ppermute | solution.py:49
  433.8 5.5 collective-permute-done.38
  439.3 3.6 collective-permute-done.34.refs_1_.refs_3_
  445.5 6.6 %shard_map.495 = (f32[1000,512]{1,0:T(8,128)S(1)}, bf16[1000,512]{1,0:T(8,128)(2,1)S(1)}) custom-call(s32[4]{0:T(128)S(1)} %pad_add_fusion.1.first_ref, s32[1,2048]{1,0:T(1,128)S(1)} %bitcast.371, bf16[512,512]{1,0:T(8,128)(2,1)S(1)} %bitcast.356, bf16[512,512]{1,0:T(8,128)(2,1)S(1)} %bitcast.361, bf16[256,512]{1,0:T(8,128)(2,1)S(1)} %bitcast.375, ...), custom_call_target="tpu_custom_call" | custom-call | flops 4194304000 | bytes 9273360 | tf_op jit(solution)/shard_map/pallas_call | solution.py:639
  452.2 7.6 %shard_map.496 = (f32[1000,512]{1,0:T(8,128)S(1)}, bf16[1000,512]{1,0:T(8,128)(2,1)}) custom-call(s32[4]{0:T(128)S(1)} %pad_add_fusion.1.first_ref, s32[1,2048]{1,0:T(1,128)S(1)} %bitcast.372, bf16[512,512]{1,0:T(8,128)(2,1)S(1)} %bitcast.357, bf16[512,512]{1,0:T(8,128)(2,1)S(1)} %bitcast.362, bf16[256,512]{1,0:T(8,128)(2,1)S(1)} %bitcast.376, ...), custom_call_target="tpu_custom_call" | custom-call | flops 4194304000 | bytes 9273360 | tf_op jit(solution)/shard_map/pallas_call | solution.py:639
  461.1 3.2 collective-permute-start.43
  464.2 5.7 collective-permute-done.43.above_ref
  469.9 6.7 %collective-permute-done.44.below_ref = bf16[13,32,256]{2,1,0:T(8,128)(2,1)S(1)} collective-permute-done((bf16[13,32,256]{2,1,0:T(8,128)(2,1)S(1)}, bf16[13,32,256]{2,1,0:T(8,128)(2,1)S(1)}, u32[]{:S(2)}, u32[]{:S(2)}) %collective-permute-start.44) | collective-permute-done | bytes 213024 | tf_op jit(solution)/shard_map/ppermute | solution.py:49
  482.7 3.6 collective-permute-start.47
  486.3 15.6 %collective-permute-done.45.two_ref = bf16[13,32,512]{2,1,0:T(8,128)(2,1)S(1)} collective-permute-done((bf16[13,32,512]{2,1,0:T(8,128)(2,1)S(1)}, bf16[13,32,512]{2,1,0:T(8,128)(2,1)S(1)}, u32[]{:S(2)}, u32[]{:S(2)}) %collective-permute-start.45) | collective-permute-done | bytes 426016 | tf_op jit(solution)/shard_map/ppermute | solution.py:49
  514.8 6.9 %collective-permute-done.50.two_ref = bf16[8,32,512]{2,1,0:T(8,128)(2,1)} collective-permute-done((bf16[8,32,512]{2,1,0:T(8,128)(2,1)}, bf16[8,32,512]{2,1,0:T(8,128)(2,1)}, u32[]{:S(2)}, u32[]{:S(2)}) %collective-permute-start.50) | collective-permute-done | bytes 262176 | tf_op jit(solution)/shard_map/ppermute | solution.py:49
  528.0 3.4 collective-permute-done.53.theirs_ref
  537.0 3.0 collective-permute-done.55
  540.6 3.0 collective-permute-done.56
  547.1 2.9 collective-permute-start.58
  556.2 5.7 fusion.87
  565.9 5.0 shard_map.505
  (533 shorter events, 172.2 us)
Async XLA Ops:
  7.2 38.1 %copy-start = (s32[2,256]{1,0:T(2,128)S(1)}, s32[2,256]{1,0:T(2,128)}, u32[]{:S(2)}) copy-start(s32[2,256]{1,0:T(2,128)} %param.28) | copy-start | bytes 6148
  7.2 139.1 %all-gather.3.cloned.1.call-start = ((), (), s32[]{:S(2)}) async-start(), calls=%async_computation.1 | async-start | bytes 7241728 | tf_op jit(solution)/shard_map/all_gather | solution.py:99
  13.3 175.8 %all-gather.5.cloned.1.call-start = ((), (), s32[]{:S(2)}) async-start(), calls=%async_computation.2 | async-start | bytes 8912896 | tf_op jit(solution)/shard_map/all_gather | solution.py:99
  14.4 23.2 %collective-permute-start.1 = (bf16[1000,512]{1,0:T(8,128)(2,1)S(1)}, bf16[1000,512]{1,0:T(8,128)(2,1)S(1)}, u32[]{:S(2)}, u32[]{:S(2)}) collective-permute-start(bf16[1000,512]{1,0:T(8,128)(2,1)S(1)} %convert_element_type.252.refs_0_), channel_id=1, source_target_pairs={{0,2},{2,0},{1,3},{3,1},{4,6},{6,4},{5,7},{7,5},{8,10},{10,8},{9,1... | collective-permute-start | bytes 3072008 | tf_op jit(solution)/shard_map/ppermute | solution.py:44
  14.9 30.4 %collective-permute-start = (bf16[1000,512]{1,0:T(8,128)(2,1)S(1)}, bf16[1000,512]{1,0:T(8,128)(2,1)S(1)}, u32[]{:S(2)}, u32[]{:S(2)}) collective-permute-start(bf16[1000,512]{1,0:T(8,128)(2,1)S(1)} %convert_element_type.252.refs_0_), channel_id=1, source_target_pairs={{0,4},{4,0},{1,5},{5,1},{2,6},{6,2},{3,7},{7,3},{8,12},{12,8},{9,1... | collective-permute-start | bytes 3072008 | tf_op jit(solution)/shard_map/ppermute | solution.py:44
  20.2 12.7 %all-to-all-start = ((s32[8,1,528]{2,1,0:T(1,128)}), s32[8,1,528]{2,1,0:T(1,128)S(1)}, u32[]{:S(2)}, u32[]{:S(2)}) async-start(s32[8,1,528]{2,1,0:T(1,128)} %broadcast_in_dim.68), calls=%async_computation | async-start | bytes 40960 | tf_op jit(solution)/shard_map/all_to_all | solution.py:805
  45.3 2.6 collective-permute-start.2
  52.4 16.7 %collective-permute-start.4 = (bf16[1,176,512]{2,1,0:T(8,128)(2,1)S(1)}, bf16[1,176,512]{2,1,0:T(8,128)(2,1)S(1)}, u32[]{:S(2)}, u32[]{:S(2)}) collective-permute-start(bf16[1,176,512]{2,1,0:T(8,128)(2,1)S(1)} %get-tuple-element.523), channel_id=1, source_target_pairs={{0,24},{8,0},{16,8},{24,16},{1,25},{9,1},{17,9},{25,17},{2,26},{10... | collective-permute-start | bytes 540680 | tf_op jit(solution)/shard_map/ppermute | solution.py:49
  56.3 17.2 %collective-permute-start.6 = (bf16[1,176,512]{2,1,0:T(8,128)(2,1)S(1)}, bf16[1,176,512]{2,1,0:T(8,128)(2,1)S(1)}, u32[]{:S(2)}, u32[]{:S(2)}) collective-permute-start(bf16[1,176,512]{2,1,0:T(8,128)(2,1)S(1)} %get-tuple-element.524), channel_id=1, source_target_pairs={{0,8},{8,16},{16,24},{24,0},{1,9},{9,17},{17,25},{25,1},{2,10},{10... | collective-permute-start | bytes 540680 | tf_op jit(solution)/shard_map/ppermute | solution.py:49
  61.4 42.1 %collective-permute-start.3 = (bf16[4,256,512]{2,1,0:T(8,128)(2,1)}, bf16[4,256,512]{2,1,0:T(8,128)(2,1)}, u32[]{:S(2)}, u32[]{:S(2)}) collective-permute-start(bf16[4,256,512]{2,1,0:T(8,128)(2,1)} %slice_bitcast_fusion), channel_id=1, source_target_pairs={{0,1},{1,0},{2,3},{3,2},{4,5},{5,4},{6,7},{7,6},{8,9},{9,8},{10,11... | collective-permute-start | bytes 3145736 | tf_op jit(solution)/shard_map/ppermute | solution.py:44
  74.3 21.1 %collective-permute-start.7 = (bf16[2,176,512]{2,1,0:T(8,128)(2,1)}, bf16[2,176,512]{2,1,0:T(8,128)(2,1)}, u32[]{:S(2)}, u32[]{:S(2)}) collective-permute-start(bf16[2,176,512]{2,1,0:T(8,128)(2,1)} %pad_maximum_fusion.3), channel_id=1, source_target_pairs={{0,8},{8,16},{16,24},{24,0},{1,9},{9,17},{17,25},{25,1},{2,10},{10... | collective-permute-start | bytes 1081352 | tf_op jit(solution)/shard_map/ppermute | solution.py:49
  76.7 25.6 %collective-permute-start.5 = (bf16[2,176,512]{2,1,0:T(8,128)(2,1)}, bf16[2,176,512]{2,1,0:T(8,128)(2,1)}, u32[]{:S(2)}, u32[]{:S(2)}) collective-permute-start(bf16[2,176,512]{2,1,0:T(8,128)(2,1)} %pad_maximum_fusion.2), channel_id=1, source_target_pairs={{0,24},{8,0},{16,8},{24,16},{1,25},{9,1},{17,9},{25,17},{2,26},{10... | collective-permute-start | bytes 1081352 | tf_op jit(solution)/shard_map/ppermute | solution.py:49
  105.2 6.3 %collective-permute-start.8 = (bf16[128,512]{1,0:T(8,128)(2,1)S(1)}, bf16[128,512]{1,0:T(8,128)(2,1)S(1)}, u32[]{:S(2)}, u32[]{:S(2)}) collective-permute-start(bf16[128,512]{1,0:T(8,128)(2,1)S(1)} %get-tuple-element.529), channel_id=1, source_target_pairs={{0,24},{8,0},{16,8},{24,16},{1,25},{9,1},{17,9},{25,17},{2,26},{10... | collective-permute-start | bytes 393224 | tf_op jit(solution)/shard_map/ppermute | solution.py:49
  107.7 7.9 %collective-permute-start.10 = (bf16[128,512]{1,0:T(8,128)(2,1)S(1)}, bf16[128,512]{1,0:T(8,128)(2,1)S(1)}, u32[]{:S(2)}, u32[]{:S(2)}) collective-permute-start(bf16[128,512]{1,0:T(8,128)(2,1)S(1)} %get-tuple-element.530), channel_id=1, source_target_pairs={{0,8},{8,16},{16,24},{24,0},{1,9},{9,17},{17,25},{25,1},{2,10},{10... | collective-permute-start | bytes 393224 | tf_op jit(solution)/shard_map/ppermute | solution.py:49
  107.7 13.5 %collective-permute-start.12 = (bf16[176,512]{1,0:T(8,128)(2,1)S(1)}, bf16[176,512]{1,0:T(8,128)(2,1)S(1)}, u32[]{:S(2)}, u32[]{:S(2)}) collective-permute-start(bf16[176,512]{1,0:T(8,128)(2,1)S(1)} %fusion.57), channel_id=1, source_target_pairs={{0,1},{1,0},{2,3},{3,2},{4,5},{5,4},{6,7},{7,6},{8,9},{9,8},{10,11... | collective-permute-start | bytes 540680 | tf_op jit(solution)/shard_map/ppermute | solution.py:44
  116.3 16.9 %collective-permute-start.11 = (bf16[256,512]{1,0:T(8,128)(2,1)}, bf16[256,512]{1,0:T(8,128)(2,1)}, u32[]{:S(2)}, u32[]{:S(2)}) collective-permute-start(bf16[256,512]{1,0:T(8,128)(2,1)} %pad_maximum_fusion.6), channel_id=1, source_target_pairs={{0,8},{8,16},{16,24},{24,0},{1,9},{9,17},{17,25},{25,1},{2,10},{10... | collective-permute-start | bytes 786440 | tf_op jit(solution)/shard_map/ppermute | solution.py:49
  119.5 23.5 %collective-permute-start.9 = (bf16[256,512]{1,0:T(8,128)(2,1)}, bf16[256,512]{1,0:T(8,128)(2,1)S(1)}, u32[]{:S(2)}, u32[]{:S(2)}) collective-permute-start(bf16[256,512]{1,0:T(8,128)(2,1)} %pad_maximum_fusion.5), channel_id=1, source_target_pairs={{0,24},{8,0},{16,8},{24,16},{1,25},{9,1},{17,9},{25,17},{2,26},{10... | collective-permute-start | bytes 786440 | tf_op jit(solution)/shard_map/ppermute | solution.py:49
  208.7 5.0 collective-permute-start.13
  214.4 7.2 %collective-permute-start.16 = (bf16[2,96,512]{2,1,0:T(8,128)(2,1)}, bf16[2,96,512]{2,1,0:T(8,128)(2,1)}, u32[]{:S(2)}, u32[]{:S(2)}) collective-permute-start(bf16[2,96,512]{2,1,0:T(8,128)(2,1)} %pad_maximum_fusion.7), channel_id=1, source_target_pairs={{0,24},{8,0},{16,8},{24,16},{1,25},{9,1},{17,9},{25,17},{2,26},{10... | collective-permute-start | bytes 589832 | tf_op jit(solution)/shard_map/ppermute | solution.py:49
  215.9 11.4 %collective-permute-start.14 = (bf16[2,96,512]{2,1,0:T(8,128)(2,1)}, bf16[2,96,512]{2,1,0:T(8,128)(2,1)}, u32[]{:S(2)}, u32[]{:S(2)}) collective-permute-start(bf16[2,96,512]{2,1,0:T(8,128)(2,1)} %pad_maximum_fusion.7), channel_id=1, source_target_pairs={{0,8},{8,16},{16,24},{24,0},{1,9},{9,17},{17,25},{25,1},{2,10},{10... | collective-permute-start | bytes 589832 | tf_op jit(solution)/shard_map/ppermute | solution.py:49
  222.5 12.6 %collective-permute-start.17 = (bf16[1,96,512]{2,1,0:T(8,128)(2,1)S(1)}, bf16[1,96,512]{2,1,0:T(8,128)(2,1)S(1)}, u32[]{:S(2)}, u32[]{:S(2)}) collective-permute-start(bf16[1,96,512]{2,1,0:T(8,128)(2,1)S(1)} %slice.471), channel_id=1, source_target_pairs={{0,24},{8,0},{16,8},{24,16},{1,25},{9,1},{17,9},{25,17},{2,26},{10... | collective-permute-start | bytes 294920 | tf_op jit(solution)/shard_map/ppermute | solution.py:49
  228.2 6.9 %collective-permute-start.15 = (bf16[1,96,512]{2,1,0:T(8,128)(2,1)S(1)}, bf16[1,96,512]{2,1,0:T(8,128)(2,1)S(1)}, u32[]{:S(2)}, u32[]{:S(2)}) collective-permute-start(bf16[1,96,512]{2,1,0:T(8,128)(2,1)S(1)} %slice.470), channel_id=1, source_target_pairs={{0,8},{8,16},{16,24},{24,0},{1,9},{9,17},{17,25},{25,1},{2,10},{10... | collective-permute-start | bytes 294920 | tf_op jit(solution)/shard_map/ppermute | solution.py:49
  253.9 3.7 collective-permute-start.18
  257.6 3.7 collective-permute-start.19
  261.4 4.6 collective-permute-start.20
  287.2 7.8 %collective-permute-start.21 = (bf16[4,96,512]{2,1,0:T(8,128)(2,1)S(1)}, bf16[4,96,512]{2,1,0:T(8,128)(2,1)S(1)}, u32[]{:S(2)}, u32[]{:S(2)}) collective-permute-start(bf16[4,96,512]{2,1,0:T(8,128)(2,1)S(1)} %slice_bitcast_fusion.2), channel_id=1, source_target_pairs={{0,1},{1,0},{2,3},{3,2},{4,5},{5,4},{6,7},{7,6},{8,9},{9,8},{10,11... | collective-permute-start | bytes 1179656 | tf_op jit(solution)/shard_map/ppermute | solution.py:44
  295.1 4.6 collective-permute-start.22
  295.2 5.9 %collective-permute-start.24 = (bf16[48,512]{1,0:T(8,128)(2,1)S(1)}, bf16[48,512]{1,0:T(8,128)(2,1)S(1)}, u32[]{:S(2)}, u32[]{:S(2)}) collective-permute-start(bf16[48,512]{1,0:T(8,128)(2,1)S(1)} %get-tuple-element.545), channel_id=1, source_target_pairs={{0,8},{8,16},{16,24},{24,0},{1,9},{9,17},{17,25},{25,1},{2,10},{10... | collective-permute-start | bytes 147464 | tf_op jit(solution)/shard_map/ppermute | solution.py:49
  301.2 6.5 %collective-permute-start.25 = (bf16[96,512]{1,0:T(8,128)(2,1)S(1)}, bf16[96,512]{1,0:T(8,128)(2,1)S(1)}, u32[]{:S(2)}, u32[]{:S(2)}) collective-permute-start(bf16[96,512]{1,0:T(8,128)(2,1)S(1)} %pad_maximum_fusion.9), channel_id=1, source_target_pairs={{0,8},{8,16},{16,24},{24,0},{1,9},{9,17},{17,25},{25,1},{2,10},{10... | collective-permute-start | bytes 294920 | tf_op jit(solution)/shard_map/ppermute | solution.py:49
  301.4 6.2 %collective-permute-start.23 = (bf16[96,512]{1,0:T(8,128)(2,1)S(1)}, bf16[96,512]{1,0:T(8,128)(2,1)S(1)}, u32[]{:S(2)}, u32[]{:S(2)}) collective-permute-start(bf16[96,512]{1,0:T(8,128)(2,1)S(1)} %pad_maximum_fusion.8), channel_id=1, source_target_pairs={{0,24},{8,0},{16,8},{24,16},{1,25},{9,1},{17,9},{25,17},{2,26},{10... | collective-permute-start | bytes 294920 | tf_op jit(solution)/shard_map/ppermute | solution.py:49
  333.3 17.7 %collective-permute-start.27 = (bf16[16,256,512]{2,1,0:T(8,128)(2,1)}, bf16[16,256,512]{2,1,0:T(8,128)(2,1)}, u32[]{:S(2)}, u32[]{:S(2)}) collective-permute-start(bf16[16,256,512]{2,1,0:T(8,128)(2,1)} %get-tuple-element.227), channel_id=1, source_target_pairs={{0,2},{2,0},{1,3},{3,1},{4,6},{6,4},{5,7},{7,5},{8,10},{10,8},{9,1... | collective-permute-start | bytes 12582920 | tf_op jit(solution)/shard_map/ppermute | solution.py:44
  338.2 12.7 %collective-permute-start.26 = (bf16[176,512]{1,0:T(8,128)(2,1)S(1)}, bf16[176,512]{1,0:T(8,128)(2,1)S(1)}, u32[]{:S(2)}, u32[]{:S(2)}) collective-permute-start(bf16[176,512]{1,0:T(8,128)(2,1)S(1)} %maximum_maximum_fusion), channel_id=1, source_target_pairs={{0,1},{1,0},{2,3},{3,2},{4,5},{5,4},{6,7},{7,6},{8,9},{9,8},{10,11... | collective-permute-start | bytes 540680 | tf_op jit(solution)/shard_map/ppermute | solution.py:44
  364.3 21.1 %collective-permute-start.30 = (bf16[13,256,512]{2,1,0:T(8,128)(2,1)}, bf16[13,256,512]{2,1,0:T(8,128)(2,1)S(1)}, u32[]{:S(2)}, u32[]{:S(2)}) collective-permute-start(bf16[13,256,512]{2,1,0:T(8,128)(2,1)} %get-tuple-element.536), channel_id=1, source_target_pairs={{0,2},{2,0},{1,3},{3,1},{4,6},{6,4},{5,7},{7,5},{8,10},{10,8},{9,1... | collective-permute-start | bytes 10223624 | tf_op jit(solution)/shard_map/ppermute | solution.py:44
  364.6 9.4 %collective-permute-start.31 = (bf16[256,512]{1,0:T(8,128)(2,1)S(1)}, bf16[256,512]{1,0:T(8,128)(2,1)S(1)}, u32[]{:S(2)}, u32[]{:S(2)}) collective-permute-start(bf16[256,512]{1,0:T(8,128)(2,1)S(1)} %multiply_convert_fusion), channel_id=1, source_target_pairs={{0,1},{1,0},{2,3},{3,2},{4,5},{5,4},{6,7},{7,6},{8,9},{9,8},{10,11... | collective-permute-start | bytes 786440 | tf_op jit(solution)/shard_map/ppermute | solution.py:44
  365.2 12.7 %collective-permute-start.29 = (bf16[2,176,512]{2,1,0:T(8,128)(2,1)S(1)}, bf16[2,176,512]{2,1,0:T(8,128)(2,1)S(1)}, u32[]{:S(2)}, u32[]{:S(2)}) collective-permute-start(bf16[2,176,512]{2,1,0:T(8,128)(2,1)S(1)} %pad_maximum_fusion.4), channel_id=1, source_target_pairs={{0,24},{8,0},{16,8},{24,16},{1,25},{9,1},{17,9},{25,17},{2,26},{10... | collective-permute-start | bytes 1081352 | tf_op jit(solution)/shard_map/ppermute | solution.py:49
  369.1 16.3 %collective-permute-start.28 = (bf16[2,176,512]{2,1,0:T(8,128)(2,1)S(1)}, bf16[2,176,512]{2,1,0:T(8,128)(2,1)S(1)}, u32[]{:S(2)}, u32[]{:S(2)}) collective-permute-start(bf16[2,176,512]{2,1,0:T(8,128)(2,1)S(1)} %pad_maximum_fusion.4), channel_id=1, source_target_pairs={{0,8},{8,16},{16,24},{24,0},{1,9},{9,17},{17,25},{25,1},{2,10},{10... | collective-permute-start | bytes 1081352 | tf_op jit(solution)/shard_map/ppermute | solution.py:49
  386.2 9.8 %collective-permute-start.33 = (bf16[1,176,512]{2,1,0:T(8,128)(2,1)S(1)}, bf16[1,176,512]{2,1,0:T(8,128)(2,1)S(1)}, u32[]{:S(2)}, u32[]{:S(2)}) collective-permute-start(bf16[1,176,512]{2,1,0:T(8,128)(2,1)S(1)} %slice.418), channel_id=1, source_target_pairs={{0,24},{8,0},{16,8},{24,16},{1,25},{9,1},{17,9},{25,17},{2,26},{10... | collective-permute-start | bytes 540680 | tf_op jit(solution)/shard_map/ppermute | solution.py:49
  388.0 8.7 %collective-permute-start.32 = (bf16[1,176,512]{2,1,0:T(8,128)(2,1)S(1)}, bf16[1,176,512]{2,1,0:T(8,128)(2,1)S(1)}, u32[]{:S(2)}, u32[]{:S(2)}) collective-permute-start(bf16[1,176,512]{2,1,0:T(8,128)(2,1)S(1)} %slice.417), channel_id=1, source_target_pairs={{0,8},{8,16},{16,24},{24,0},{1,9},{9,17},{17,25},{25,1},{2,10},{10... | collective-permute-start | bytes 540680 | tf_op jit(solution)/shard_map/ppermute | solution.py:49
  397.4 45.5 %collective-permute-start.34 = (bf16[8,256,512]{2,1,0:T(8,128)(2,1)}, bf16[8,256,512]{2,1,0:T(8,128)(2,1)}, u32[]{:S(2)}, u32[]{:S(2)}) collective-permute-start(bf16[8,256,512]{2,1,0:T(8,128)(2,1)} %get-tuple-element.258), channel_id=1, source_target_pairs={{0,1},{1,0},{2,3},{3,2},{4,5},{5,4},{6,7},{7,6},{8,9},{9,8},{10,11... | collective-permute-start | bytes 6291464 | tf_op jit(solution)/shard_map/ppermute | solution.py:44
  398.9 40.4 %collective-permute-start.35 = (bf16[13,128,512]{2,1,0:T(8,128)(2,1)}, bf16[13,128,512]{2,1,0:T(8,128)(2,1)S(1)}, u32[]{:S(2)}, u32[]{:S(2)}) collective-permute-start(bf16[13,128,512]{2,1,0:T(8,128)(2,1)} %get-tuple-element.260), channel_id=1, source_target_pairs={{0,4},{4,0},{1,5},{5,1},{2,6},{6,2},{3,7},{7,3},{8,12},{12,8},{9,1... | collective-permute-start | bytes 5111816 | tf_op jit(solution)/shard_map/ppermute | solution.py:44
  399.5 21.9 %collective-permute-start.37 = (bf16[2,256,512]{2,1,0:T(8,128)(2,1)}, bf16[2,256,512]{2,1,0:T(8,128)(2,1)S(1)}, u32[]{:S(2)}, u32[]{:S(2)}) collective-permute-start(bf16[2,256,512]{2,1,0:T(8,128)(2,1)} %pad_maximum_fusion.1), channel_id=1, source_target_pairs={{0,24},{8,0},{16,8},{24,16},{1,25},{9,1},{17,9},{25,17},{2,26},{10... | collective-permute-start | bytes 1572872 | tf_op jit(solution)/shard_map/ppermute | solution.py:49
  401.3 24.0 %collective-permute-start.36 = (bf16[2,256,512]{2,1,0:T(8,128)(2,1)}, bf16[2,256,512]{2,1,0:T(8,128)(2,1)S(1)}, u32[]{:S(2)}, u32[]{:S(2)}) collective-permute-start(bf16[2,256,512]{2,1,0:T(8,128)(2,1)} %pad_maximum_fusion.1), channel_id=1, source_target_pairs={{0,8},{8,16},{16,24},{24,0},{1,9},{9,17},{17,25},{25,1},{2,10},{10... | collective-permute-start | bytes 1572872 | tf_op jit(solution)/shard_map/ppermute | solution.py:49
  425.3 8.5 %collective-permute-start.39 = (bf16[1,256,512]{2,1,0:T(8,128)(2,1)S(1)}, bf16[1,256,512]{2,1,0:T(8,128)(2,1)S(1)}, u32[]{:S(2)}, u32[]{:S(2)}) collective-permute-start(bf16[1,256,512]{2,1,0:T(8,128)(2,1)S(1)} %slice.420), channel_id=1, source_target_pairs={{0,24},{8,0},{16,8},{24,16},{1,25},{9,1},{17,9},{25,17},{2,26},{10... | collective-permute-start | bytes 786440 | tf_op jit(solution)/shard_map/ppermute | solution.py:49
  427.1 12.2 %collective-permute-start.38 = (bf16[1,256,512]{2,1,0:T(8,128)(2,1)S(1)}, bf16[1,256,512]{2,1,0:T(8,128)(2,1)S(1)}, u32[]{:S(2)}, u32[]{:S(2)}) collective-permute-start(bf16[1,256,512]{2,1,0:T(8,128)(2,1)S(1)} %slice.419), channel_id=1, source_target_pairs={{0,8},{8,16},{16,24},{24,0},{1,9},{9,17},{17,25},{25,1},{2,10},{10... | collective-permute-start | bytes 786440 | tf_op jit(solution)/shard_map/ppermute | solution.py:49
  444.9 31.8 %collective-permute-start.40 = (bf16[8,128,512]{2,1,0:T(8,128)(2,1)S(1)}, bf16[8,128,512]{2,1,0:T(8,128)(2,1)S(1)}, u32[]{:S(2)}, u32[]{:S(2)}) collective-permute-start(bf16[8,128,512]{2,1,0:T(8,128)(2,1)S(1)} %get-tuple-element.284), channel_id=1, source_target_pairs={{0,4},{4,0},{1,5},{5,1},{2,6},{6,2},{3,7},{7,3},{8,12},{12,8},{9,1... | collective-permute-start | bytes 3145736 | tf_op jit(solution)/shard_map/ppermute | solution.py:44
  452.1 24.5 %collective-permute-start.41 = (bf16[1000,512]{1,0:T(8,128)(2,1)S(1)}, bf16[1000,512]{1,0:T(8,128)(2,1)}, u32[]{:S(2)}, u32[]{:S(2)}) collective-permute-start(bf16[1000,512]{1,0:T(8,128)(2,1)S(1)} %get-tuple-element.292), channel_id=1, source_target_pairs={{0,2},{2,0},{1,3},{3,1},{4,6},{6,4},{5,7},{7,5},{8,10},{10,8},{9,1... | collective-permute-start | bytes 3072008 | tf_op jit(solution)/shard_map/ppermute | solution.py:44
  459.8 16.9 %collective-permute-start.42 = (bf16[1000,512]{1,0:T(8,128)(2,1)}, bf16[1000,512]{1,0:T(8,128)(2,1)S(1)}, u32[]{:S(2)}, u32[]{:S(2)}) collective-permute-start(bf16[1000,512]{1,0:T(8,128)(2,1)} %get-tuple-element.295), channel_id=1, source_target_pairs={{0,2},{2,0},{1,3},{3,1},{4,6},{6,4},{5,7},{7,5},{8,10},{10,8},{9,1... | collective-permute-start | bytes 3072008 | tf_op jit(solution)/shard_map/ppermute | solution.py:44
  461.1 8.8 %collective-permute-start.43 = (bf16[13,32,256]{2,1,0:T(8,128)(2,1)S(1)}, bf16[13,32,256]{2,1,0:T(8,128)(2,1)S(1)}, u32[]{:S(2)}, u32[]{:S(2)}) collective-permute-start(bf16[13,32,256]{2,1,0:T(8,128)(2,1)S(1)} %get-tuple-element.300), channel_id=1, source_target_pairs={{0,24},{8,0},{16,8},{24,16},{1,25},{9,1},{17,9},{25,17},{2,26},{10... | collective-permute-start | bytes 638984 | tf_op jit(solution)/shard_map/ppermute | solution.py:49
  464.2 12.4 %collective-permute-start.44 = (bf16[13,32,256]{2,1,0:T(8,128)(2,1)S(1)}, bf16[13,32,256]{2,1,0:T(8,128)(2,1)S(1)}, u32[]{:S(2)}, u32[]{:S(2)}) collective-permute-start(bf16[13,32,256]{2,1,0:T(8,128)(2,1)S(1)} %get-tuple-element.301), channel_id=1, source_target_pairs={{0,8},{8,16},{16,24},{24,0},{1,9},{9,17},{17,25},{25,1},{2,10},{10... | collective-permute-start | bytes 638984 | tf_op jit(solution)/shard_map/ppermute | solution.py:49
  478.7 28.0 %collective-permute-start.49 = (bf16[1000,512]{1,0:T(8,128)(2,1)S(1)}, bf16[1000,512]{1,0:T(8,128)(2,1)S(1)}, u32[]{:S(2)}, u32[]{:S(2)}) collective-permute-start(bf16[1000,512]{1,0:T(8,128)(2,1)S(1)} %add_convert_fusion.2), channel_id=1, source_target_pairs={{0,4},{4,0},{1,5},{5,1},{2,6},{6,2},{3,7},{7,3},{8,12},{12,8},{9,1... | collective-permute-start | bytes 3072008 | tf_op jit(solution)/shard_map/ppermute | solution.py:44
  480.3 21.5 %collective-permute-start.45 = (bf16[13,32,512]{2,1,0:T(8,128)(2,1)S(1)}, bf16[13,32,512]{2,1,0:T(8,128)(2,1)S(1)}, u32[]{:S(2)}, u32[]{:S(2)}) collective-permute-start(bf16[13,32,512]{2,1,0:T(8,128)(2,1)S(1)} %get-tuple-element.308), channel_id=1, source_target_pairs={{0,24},{8,0},{16,8},{24,16},{1,25},{9,1},{17,9},{25,17},{2,26},{10... | collective-permute-start | bytes 1277960 | tf_op jit(solution)/shard_map/ppermute | solution.py:49
  482.1 20.2 %collective-permute-start.46 = (bf16[13,32,512]{2,1,0:T(8,128)(2,1)S(1)}, bf16[13,32,512]{2,1,0:T(8,128)(2,1)S(1)}, u32[]{:S(2)}, u32[]{:S(2)}) collective-permute-start(bf16[13,32,512]{2,1,0:T(8,128)(2,1)S(1)} %get-tuple-element.309), channel_id=1, source_target_pairs={{0,8},{8,16},{16,24},{24,0},{1,9},{9,17},{17,25},{25,1},{2,10},{10... | collective-permute-start | bytes 1277960 | tf_op jit(solution)/shard_map/ppermute | solution.py:49
  482.7 21.7 %collective-permute-start.47 = (bf16[8,32,256]{2,1,0:T(8,128)(2,1)S(1)}, bf16[8,32,256]{2,1,0:T(8,128)(2,1)S(1)}, u32[]{:S(2)}, u32[]{:S(2)}) collective-permute-start(bf16[8,32,256]{2,1,0:T(8,128)(2,1)S(1)} %get-tuple-element.314), channel_id=1, source_target_pairs={{0,24},{8,0},{16,8},{24,16},{1,25},{9,1},{17,9},{25,17},{2,26},{10... | collective-permute-start | bytes 393224 | tf_op jit(solution)/shard_map/ppermute | solution.py:49
  486.3 39.3 %copy-start.7 = (f32[1000,512]{1,0:T(8,128)S(1)}, f32[1000,512]{1,0:T(8,128)}, u32[]{:S(2)}) copy-start(f32[1000,512]{1,0:T(8,128)} %copy-done.6) | copy-start | bytes 6144004
  486.3 20.4 %collective-permute-start.48 = (bf16[8,32,256]{2,1,0:T(8,128)(2,1)S(1)}, bf16[8,32,256]{2,1,0:T(8,128)(2,1)S(1)}, u32[]{:S(2)}, u32[]{:S(2)}) collective-permute-start(bf16[8,32,256]{2,1,0:T(8,128)(2,1)S(1)} %get-tuple-element.315), channel_id=1, source_target_pairs={{0,8},{8,16},{16,24},{24,0},{1,9},{9,17},{17,25},{25,1},{2,10},{10... | collective-permute-start | bytes 393224 | tf_op jit(solution)/shard_map/ppermute | solution.py:49
  506.6 17.3 %collective-permute-start.52 = (bf16[13,32,512]{2,1,0:T(8,128)(2,1)S(1)}, bf16[13,32,512]{2,1,0:T(8,128)(2,1)S(1)}, u32[]{:S(2)}, u32[]{:S(2)}) collective-permute-start(bf16[13,32,512]{2,1,0:T(8,128)(2,1)S(1)} %shard_map.499.one_ref), channel_id=1, source_target_pairs={{0,1},{1,0},{2,3},{3,2},{4,5},{5,4},{6,7},{7,6},{8,9},{9,8},{10,11... | collective-permute-start | bytes 1277960 | tf_op jit(solution)/shard_map/ppermute | solution.py:44
  508.9 12.8 %collective-permute-start.50 = (bf16[8,32,512]{2,1,0:T(8,128)(2,1)}, bf16[8,32,512]{2,1,0:T(8,128)(2,1)}, u32[]{:S(2)}, u32[]{:S(2)}) collective-permute-start(bf16[8,32,512]{2,1,0:T(8,128)(2,1)} %get-tuple-element.324), channel_id=1, source_target_pairs={{0,24},{8,0},{16,8},{24,16},{1,25},{9,1},{17,9},{25,17},{2,26},{10... | collective-permute-start | bytes 786440 | tf_op jit(solution)/shard_map/ppermute | solution.py:49
  510.9 10.8 %collective-permute-start.51 = (bf16[8,32,512]{2,1,0:T(8,128)(2,1)}, bf16[8,32,512]{2,1,0:T(8,128)(2,1)}, u32[]{:S(2)}, u32[]{:S(2)}) collective-permute-start(bf16[8,32,512]{2,1,0:T(8,128)(2,1)} %get-tuple-element.325), channel_id=1, source_target_pairs={{0,8},{8,16},{16,24},{24,0},{1,9},{9,17},{17,25},{25,1},{2,10},{10... | collective-permute-start | bytes 786440 | tf_op jit(solution)/shard_map/ppermute | solution.py:49
  524.9 6.4 %collective-permute-start.53 = (bf16[8,32,512]{2,1,0:T(8,128)(2,1)S(1)}, bf16[8,32,512]{2,1,0:T(8,128)(2,1)S(1)}, u32[]{:S(2)}, u32[]{:S(2)}) collective-permute-start(bf16[8,32,512]{2,1,0:T(8,128)(2,1)S(1)} %shard_map.502.mine_ref), channel_id=1, source_target_pairs={{0,1},{1,0},{2,3},{3,2},{4,5},{5,4},{6,7},{7,6},{8,9},{9,8},{10,11... | collective-permute-start | bytes 786440 | tf_op jit(solution)/shard_map/ppermute | solution.py:44
  535.2 1.1 collective-permute-start.54
  536.4 3.5 collective-permute-start.55
  540.0 3.5 collective-permute-start.56
  543.6 3.5 collective-permute-start.57
  547.1 4.5 collective-permute-start.58
  (118 other events, 802.4 us)
Sparse Core Ops, SparseCore 0:
  13.4 88.2 all-gather.2
  104.5 84.5 all-gather.4
